TPU v7x, 128 devices: a whole 4x4x4 slice. The times are simulated.
128 devices in a mesh: shard: 2 (over z_lo), context: 16 (over x, y), tensor: 4 (over z_hi, core).
Axes of the slice: x: 4, y: 4, z: 4 (z_hi: 2, z_lo: 2; z = z_hi * 2 + z_lo), core: 2. Of those that a mesh axis runs over, the one named last changes fastest.
Arguments:
- tokens: bfloat16 [4, 4096, 960], P('shard', ('context', 'tensor')), may hold values from -6 to 6
- positions: int32 [4, 4096], P('shard', ('context', 'tensor')), may hold values from 0 to 4095, as said below
- out_grad: bfloat16 [4, 4096, 960], P('shard', ('context', 'tensor')), may hold values from -6 to 6
- attn_gain: bfloat16 [960], P(('shard', 'context')), may hold values from 0.099609375 to 1.8984375
- w_query: bfloat16 [960, 960], P(('shard', 'context')), may hold values from -0.1875 to 0.1875
- key_weight: bfloat16 [960, 320], P(('shard', 'context')), may hold values from -0.1875 to 0.1875
- value_weight: bfloat16 [960, 320], P(('shard', 'context')), may hold values from -0.1875 to 0.1875
- w_out: bfloat16 [960, 960], P(('shard', 'context')), may hold values from -1.5 to 1.5
- mlp_gain: bfloat16 [960], P(('shard', 'context')), may hold values from 0.099609375 to 1.8984375
- w_gate: bfloat16 [960, 2560], P(('shard', 'context'), 'tensor'), may hold values from -0.1875 to 0.1875
- w_up: bfloat16 [960, 2560], P(('shard', 'context'), 'tensor'), may hold values from -0.1875 to 0.1875
- w_down: bfloat16 [2560, 960], P('tensor', ('shard', 'context')), may hold values from -0.125 to 0.125
Outputs:
- mixed: bfloat16 [4, 4096, 960], P('shard', ('context', 'tensor'))
- tokens_grad: float32 [4, 4096, 960], P('shard', ('context', 'tensor'))
- attn_gain_grad: float32 [960], P(('shard', 'context'))
- w_query_grad: float32 [960, 960], P(('shard', 'context'))
- w_key_grad: float32 [960, 320], P(('shard', 'context'))
- w_value_grad: float32 [960, 320], P(('shard', 'context'))
- w_out_grad: float32 [960, 960], P(('shard', 'context'))
- mlp_gain_grad: float32 [960], P(('shard', 'context'))
- w_gate_grad: float32 [960, 2560], P(('shard', 'context'), 'tensor')
- w_up_grad: float32 [960, 2560], P(('shard', 'context'), 'tensor')
- w_down_grad: float32 [2560, 960], P('tensor', ('shard', 'context'))
Inputs may be any that keep to these rules, and one draw needn't show every extreme that they name: In each sequence the positions count up by one from 0, starting anew at the first token and at the first token of each packed document; at least one sequence is a single document.
All inputs are finite; a program needn't handle non-finite values.
Results may differ from a plain program's by a relative error of at most 0.029.
Values may be sent and summed in bfloat16 or wider, within the bound.
No kernel may reach another device: no remote copies, remote signals or barrier semaphores. Data moves between devices by JAX's collectives and lax.ppermute only.
A program may use at most 128 MiB of HBM per device.

v0:
```python
import math

import jax
import jax.numpy as jnp
from jax import lax
from jax.sharding import PartitionSpec as P

QUERY_HEADS = 15
KEY_HEADS = 5
HEAD_SIZE = 64


EPSILON = 1e-05
ROPE_BASE = 100000.0
MASKED = -1e30


def sent_together(arrays, axis, dim, along):
    widths = [math.prod(a.shape[along:]) for a in arrays]
    both = jnp.concatenate(
        [a.reshape(*a.shape[:along], w) for a, w in zip(arrays, widths)], axis=along
    )
    result = lax.all_gather(both, axis, axis=dim, tiled=True)
    pieces = jnp.split(result, [sum(widths[:k]) for k in range(1, len(widths))], axis=along)
    return tuple(
        (b.reshape(*result.shape[:along], *a.shape[along:]) for a, b in zip(arrays, pieces))
    )


def turned_gather(arrays, axis, dims):
    turned = [jnp.moveaxis(a, dim, 0) for a, dim in zip(arrays, dims)]
    widths = [t[0].size for t in turned]
    both = jnp.concatenate([t.reshape(-1, w) for t, w in zip(turned, widths)], axis=1)
    result = lax.all_gather(both, axis, axis=0, tiled=True)
    pieces = jnp.split(result, [sum(widths[:k]) for k in range(1, len(widths))], axis=1)
    return tuple(
        (
            jnp.moveaxis(b.reshape(-1, *t.shape[1:]), 0, dim)
            for b, t, dim in zip(pieces, turned, dims)
        )
    )


def copy_for_each(array, axis):
    copies = jnp.broadcast_to(array, (lax.axis_size(axis), *array.shape))
    return lax.all_to_all(copies, axis, split_axis=0, concat_axis=0, tiled=True)


def laid_out(pieces, dim):
    lengths = list(pieces.shape[1:])
    lengths[dim] *= pieces.shape[0]
    return jnp.moveaxis(pieces, 0, dim).reshape(lengths)


def gather_directly(array, axis, dim):
    pieces = copy_for_each(array, axis)
    return laid_out(pieces, dim)


def cut_along(array, dim, size):
    before, after = (array.shape[:dim], array.shape[dim + 1 :])
    return jnp.moveaxis(array.reshape(*before, size, -1, *after), dim, 0)


def summed_on_arrival(array, axis, dim):
    size = lax.axis_size(axis)
    pieces = lax.all_to_all(cut_along(array, dim, size), axis, 0, 0, tiled=True)
    return jnp.sum(pieces.astype(jnp.float32), axis=0)


def one_scatter(arrays, axis, dims):
    size = lax.axis_size(axis)
    pieces = [cut_along(a, dim, size) for a, dim in zip(arrays, dims)]
    lines = jnp.concatenate([b.reshape(size, -1) for b in pieces], axis=1)
    extent = max(16, -(-lines.shape[1] // 1024) * 8)
    lines = jnp.pad(lines, ((0, 0), (0, extent * 128 - lines.shape[1]))).reshape(-1, 128)
    flat, at, gathered = (lax.psum_scatter(lines, axis, tiled=True).reshape(-1), 0, [])
    for b in pieces:
        part = b[0]
        gathered.append(flat[at : at + part.size].reshape(part.shape))
        at += part.size
    return tuple(gathered)


def of_everyone(array, axis):
    return copy_for_each(array, axis).astype(jnp.float32).sum(axis=0)


def normalize(value_rows):
    factor = lax.rsqrt(jnp.mean(value_rows * value_rows, axis=-1, keepdims=True) + EPSILON)
    return (value_rows * factor, factor)


def norm_back(grad, normed, factor):
    return factor * (grad - normed * jnp.mean(grad * normed, axis=-1, keepdims=True))


def tables(positions, width):
    half = width // 2
    freq = ROPE_BASE ** (-2.0 * jnp.arange(half, dtype=jnp.float32) / width)
    theta = positions.astype(jnp.float32)[..., None] * freq
    return (jnp.cos(theta), jnp.sin(theta))


def apply_rotation(value_rows, cosine_table, sine_table):
    half = value_rows.shape[-1] // 2
    first = value_rows[..., :half]
    second = value_rows[..., half:]
    return jnp.concatenate(
        [first * cosine_table - second * sine_table, second * cosine_table + first * sine_table],
        axis=-1,
    )


def reverse_rotation(grads, cosine_table, sine_table):
    half = grads.shape[-1] // 2
    first = grads[..., :half]
    second = grads[..., half:]
    return jnp.concatenate(
        [first * cosine_table + second * sine_table, second * cosine_table - first * sine_table],
        axis=-1,
    )


def masked_scores(query_rows, key_rows, start, first_row):
    raw = jnp.einsum("sqgrd,skgd->sgrqk", query_rows, key_rows, preferred_element_type=jnp.float32)
    rows = first_row + jnp.arange(query_rows.shape[1], dtype=jnp.int32)
    cols = start + jnp.arange(key_rows.shape[1], dtype=jnp.int32)
    keep = cols[None, :] <= rows[:, None]
    return jnp.where(keep, raw * (1.0 / math.sqrt(query_rows.shape[-1])), MASKED)


def shards(
    tokens,
    positions,
    out_grad,
    attn_gain,
    w_query,
    key_weight,
    value_weight,
    w_out,
    mlp_gain,
    w_gate,
    w_up,
    w_down,
):
    gain_attn, query_full, key_full, value_full, out_full = sent_together(
        (attn_gain, w_query, key_weight, value_weight, w_out), ("shard", "context"), 0, 1
    )
    gain_mlp, gate_full, up_full, down_full = turned_gather(
        (mlp_gain, w_gate, w_up, w_down), ("shard", "context"), (0, 0, 0, 1)
    )
    sequence_count, block_length, width = tokens.shape
    count_of_rows = sequence_count * block_length
    query_width = QUERY_HEADS * HEAD_SIZE
    key_value_width = KEY_HEADS * HEAD_SIZE
    head_groups = QUERY_HEADS // KEY_HEADS
    scale = 1.0 / math.sqrt(HEAD_SIZE)
    resid_in = tokens.reshape(count_of_rows, width).astype(jnp.float32)
    normed_attn, factor_attn = normalize(resid_in)
    hidden_attn = (normed_attn * gain_attn.astype(jnp.float32)).astype(jnp.bfloat16)
    proj_weights = jnp.concatenate([query_full, key_full, value_full], axis=1)
    projected_rows = jnp.dot(hidden_attn, proj_weights, preferred_element_type=jnp.float32)
    cosine_table, sine_table = tables(positions.reshape(count_of_rows), HEAD_SIZE)
    cosine_table = cosine_table[:, None, :]
    sine_table = sine_table[:, None, :]
    query_rows = apply_rotation(
        projected_rows[:, :query_width].reshape(count_of_rows, QUERY_HEADS, HEAD_SIZE),
        cosine_table,
        sine_table,
    ).astype(jnp.bfloat16)
    keys_own = apply_rotation(
        projected_rows[:, query_width : query_width + key_value_width].reshape(
            count_of_rows, KEY_HEADS, HEAD_SIZE
        ),
        cosine_table,
        sine_table,
    ).astype(jnp.bfloat16)
    values_own = projected_rows[:, query_width + key_value_width :].astype(jnp.bfloat16)
    packed = jnp.concatenate(
        [keys_own.reshape(count_of_rows, key_value_width), values_own], axis=1
    ).reshape(sequence_count, block_length, 2 * key_value_width)
    kv_all = lax.all_gather(packed, ("context", "tensor"), axis=1, tiled=True)
    total_len = kv_all.shape[1]
    key_tile_block = min(512, total_len)
    level = lax.axis_index("context") * lax.axis_size("tensor") + lax.axis_index("tensor")
    first_row = level * block_length
    count = (first_row + block_length + key_tile_block - 1) // key_tile_block
    query_lattice = query_rows.reshape(
        sequence_count, block_length, KEY_HEADS, head_groups, HEAD_SIZE
    )

    def split_block(start):
        portion = lax.dynamic_slice_in_dim(kv_all, start, key_tile_block, 1)
        key_rows = portion[..., :key_value_width].reshape(
            sequence_count, key_tile_block, KEY_HEADS, HEAD_SIZE
        )
        value_rows = portion[..., key_value_width:].reshape(
            sequence_count, key_tile_block, KEY_HEADS, HEAD_SIZE
        )
        return (key_rows, value_rows)

    def max_step(index, carry):
        top, mass = carry
        start = index * key_tile_block
        key_rows, value_rows = split_block(start)
        scores = masked_scores(query_lattice, key_rows, start, first_row)
        new_top = jnp.maximum(top, jnp.max(scores, axis=-1))
        mass = mass * jnp.exp(top - new_top) + jnp.sum(
            jnp.exp(scores - new_top[..., None]), axis=-1
        )
        return (new_top, mass)

    statistic_shape = (sequence_count, KEY_HEADS, head_groups, block_length)
    top, mass = lax.fori_loop(
        0,
        count,
        max_step,
        (jnp.full(statistic_shape, MASKED, jnp.float32), jnp.zeros(statistic_shape, jnp.float32)),
    )
    log_mass = top + jnp.log(mass)

    def value_step(index, acc):
        start = index * key_tile_block
        key_rows, value_rows = split_block(start)
        scores = masked_scores(query_lattice, key_rows, start, first_row)
        weights = jnp.exp(scores - log_mass[..., None]).astype(jnp.bfloat16)
        return acc + jnp.einsum(
            "sgrqk,skgd->sqgrd", weights, value_rows, preferred_element_type=jnp.float32
        )

    attended_rows = lax.fori_loop(0, count, value_step, jnp.zeros(query_lattice.shape, jnp.float32))
    attended_low = attended_rows.reshape(count_of_rows, query_width).astype(jnp.bfloat16)
    resid_mid = resid_in + jnp.dot(attended_low, out_full, preferred_element_type=jnp.float32)
    normed_mlp, factor_mlp = normalize(resid_mid)
    hidden_mlp = (normed_mlp * gain_mlp.astype(jnp.float32)).astype(jnp.bfloat16)
    mlp_rows = gather_directly(hidden_mlp.reshape(sequence_count, block_length, width), "tensor", 1)
    group_rows = mlp_rows.shape[1]
    mlp_flat = mlp_rows.reshape(sequence_count * group_rows, width)
    gate = jnp.dot(mlp_flat, gate_full, preferred_element_type=jnp.float32)
    upward = jnp.dot(mlp_flat, up_full, preferred_element_type=jnp.float32)
    swished = jax.nn.silu(gate)
    activated = (swished * upward).astype(jnp.bfloat16)
    partial_out = jnp.dot(activated, down_full, preferred_element_type=jnp.float32).reshape(
        sequence_count, group_rows, width
    )
    mlp_share = summed_on_arrival(partial_out.astype(jnp.bfloat16), "tensor", 1)
    mixed = (resid_mid.reshape(sequence_count, block_length, width) + mlp_share).astype(
        jnp.bfloat16
    )
    grad_rows = gather_directly(out_grad, "tensor", 1).reshape(sequence_count * group_rows, width)
    down_grad = jnp.einsum("rf,rd->fd", activated, grad_rows, preferred_element_type=jnp.float32)
    act_grad = jnp.einsum("rd,fd->rf", grad_rows, down_full, preferred_element_type=jnp.float32)
    sigma = jax.nn.sigmoid(gate)
    gate_grad = (act_grad * upward * sigma * (1.0 + gate * (1.0 - sigma))).astype(jnp.bfloat16)
    up_grad_low = (act_grad * swished).astype(jnp.bfloat16)
    gate_weight_grad = jnp.einsum(
        "rd,rf->df", mlp_flat, gate_grad, preferred_element_type=jnp.float32
    )
    up_weight_grad = jnp.einsum(
        "rd,rf->df", mlp_flat, up_grad_low, preferred_element_type=jnp.float32
    )
    hidden_part = jnp.einsum(
        "rf,df->rd", gate_grad, gate_full, preferred_element_type=jnp.float32
    ) + jnp.einsum("rf,df->rd", up_grad_low, up_full, preferred_element_type=jnp.float32)
    hidden_grad = summed_on_arrival(
        hidden_part.reshape(sequence_count, group_rows, width).astype(jnp.bfloat16), "tensor", 1
    ).reshape(count_of_rows, width)
    gain_mlp_part = jnp.sum(hidden_grad * normed_mlp, axis=0)
    resid_grad = out_grad.reshape(count_of_rows, width).astype(jnp.float32) + norm_back(
        hidden_grad * gain_mlp.astype(jnp.float32), normed_mlp, factor_mlp
    )
    branch_grad = resid_grad.astype(jnp.bfloat16)
    out_weight_grad = jnp.einsum(
        "rk,rd->kd", attended_low, branch_grad, preferred_element_type=jnp.float32
    )
    attended_gradient = jnp.einsum(
        "rd,kd->rk", branch_grad, out_full, preferred_element_type=jnp.float32
    ).astype(jnp.bfloat16)
    gradient_lattice = attended_gradient.reshape(
        sequence_count, block_length, KEY_HEADS, head_groups, HEAD_SIZE
    )
    delta = jnp.einsum("sqgrd,sqgrd->sgrq", gradient_lattice.astype(jnp.float32), attended_rows)

    def grad_step(index, carry):
        query_acc, kv_grad = carry
        start = index * key_tile_block
        key_rows, value_rows = split_block(start)
        scores = masked_scores(query_lattice, key_rows, start, first_row)
        weights = jnp.exp(scores - log_mass[..., None])
        weight_grad = jnp.einsum(
            "sqgrd,skgd->sgrqk", gradient_lattice, value_rows, preferred_element_type=jnp.float32
        )
        score_grad = (weights * (weight_grad - delta[..., None]) * scale).astype(jnp.bfloat16)
        query_acc = query_acc + jnp.einsum(
            "sgrqk,skgd->sqgrd", score_grad, key_rows, preferred_element_type=jnp.float32
        )
        key_part = jnp.einsum(
            "sgrqk,sqgrd->skgd", score_grad, query_lattice, preferred_element_type=jnp.float32
        )
        value_part = jnp.einsum(
            "sgrqk,sqgrd->skgd",
            weights.astype(jnp.bfloat16),
            gradient_lattice,
            preferred_element_type=jnp.float32,
        )
        both = jnp.concatenate(
            [
                key_part.reshape(sequence_count, key_tile_block, key_value_width),
                value_part.reshape(sequence_count, key_tile_block, key_value_width),
            ],
            axis=-1,
        )
        kv_grad = lax.dynamic_update_slice_in_dim(kv_grad, both, start, 1)
        return (query_acc, kv_grad)

    query_acc, kv_grad = lax.fori_loop(
        0,
        count,
        grad_step,
        (
            jnp.zeros(query_lattice.shape, jnp.float32),
            jnp.zeros((sequence_count, total_len, 2 * key_value_width), jnp.float32),
        ),
    )
    kv_middle = lax.psum_scatter(
        kv_grad.astype(jnp.bfloat16), "context", scatter_dimension=1, tiled=True
    )
    local_key_value = summed_on_arrival(kv_middle, "tensor", 1)
    local_key_value = local_key_value.reshape(count_of_rows, 2 * key_value_width)
    query_pre = reverse_rotation(
        query_acc.reshape(count_of_rows, QUERY_HEADS, HEAD_SIZE), cosine_table, sine_table
    ).reshape(count_of_rows, query_width)
    key_unrotated = reverse_rotation(
        local_key_value[:, :key_value_width].reshape(count_of_rows, KEY_HEADS, HEAD_SIZE),
        cosine_table,
        sine_table,
    ).reshape(count_of_rows, key_value_width)
    proj_grad = jnp.concatenate(
        [query_pre, key_unrotated, local_key_value[:, key_value_width:]], axis=1
    ).astype(jnp.bfloat16)
    proj_weight_grad = jnp.einsum(
        "rd,rk->dk", hidden_attn, proj_grad, preferred_element_type=jnp.float32
    )
    hidden_attn_grad = jnp.einsum(
        "rk,dk->rd", proj_grad, proj_weights, preferred_element_type=jnp.float32
    )
    gain_attn_part = jnp.sum(hidden_attn_grad * normed_attn, axis=0)
    tokens_grad = resid_grad + norm_back(
        hidden_attn_grad * gain_attn.astype(jnp.float32), normed_attn, factor_attn
    )
    gate_out, up_out, down_out = tuple(
        (
            part.astype(jnp.float32)
            for part in one_scatter(
                (
                    gate_weight_grad.astype(jnp.bfloat16),
                    up_weight_grad.astype(jnp.bfloat16),
                    down_grad.astype(jnp.bfloat16),
                ),
                ("shard", "context"),
                (0, 0, 1),
            )
        )
    )
    summed = tuple(
        (
            part.astype(jnp.float32)
            for part in one_scatter(
                (
                    gain_attn_part.astype(jnp.bfloat16),
                    proj_weight_grad[:, :query_width].astype(jnp.bfloat16),
                    proj_weight_grad[:, query_width : query_width + key_value_width].astype(
                        jnp.bfloat16
                    ),
                    proj_weight_grad[:, query_width + key_value_width :].astype(jnp.bfloat16),
                    out_weight_grad.astype(jnp.bfloat16),
                    gain_mlp_part.astype(jnp.bfloat16),
                ),
                ("shard", "context"),
                (0, 0, 0, 0, 0, 0),
            )
        )
    )
    gain_a_out, query_out, key_out, value_out, wout_out, gain_m_out = (
        of_everyone(summed[0].astype(jnp.bfloat16), "tensor").astype(jnp.float32),
        of_everyone(summed[1].astype(jnp.bfloat16), "tensor").astype(jnp.float32),
        of_everyone(summed[2].astype(jnp.bfloat16), "tensor").astype(jnp.float32),
        of_everyone(summed[3].astype(jnp.bfloat16), "tensor").astype(jnp.float32),
        of_everyone(summed[4].astype(jnp.bfloat16), "tensor").astype(jnp.float32),
        of_everyone(summed[5].astype(jnp.bfloat16), "tensor").astype(jnp.float32),
    )
    return (
        mixed,
        tokens_grad.reshape(sequence_count, block_length, width),
        gain_a_out,
        query_out,
        key_out,
        value_out,
        wout_out,
        gain_m_out,
        gate_out,
        up_out,
        down_out,
    )


def solution(mesh):
    return jax.shard_map(
        shards,
        mesh=mesh,
        in_specs=(
            P("shard", ("context", "tensor"), None),
            P("shard", ("context", "tensor")),
            P("shard", ("context", "tensor"), None),
            P(("shard", "context")),
            P(("shard", "context"), None),
            P(("shard", "context"), None),
            P(("shard", "context"), None),
            P(("shard", "context"), None),
            P(("shard", "context")),
            P(("shard", "context"), "tensor"),
            P(("shard", "context"), "tensor"),
            P("tensor", ("shard", "context")),
        ),
        out_specs=(
            P("shard", ("context", "tensor"), None),
            P("shard", ("context", "tensor"), None),
            P(("shard", "context")),
            P(("shard", "context"), None),
            P(("shard", "context"), None),
            P(("shard", "context"), None),
            P(("shard", "context"), None),
            P(("shard", "context")),
            P(("shard", "context"), "tensor"),
            P(("shard", "context"), "tensor"),
            P("tensor", ("shard", "context")),
        ),
        check_vma=False,
    )
```

profile of v0, /device:TPU:1, one launch (start us, length us, event | category | flops | bytes accessed | tf_op | source)
XLA Modules:
  0.0 1330.8 jit_solution(6322751198072468232)
XLA Ops:
  15.7 140.2 %all-gather.8.cloned.1.call-done = bf16[32,30,2561]{2,1,0:T(8,128)(2,1)} async-done(((bf16[1,30,2561]{2,1,0:T(8,128)(2,1)}), bf16[32,30,2561]{2,1,0:T(8,128)(2,1)}) %all-gather.8.cloned.1.call-update) | async-done | bytes 4917136 | tf_op jit(solution)/shard_map/all_gather | solution.py:23
  155.8 8.0 reshape.345
  165.0 5.1 fusion.31
  173.7 23.9 %all-to-all-start.2 = ((bf16[4,2,64,960]{3,2,1,0:T(8,128)(2,1)}), bf16[4,2,64,960]{3,2,1,0:T(8,128)(2,1)}, u32[]{:S(2)}, u32[]{:S(2)}) async-start(bf16[4,2,64,960]{3,2,1,0:T(8,128)(2,1)} %broadcast_in_dim.78), calls=%async_computation.2 | async-start | bytes 2097152 | tf_op jit(solution)/shard_map/all_to_all | solution.py:46
  197.5 117.9 %all-gather.10.cloned.1.call-done = bf16[32,30,1921]{2,1,0:T(8,128)(2,1)} async-done(((bf16[1,30,1921]{2,1,0:T(8,128)(2,1)}), bf16[32,30,1921]{2,1,0:T(8,128)(2,1)}) %all-gather.10.cloned.1.call-update) | async-done | bytes 3688336 | tf_op jit(solution)/shard_map/all_gather | solution.py:34
  315.4 5.5 reshape.347
  323.9 104.7 %all-gather.6.cloned.1.call-done = bf16[2,4096,640]{2,0,1:T(2,128)(2,1)} async-done(((bf16[2,64,640]{2,0,1:T(2,128)(2,1)}), bf16[2,4096,640]{2,0,1:T(2,128)(2,1)}) %all-gather.6.cloned.1.call-update) | async-done | bytes 10485776 | tf_op jit(solution)/shard_map/all_gather | solution.py:183
  428.6 26.4 %copy.227 = bf16[2,4096,640]{1,2,0:T(8,128)(2,1)} copy(bf16[2,4096,640]{2,0,1:T(2,128)(2,1)} %all-gather.6.cloned.1.call-done) | data formatting | bytes 20971520 | tf_op jit(solution)/shard_map/while | solution.py:232
  475.1 12.9 all-to-all-done
  503.6 5.1 all-to-all-start.3
  510.1 13.8 %all-to-all-done.3 = bf16[4,2,64,960]{3,2,1,0:T(8,128)(2,1)} async-done(((bf16[4,2,64,960]{3,2,1,0:T(8,128)(2,1)}), bf16[4,2,64,960]{3,2,1,0:T(8,128)(2,1)}, u32[]{:S(2)}, u32[]{:S(2)}) %all-to-all-start.3) | async-done | bytes 983072 | tf_op jit(solution)/shard_map/all_to_all | solution.py:67
  532.7 4.6 broadcast_in_dim.79.clone
  537.3 12.4 while.36
  556.9 9.0 reshape.335
  580.0 5.3 reshape.336
  585.4 183.0 %reduce-scatter.3.cloned.1.call-done = bf16[2,256,640]{2,1,0:T(8,128)(2,1)} async-done(((bf16[2,4096,640]{2,1,0:T(8,128)(2,1)}), bf16[2,256,640]{2,1,0:T(8,128)(2,1)}) %reduce-scatter.3.cloned.1.call-update) | async-done | bytes 655376 | tf_op jit(solution)/shard_map/reduce_scatter | solution.py:326
  770.3 6.0 all-to-all-start.4
  789.0 4.7 multiply_reduce_fusion.3
  797.5 4.7 reshape_reshape.26
  809.2 11.7 dynamic-update-slice.1
  820.9 6.1 dynamic-update-slice.2
  827.0 6.2 dynamic-update-slice.3
  833.2 11.1 dynamic-update-slice.4
  845.6 5.0 pad.8
  850.6 6.2 reshape.328
  862.0 4.8 all-to-all-start.1
  868.2 18.5 %all-to-all-done.1 = bf16[4,2,64,960]{3,2,1,0:T(8,128)(2,1)S(1)} async-done(((bf16[4,2,64,960]{3,2,1,0:T(8,128)(2,1)}), bf16[4,2,64,960]{3,2,1,0:T(8,128)(2,1)S(1)}, u32[]{:S(2)}, u32[]{:S(2)}) %all-to-all-start.1) | async-done | bytes 983072 | tf_op jit(solution)/shard_map/all_to_all | solution.py:67
  887.7 182.9 %all-reduce.5.cloned.1.call-done = bf16[14592,128]{1,0:T(8,128)(2,1)} async-done(((bf16[14592,128]{1,0:T(8,128)(2,1)}), bf16[14592,128]{1,0:T(8,128)(2,1)}) %all-reduce.5.cloned.1.call-update) | async-done | bytes 3735568
  1073.8 164.2 %reduce-scatter.5.cloned.1.call-done = bf16[608,128]{1,0:T(8,128)(2,1)} async-done(((bf16[19456,128]{1,0:T(8,128)(2,1)}), bf16[608,128]{1,0:T(8,128)(2,1)}) %reduce-scatter.5.cloned.1.call-update) | async-done | bytes 155664 | tf_op jit(solution)/shard_map/reduce_scatter | solution.py:77
  1239.3 27.5 %all-to-all-start.5 = ((bf16[4,1,30]{2,1,0:T(2,128)(2,1)}), bf16[4,1,30]{2,1,0:T(2,128)(2,1)S(1)}, u32[]{:S(2)}, u32[]{:S(2)}) async-start(bf16[4,1,30]{2,1,0:T(2,128)(2,1)} %broadcast_in_dim.80), calls=%async_computation.7 | async-start | bytes 4096 | tf_op jit(solution)/shard_map/all_to_all | solution.py:46
  1305.6 5.5 all-to-all-done.6
  1317.5 5.3 all-to-all-done.9
  (248 shorter events, 185.4 us)
Async XLA Ops:
  7.2 148.6 %all-gather.8.cloned.1.call-start = ((), (), s32[]{:S(2)}) async-start(), calls=%async_computation.16 | async-start | bytes 5677056 | tf_op jit(solution)/shard_map/all_gather | solution.py:23
  9.7 305.7 %all-gather.10.cloned.1.call-start = ((), (), s32[]{:S(2)}) async-start(), calls=%async_computation.17 | async-start | bytes 4325376 | tf_op jit(solution)/shard_map/all_gather | solution.py:34
  12.2 416.4 %all-gather.6.cloned.1.call-start = ((), (), s32[]{:S(2)}) async-start(), calls=%async_computation.13 | async-start | bytes 10649600 | tf_op jit(solution)/shard_map/all_gather | solution.py:183
  13.4 449.8 %copy-start.4 = (f32[128,960]{0,1:T(8,128)}, f32[128,960]{0,1:T(8,128)S(1)}, u32[]{:S(2)}) copy-start(f32[128,960]{0,1:T(8,128)S(1)} %copy.230) | copy-start | bytes 1474564
  14.7 150.2 %copy-start.25 = (f32[128]{0:T(128)}, f32[128]{0:T(128)S(1)}, u32[]{:S(2)}) copy-start(f32[128]{0:T(128)S(1)} %rsqrt.20) | copy-start | bytes 1540
  173.7 293.6 %all-to-all-start.2 = ((bf16[4,2,64,960]{3,2,1,0:T(8,128)(2,1)}), bf16[4,2,64,960]{3,2,1,0:T(8,128)(2,1)}, u32[]{:S(2)}, u32[]{:S(2)}) async-start(bf16[4,2,64,960]{3,2,1,0:T(8,128)(2,1)} %broadcast_in_dim.78), calls=%async_computation.2 | async-start | bytes 2097152 | tf_op jit(solution)/shard_map/all_to_all | solution.py:46
  322.9 132.1 %copy-start.10 = (bf16[2,64,5,3,64]{1,0,4,3,2:T(2,128)(2,1)}, bf16[2,64,5,3,64]{1,0,4,3,2:T(2,128)(2,1)S(1)}, u32[]{:S(2)}) copy-start(bf16[2,64,5,3,64]{1,0,4,3,2:T(2,128)(2,1)S(1)} %constant_dynamic-update-slice_fusion.1) | copy-start | bytes 737284
  466.9 59.1 %copy-start.1 = (f32[128,960]{0,1:T(8,128)}, f32[128,960]{0,1:T(8,128)S(1)}, u32[]{:S(2)}) copy-start(f32[128,960]{0,1:T(8,128)S(1)} %get-tuple-element.475) | copy-start | bytes 1474564
  468.4 19.7 %all-to-all-start = ((bf16[4,2,64,960]{3,2,1,0:T(8,128)(2,1)}), bf16[4,2,64,960]{3,2,1,0:T(8,128)(2,1)}, u32[]{:S(2)}, u32[]{:S(2)}) async-start(bf16[4,2,64,960]{3,2,1,0:T(8,128)(2,1)} %broadcast_in_dim.77), calls=%async_computation | async-start | bytes 2097152 | tf_op jit(solution)/shard_map/all_to_all | solution.py:46
  499.0 9.8 copy-start.13
  499.0 10.9 copy-start.11
  503.6 20.3 %all-to-all-start.3 = ((bf16[4,2,64,960]{3,2,1,0:T(8,128)(2,1)}), bf16[4,2,64,960]{3,2,1,0:T(8,128)(2,1)}, u32[]{:S(2)}, u32[]{:S(2)}) async-start(bf16[4,2,64,960]{3,2,1,0:T(8,128)(2,1)} %copy.240), calls=%async_computation.3 | async-start | bytes 2097152 | tf_op jit(solution)/shard_map/all_to_all | solution.py:67
  508.7 259.6 %reduce-scatter.3.cloned.1.call-start = ((), (), s32[]{:S(2)}) async-start(), calls=%async_computation.14 | async-start | bytes 11141120 | tf_op jit(solution)/shard_map/reduce_scatter | solution.py:326
  549.8 520.7 %all-reduce.5.cloned.1.call-start = ((), (), s32[]{:S(2)}) async-start(), calls=%async_computation.18 | async-start | bytes 7471104
  585.3 191.0 %copy-start.8 = (f32[128,960]{0,1:T(8,128)S(1)}, f32[128,960]{0,1:T(8,128)}, u32[]{:S(2)}) copy-start(f32[128,960]{0,1:T(8,128)} %copy-done.7) | copy-start | bytes 1474564
  585.4 191.0 %copy-start.19 = (bf16[128,960]{0,1:T(8,128)(2,1)S(1)}, bf16[128,960]{0,1:T(8,128)(2,1)}, u32[]{:S(2)}) copy-start(bf16[128,960]{0,1:T(8,128)(2,1)} %copy-done.18) | copy-start | bytes 737284
  770.3 17.0 %all-to-all-start.4 = ((bf16[4,2,64,640]{3,2,1,0:T(8,128)(2,1)}), bf16[4,2,64,640]{3,2,1,0:T(8,128)(2,1)}, u32[]{:S(2)}, u32[]{:S(2)}) async-start(bf16[4,2,64,640]{3,2,1,0:T(8,128)(2,1)} %copy.248), calls=%async_computation.5 | async-start | bytes 1310720 | tf_op jit(solution)/shard_map/all_to_all | solution.py:67
  776.3 461.7 %reduce-scatter.5.cloned.1.call-start = ((), (), s32[]{:S(2)}) async-start(), calls=%async_computation.15 | async-start | bytes 5136384 | tf_op jit(solution)/shard_map/reduce_scatter | solution.py:77
  779.5 9.4 copy-start.5
  779.5 9.4 copy-start.26
  805.7 27.4 %copy-start.3 = (bf16[32,28800]{1,0:T(8,128)(2,1)S(1)}, bf16[32,28800]{1,0:T(8,128)(2,1)}, u32[]{:S(2)}) copy-start(bf16[32,28800]{1,0:T(8,128)(2,1)} %reshape_reshape.29) | copy-start | bytes 5529604
  862.0 211.9 %copy-start.29 = (f32[128]{0:T(128)S(1)}, f32[128]{0:T(128)}, u32[]{:S(2)}) copy-start(f32[128]{0:T(128)} %get-tuple-element.395) | copy-start | bytes 1540
  862.0 404.8 %copy-start.6 = (f32[128,960]{0,1:T(8,128)S(1)}, f32[128,960]{0,1:T(8,128)}, u32[]{:S(2)}) copy-start(f32[128,960]{0,1:T(8,128)} %copy-done.4) | copy-start | bytes 1474564
  862.0 404.8 %copy-start.9 = (f32[128,960]{0,1:T(8,128)S(1)}, f32[128,960]{0,1:T(8,128)}, u32[]{:S(2)}) copy-start(f32[128,960]{0,1:T(8,128)} %copy-done.7) | copy-start | bytes 1474564
  862.0 404.8 %copy-start.23 = (f32[128,960]{0,1:T(8,128)S(1)}, f32[128,960]{0,1:T(8,128)}, u32[]{:S(2)}) copy-start(f32[128,960]{0,1:T(8,128)} %get-tuple-element.476) | copy-start | bytes 1474564
  862.0 24.7 %all-to-all-start.1 = ((bf16[4,2,64,960]{3,2,1,0:T(8,128)(2,1)}), bf16[4,2,64,960]{3,2,1,0:T(8,128)(2,1)S(1)}, u32[]{:S(2)}, u32[]{:S(2)}) async-start(bf16[4,2,64,960]{3,2,1,0:T(8,128)(2,1)} %copy.236), calls=%async_computation.1 | async-start | bytes 2097152 | tf_op jit(solution)/shard_map/all_to_all | solution.py:67
  1239.3 31.9 %all-to-all-start.5 = ((bf16[4,1,30]{2,1,0:T(2,128)(2,1)}), bf16[4,1,30]{2,1,0:T(2,128)(2,1)S(1)}, u32[]{:S(2)}, u32[]{:S(2)}) async-start(bf16[4,1,30]{2,1,0:T(2,128)(2,1)} %broadcast_in_dim.80), calls=%async_computation.7 | async-start | bytes 4096 | tf_op jit(solution)/shard_map/all_to_all | solution.py:46
  1271.9 8.4 all-to-all-start.10
  1280.9 8.8 all-to-all-start.7
  1290.4 9.1 all-to-all-start.8
  1300.2 11.0 all-to-all-start.6
  1311.9 10.9 all-to-all-start.9
  (17 other events, 76.0 us)
Sparse Core Ops, SparseCore 0:
  10.2 145.5 all-gather.7
  158.0 157.3 all-gather.9
  319.1 109.4 all-gather.5
  549.9 218.3 reduce-scatter.2
  770.7 299.7 all-reduce.4
  1072.9 165.0 reduce-scatter.4
where the time goes:
time: 1340 us; the launch traced here: 1330 us
  waiting for transfers between devices  967 us (72%)
  local copies, waits for them, and re-layouts  185 us (14%)
  starting transfers between devices  92.8 us (7%)
  matrix products  48.1 us (4%)
  other arithmetic  20.6 us (2%)
  between operations  16.1 us (1%)
    unnamed x7, waiting for transfers between devices  183 us
    reduce_scatter x1, waiting for transfers between devices, shards(): lax.psum_scatter(kv_grad.astype(jnp.bfloat16), 'context', scatter_dimensi...  183 us
    reduce_scatter x1, waiting for transfers between devices, one_scatter(): lax.psum_scatter(lines, axis, tiled=True).reshape(-1)  164 us
    all_gather x1, waiting for transfers between devices, sent_together(): result = lax.all_gather(both, axis, axis=dim, tiled=True)  140 us
    all_gather x1, waiting for transfers between devices, turned_gather(): result = lax.all_gather(both, axis, axis=0, tiled=True)  118 us
    all_gather x1, waiting for transfers between devices, shards(): kv_all = lax.all_gather(packed, ('context', 'tensor'), axis=1, tiled=True)  105 us
    all_to_all x8, starting transfers between devices, copy_for_each(): return lax.all_to_all(copies, axis, split_axis=0, concat_axis=0, tiled=True)  76.4 us
    unnamed x74, local copies, waits for them, and re-layouts  53.9 us
  transfers between devices with their start and end apart: 17, of which 16 were waited for; matrix products, arithmetic and copies ran while one was open for 15% of the time, Pallas kernels for 0%

commit v1 on v0

v1 whole, which is shorter than its diff:
```python
import math

import jax
import jax.numpy as jnp
from jax import lax
from jax.experimental import pallas as pl
from jax.experimental.pallas import tpu as pltpu
from jax.sharding import PartitionSpec as P

QH = 15
KH = 5
REP = 3
D = 64
WIDTH = 960
BLK = 30
PADB = 32
NB = 32
WP = NB * PADB
QKV = 1600
FFS = 640
QUART = 448
T = 128
EPSILON = 1e-05
ROPE_BASE = 100000.0
MASKED = -1e30
F32 = jnp.float32
BF16 = jnp.bfloat16
HIGHEST = lax.Precision.HIGHEST
SC = ("shard", "context")
CT = ("context", "tensor")
ALL = ("shard", "context", "tensor")
QB = 8
KB = 512
QN = 256


def dot(a, b, precision=None):
    return lax.dot_general(
        a, b, (((1,), (0,)), ((), ())), precision=precision, preferred_element_type=F32
    )


def dot_t(a, b, precision=None):
    return lax.dot_general(
        a, b, (((1,), (1,)), ((), ())), precision=precision, preferred_element_type=F32
    )


def tdot(a, b):
    return lax.dot_general(a, b, (((0,), (0,)), ((), ())), preferred_element_type=F32)


def call(fn, outs, *args, scratch=(), name=None):
    return pl.pallas_call(
        fn,
        out_shape=tuple(jax.ShapeDtypeStruct(s, d) for s, d in outs),
        scratch_shapes=list(scratch),
        compiler_params=pltpu.CompilerParams(vmem_limit_bytes=56 * 1024 * 1024),
        name=name,
    )(*args)


def exchange(v, axes):
    return lax.all_to_all(v, axes, 0, 0, tiled=True)


def to_all(v, axes):
    n = math.prod(lax.axis_size(a) for a in ((axes,) if isinstance(axes, str) else axes))
    return exchange(jnp.broadcast_to(v, (n, *v.shape)), axes)


def normed(x):
    r = lax.rsqrt(jnp.sum(x * x, axis=-1, keepdims=True) * (1.0 / WIDTH) + EPSILON)
    return x * r, r


def norm_back(m, n, r):
    return r * (m - n * (jnp.sum(m * n, axis=-1, keepdims=True) * (1.0 / WIDTH)))


def turn(x, cos, sin):
    lane = lax.broadcasted_iota(jnp.int32, x.shape, 1)
    partner = jnp.where(
        lax.rem(lane, 64) < 32, pltpu.roll(x, 96, 1), pltpu.roll(x, 32, 1)
    )
    return x * cos + partner * sin


def units():
    for s in range(2):
        for head in range(QH):
            for half in range(2):
                unit = s * 30 + head * 2 + half
                yield unit, s * 64 + half * 32, head * D


def pack_rows(src, send, first):
    for unit, row, col in units():
        send[unit, first : first + 16, :] = jnp.concatenate(
            [src[row : row + 16, col : col + D], src[row + 16 : row + 32, col : col + D]], axis=1
        ).astype(send.dtype)


def unpack_rows(recv, dst, first):
    for unit, row, col in units():
        part = recv[unit, first : first + 16, :].astype(dst.dtype)
        dst[row : row + 16, col : col + D] = part[:, :D]
        dst[row + 16 : row + 32, col : col + D] = part[:, D:]


def pad_kernel(x, dy, e, xp, dyp):
    xp[...] = dot(x[...], e[...]).astype(BF16)
    dyp[...] = dot(dy[...], e[...]).astype(BF16)


def project_kernel(xp, gain, w, cos, sin, send, h1_out, rows):
    n1, _ = normed(xp[...].astype(F32))
    h1 = (n1 * gain[...]).astype(BF16)
    h1_out[...] = h1
    qkv = dot(h1, w[...].reshape(WP, QKV))
    for j in range(10):
        part = turn(qkv[:, 128 * j : 128 * j + 128], cos[...], sin[...])
        lane = lax.broadcasted_iota(jnp.int32, part.shape, 1) + 128 * j
        rows[:, 128 * j : 128 * j + 128] = part
    send[60:64] = jnp.zeros((4, 80, 128), BF16)
    for unit, row, col in units():
        send[unit, 64:80, :] = (
            jnp.concatenate(
                [rows[row : row + 16, col : col + D], rows[row + 16 : row + 32, col : col + D]],
                axis=1,
            ).astype(BF16)
            * 0.125
        ).astype(BF16)
    for s in range(2):
        for g in range(KH):
            both = jnp.concatenate(
                [
                    rows[s * 64 : s * 64 + 64, 960 + D * g : 960 + D * g + D],
                    qkv[s * 64 : s * 64 + 64, 1280 + D * g : 1280 + D * g + D],
                ],
                axis=1,
            ).astype(BF16)
            for u in range(6):
                send[s * 30 + g * 6 + u, 0:64, :] = both


def low_pair(block):
    lane = lax.broadcasted_iota(jnp.int32, block.shape, 1)
    zero = jnp.zeros_like(block)
    return jnp.concatenate(
        [
            jnp.where(lane < D, block, zero),
            jnp.where(lane < D, pltpu.roll(block, D, 1), zero),
        ],
        axis=0,
    ).astype(BF16)


def high_pair(block):
    lane = lax.broadcasted_iota(jnp.int32, block.shape, 1)
    zero = jnp.zeros_like(block)
    return jnp.concatenate(
        [
            jnp.where(lane >= D, pltpu.roll(block, D, 1), zero),
            jnp.where(lane >= D, block, zero),
        ],
        axis=0,
    ).astype(BF16)


def load_pair(ref, qb, first):
    return ref[pl.ds(qb * 8, 8), first : first + 16, :].reshape(T, 128).astype(F32)


def unpair(cols):
    flat = cols.T
    return jnp.concatenate([flat[:T], flat[T:]], axis=1).astype(BF16).reshape(8, 16, 128)


def attend_kernel(recv, qpos, send, o_out, lse_out, kv_t, scores):
    for kb in range(QB):
        block = recv[kb * 8 : kb * 8 + 8, 0:64, :].reshape(KB, 128)
        kv_t[kb] = block.astype(F32).T.astype(BF16)

    def key_block(kb):
        return recv[pl.ds(kb * 8, 8), 0:64, :].reshape(KB, 128)

    def one(qb, carry):
        q = low_pair(load_pair(recv, qb, 64))

        def first(kb, top):
            raw = dot_t(key_block(kb), q)
            scores[kb] = raw
            return jnp.maximum(top, jnp.max(raw.reshape(KB // 8, 8, QN), axis=0))

        top = lax.fori_loop(0, qb, first, jnp.full((8, QN), MASKED, F32))
        raw = dot_t(key_block(qb), q)
        kpos = lax.broadcasted_iota(jnp.int32, (KB, QN), 0)
        raw = jnp.where(kpos <= qpos[...], raw, MASKED)
        scores[qb] = raw
        top = jnp.maximum(top, jnp.max(raw.reshape(KB // 8, 8, QN), axis=0))
        top = jnp.max(top, axis=0, keepdims=True)

        def second(kb, carry):
            mass, acc = carry
            p = jnp.exp(scores[kb] - top)
            mass = mass + jnp.sum(p.reshape(KB // 8, 8, QN), axis=0)
            acc = acc + dot(kv_t[kb, D:, :], p.astype(BF16))
            return mass, acc

        mass, acc = lax.fori_loop(
            0, qb + 1, second, (jnp.zeros((8, QN), F32), jnp.zeros((D, QN), F32))
        )
        mass = jnp.sum(mass, axis=0, keepdims=True)
        acc = acc / mass
        o_out[qb] = acc
        lse_out[qb] = jnp.broadcast_to(top + jnp.log(mass), (8, QN))
        send[pl.ds(qb * 8, 8)] = unpair(acc)
        return carry

    lax.fori_loop(0, QB, one, 0)


def attend_back_kernel(recv, qpos, drecv, o_in, lse_in, send, kv_t, dkv):
    for kb in range(QB):
        block = recv[kb * 8 : kb * 8 + 8, 0:64, :].reshape(KB, 128)
        kv_t[kb] = block[:, :D].astype(F32).T.astype(BF16)
    dkv[...] = jnp.zeros_like(dkv)

    def one(qb, carry):
        q = low_pair(load_pair(recv, qb, 64))
        pair = load_pair(drecv, qb, 0)
        dz = high_pair(pair)
        flat = jnp.concatenate([pair[:, :D], pair[:, D:]], axis=0)
        delta = jnp.sum(flat.T * o_in[qb], axis=0, keepdims=True)
        lse = lse_in[qb][0:1]

        def tile(kb, acc, diagonal):
            block = recv[pl.ds(kb * 8, 8), 0:64, :].reshape(KB, 128)
            raw = dot_t(block, q)
            if diagonal:
                kpos = lax.broadcasted_iota(jnp.int32, (KB, QN), 0)
                raw = jnp.where(kpos <= qpos[...], raw, MASKED)
            p = jnp.exp(raw - lse)
            ds = (p * (dot_t(block, dz) - delta)).astype(BF16)
            dkv[kb] += dot(ds, q) + dot(p.astype(BF16), dz)
            return acc + dot(kv_t[kb], ds)

        acc = lax.fori_loop(0, qb, lambda kb, a: tile(kb, a, False), jnp.zeros((D, QN), F32))
        acc = tile(qb, acc, True)
        send[pl.ds(qb * 8, 8), 64:80, :] = unpair(acc * 0.125)
        return carry

    lax.fori_loop(0, QB, one, 0)
    for kb in range(QB):
        send[kb * 8 : kb * 8 + 8, 0:64, :] = dkv[kb].astype(BF16).reshape(8, 64, 128)


def out_kernel(recv, xp, e, gain, w, olp_out, x1_out, h2_out, ol):
    unpack_rows(recv, ol, 0)
    olp = dot(ol[...], e[...]).astype(BF16)
    olp_out[...] = olp
    x1 = xp[...].astype(F32) + dot(olp, w[...].reshape(WP, WP))
    x1_out[...] = x1
    n2, _ = normed(x1)
    h2_out[...] = (n2 * gain[...]).astype(BF16)


def mlp_kernel(h2, dy, w, part, dh2, act, dgate, dup):
    wg = w[:, 0:32, :].reshape(WP, FFS)
    wu = w[:, 32:64, :].reshape(WP, FFS)
    wd = w[:, 64:96, :].reshape(WP, FFS)
    for i in range(4):
        h = h2[i]
        gate = dot(h, wg)
        up = dot(h, wu)
        sig = jax.nn.sigmoid(gate)
        silu = gate * sig
        a = (silu * up).astype(BF16)
        act[i] = a
        part[i] = dot_t(a, wd).astype(BF16)
        dact = dot(dy[i], wd)
        dg = (dact * up * sig * (1.0 + gate * (1.0 - sig))).astype(BF16)
        du = (dact * silu).astype(BF16)
        dgate[i] = dg
        dup[i] = du
        dh2[i] = (dot_t(dg, wg) + dot_t(du, wu)).astype(BF16)


def mlp_grad_kernel(h2, dy, act, dgate, dup, out):
    h = h2[...].reshape(4 * T, WP)
    out[:, 0:32, :] = tdot(h, dgate[...].reshape(4 * T, FFS)).astype(BF16).reshape(NB, 32, FFS)
    out[:, 32:64, :] = tdot(h, dup[...].reshape(4 * T, FFS)).astype(BF16).reshape(NB, 32, FFS)
    d = dy[...].reshape(4 * T, WP)
    out[:, 64:96, :] = tdot(d, act[...].reshape(4 * T, FFS)).astype(BF16).reshape(NB, 32, FFS)


def mixed_kernel(parts, x1, e, out):
    total = jnp.sum(parts[...].astype(F32), axis=0)
    out[...] = dot_t((x1[...] + total).astype(BF16), e[...]).astype(BF16)


def mid_back_kernel(parts, x1, gain, dyp, w, e, dx1_out, da_out, send, gain_part, dol):
    dh2 = jnp.sum(parts[...].astype(F32), axis=0)
    n2, r2 = normed(x1[...])
    gain_part[...] = jnp.sum(dh2 * n2, axis=0, keepdims=True)
    dx1 = dyp[...].astype(F32) + norm_back(dh2 * gain[...], n2, r2)
    dx1_out[...] = dx1
    da = dx1.astype(BF16)
    da_out[...] = da
    wide = dot_t(da, w[...].reshape(WP, WP)).astype(BF16)
    dol[...] = dot_t(wide, e[...]).astype(BF16)
    send[60:64] = jnp.zeros((4, 16, 128), BF16)
    pack_rows(dol, send, 0)


def out_grad_kernel(olp, da, out):
    for t in range(4):
        out[:, t] = (
            tdot(olp[...], da[:, 256 * t : 256 * t + 256]).astype(BF16).reshape(NB, 32, 256)
        )


def unpack_back_kernel(recv, cos, sin, full, send, rows):
    unpack_rows(recv, rows, 64)
    full[:, QKV:] = jnp.zeros((T, 4 * QUART - QKV), BF16)
    for s in range(2):
        for g in range(KH):
            total = recv[s * 30 + g * 6, 0:64, :].astype(F32)
            for u in range(1, 6):
                total = total + recv[s * 30 + g * 6 + u, 0:64, :].astype(F32)
            rows[s * 64 : s * 64 + 64, 960 + D * g : 960 + D * g + D] = total[:, :D]
            full[s * 64 : s * 64 + 64, 1280 + D * g : 1280 + D * g + D] = total[:, D:].astype(BF16)
    for j in range(10):
        full[:, 128 * j : 128 * j + 128] = turn(
            rows[:, 128 * j : 128 * j + 128], cos[...], -sin[...]
        ).astype(BF16)
    for t in range(4):
        send[t] = full[:, QUART * t : QUART * t + QUART]


def tokens_back_kernel(full, w, xp, gain, dx1, e, tokens_grad, gain_part):
    dh1 = dot_t(full[:, :QKV], w[...].reshape(WP, QKV))
    n1, r1 = normed(xp[...].astype(F32))
    gain_part[...] = jnp.sum(dh1 * n1, axis=0, keepdims=True)
    grad = dx1[...] + norm_back(dh1 * gain[...], n1, r1)
    tokens_grad[...] = dot_t(grad, e[...].astype(F32), HIGHEST)


def proj_grad_kernel(h1, dq, gains, out):
    out[...] = (
        tdot(h1[...].reshape(4 * T, WP), dq[...].reshape(4 * T, QUART))
        .astype(BF16)
        .reshape(NB, 32, QUART)
    )
    out[:, 30:31, :] = gains[...]


def pad_rows(w, extra=None):
    rows = [w]
    if extra is not None:
        rows.append(jnp.pad(extra[None, :], ((0, 0), (0, w.shape[1] - extra.shape[0]))))
    rows.append(jnp.zeros((PADB - BLK - (extra is not None), w.shape[1]), w.dtype))
    return jnp.concatenate(rows, axis=0)


def shards(
    tokens,
    positions,
    out_grad,
    attn_gain,
    w_query,
    key_weight,
    value_weight,
    w_out,
    mlp_gain,
    w_gate,
    w_up,
    w_down,
):
    i = lax.broadcasted_iota(jnp.int32, (WIDTH, WP), 0)
    j = lax.broadcasted_iota(jnp.int32, (WIDTH, WP), 1)
    spread = (j == (i // BLK) * PADB + i % BLK).astype(BF16)

    w1 = to_all(pad_rows(jnp.concatenate([w_query, key_weight, value_weight], axis=1), attn_gain), SC)
    gain1 = w1[:, 30, :PADB].reshape(1, WP).astype(F32)

    own_out = jnp.dot(w_out, spread, preferred_element_type=F32).astype(BF16)
    own_mlp = jnp.concatenate(
        [pad_rows(w_gate, mlp_gain), pad_rows(w_up), pad_rows(w_down.T)], axis=0
    )
    own_out, own_mlp, w1 = lax.optimization_barrier((own_out, own_mlp, w1))
    w2 = to_all(pad_rows(own_out), SC)
    w3 = to_all(own_mlp, SC)
    gain2 = w3[:, 30, :PADB].reshape(1, WP).astype(F32)

    half = D // 2
    freq = ROPE_BASE ** (-2.0 * jnp.arange(half, dtype=F32) / D)
    theta = positions.reshape(T).astype(F32)[:, None] * freq
    c, s = jnp.cos(theta), jnp.sin(theta)
    cos = jnp.concatenate([c, c, c, c], axis=1)
    sin = jnp.concatenate([-s, s, -s, s], axis=1)

    xp, dyp = call(
        pad_kernel,
        [((T, WP), BF16), ((T, WP), BF16)],
        tokens.reshape(T, WIDTH),
        out_grad.reshape(T, WIDTH),
        spread,
    )
    dy_all = to_all(dyp, "tensor").reshape(4, T, WP)

    send, h1 = call(
        project_kernel,
        [((64, 80, 128), BF16), ((T, WP), BF16)],
        xp, gain1, w1, cos, sin,
        scratch=[pltpu.VMEM((T, 1280), F32)],
    )
    recv = exchange(send, CT)
    h1_all = to_all(h1, "tensor").reshape(4, T, WP)

    lane = jnp.arange(QN, dtype=jnp.int32)
    qpos = (
        64 * ((lane % T) // 16)
        + 32 * (lax.axis_index("tensor") % 2)
        + 16 * (lane // T)
        + lane % 16
    ).reshape(1, QN)
    o_send, o_cols, lse = call(
        attend_kernel,
        [((64, 16, 128), BF16), ((QB, D, QN), F32), ((QB, 8, QN), F32)],
        recv, qpos,
        scratch=[pltpu.VMEM((QB, 128, KB), BF16), pltpu.VMEM((QB, KB, QN), F32)],
    )
    o_recv = exchange(o_send, CT)

    olp, x1, h2 = call(
        out_kernel,
        [((T, WP), BF16), ((T, WP), F32), ((T, WP), BF16)],
        o_recv, xp, spread, gain2, w2,
        scratch=[pltpu.VMEM((T, WIDTH), BF16)],
    )
    h2_all = to_all(h2, "tensor").reshape(4, T, WP)

    part, dh2_part, act, dgate, dup = call(
        mlp_kernel,
        [((4, T, WP), BF16), ((4, T, WP), BF16)] + [((4, T, FFS), BF16)] * 3,
        h2_all, dy_all, w3,
    )
    dh2_recv = exchange(dh2_part, "tensor")
    (mlp_grad,) = call(
        mlp_grad_kernel, [((NB, 96, FFS), BF16)], h2_all, dy_all, act, dgate, dup
    )

    dx1, da, d_send, gain2_part = call(
        mid_back_kernel,
        [((T, WP), F32), ((T, WP), BF16), ((64, 16, 128), BF16), ((1, WP), F32)],
        dh2_recv, x1, gain2, dyp, w2, spread,
        scratch=[pltpu.VMEM((T, WIDTH), BF16)],
    )
    d_recv = exchange(d_send, CT)
    part_recv = exchange(part, "tensor")
    mlp_recv = exchange(mlp_grad, SC)

    (mixed,) = call(mixed_kernel, [((T, WIDTH), BF16)], part_recv, x1, spread)
    (out_w_grad,) = call(out_grad_kernel, [((NB, 4, 32, 256), BF16)], olp, da)
    out_recv = exchange(out_w_grad.reshape(NB * 4, 32, 256), ALL)

    (back_send,) = call(
        attend_back_kernel,
        [((64, 80, 128), BF16)],
        recv, qpos, d_recv, o_cols, lse,
        scratch=[pltpu.VMEM((QB, D, KB), BF16), pltpu.VMEM((QB, KB, 128), F32)],
    )
    back_recv = exchange(back_send, CT)

    full, dq_send = call(
        unpack_back_kernel,
        [((T, 4 * QUART), BF16), ((4, T, QUART), BF16)],
        back_recv, cos, sin,
        scratch=[pltpu.VMEM((T, 1280), F32)],
    )
    dq_recv = exchange(dq_send, "tensor")
    tokens_grad, gain1_part = call(
        tokens_back_kernel,
        [((T, WIDTH), F32), ((1, WP), F32)],
        full, w1, xp, gain1, dx1, spread,
    )
    gains = jnp.concatenate(
        [gain1_part.reshape(NB, PADB), gain2_part.reshape(NB, PADB)], axis=1
    ).astype(BF16)
    gains = jnp.pad(gains, ((0, 0), (0, QUART - 2 * PADB))).reshape(NB, 1, QUART)
    (proj_grad,) = call(
        proj_grad_kernel, [((NB, 32, QUART), BF16)], h1_all, dq_recv, gains
    )
    proj_sum = jnp.sum(exchange(proj_grad, SC).astype(F32), axis=0)

    mlp_sum = jnp.sum(mlp_recv.astype(F32), axis=0)
    out_sum = jnp.sum(out_recv.astype(F32), axis=0)
    out_all = to_all(out_sum.astype(BF16), "tensor")
    out_all = jnp.moveaxis(out_all, 0, 1).reshape(32, WP)[:BLK].astype(BF16)
    wout_grad = jnp.einsum("rp,dp->rd", out_all, spread, preferred_element_type=F32)

    proj_all = to_all(proj_sum.astype(BF16), "tensor").astype(F32)
    gain_sums = jnp.sum(proj_all[:, 30, : 2 * PADB], axis=0)
    proj_full = jnp.moveaxis(proj_all[:, :BLK], 0, 1).reshape(BLK, 4 * QUART)
    return (
        mixed.reshape(tokens.shape),
        tokens_grad.reshape(tokens.shape),
        gain_sums[:BLK],
        proj_full[:, :960],
        proj_full[:, 960:1280],
        proj_full[:, 1280:1600],
        wout_grad,
        gain_sums[PADB : PADB + BLK],
        mlp_sum[:BLK],
        mlp_sum[32 : 32 + BLK],
        mlp_sum[64 : 64 + BLK].T,
    )


def solution(mesh):
    tok = P("shard", ("context", "tensor"), None)
    vec = P(SC)
    row = P(SC, None)
    wide = P(SC, "tensor")
    return jax.shard_map(
        shards,
        mesh=mesh,
        in_specs=(
            tok, P("shard", ("context", "tensor")), tok,
            vec, row, row, row, row, vec, wide, wide, P("tensor", SC),
        ),
        out_specs=(
            tok, tok, vec, row, row, row, row, vec, wide, wide, P("tensor", SC),
        ),
        check_vma=False,
    )
```

time: 1340 us -> 546 us (0.41)
  waiting for transfers between devices: 967 us -> 161 us
  blocking collectives: 0 us -> 167 us
  local copies, waits for them, and re-layouts: 185 us -> 30.5 us
  Pallas kernels: 0 us -> 100 us
  matrix products: 48.1 us -> 3.56 us
  starting transfers between devices: 92.8 us -> 67.6 us
  between operations: 16.1 us -> 1.06 us
    all_gather x3 -> x0, waiting for transfers between devices: 363 us -> none  [the longest x1 140 us: sent_together(): result = lax.all_gather(both, axis, axis=dim, tiled=True)]
    reduce_scatter x2 -> x0, waiting for transfers between devices: 347 us -> none  [the longest x1 183 us: shards(): lax.psum_scatter(kv_grad.astype(jnp.bfloat16), 'context', scatter_dimensi...]
    unnamed x7 -> x0, waiting for transfers between devices: 183 us -> none
    all_to_all x0 -> x6, blocking collectives: none -> 167 us  [exchange(): return lax.all_to_all(v, axes, 0, 0, tiled=True)]
    pallas_call x0 -> x13, Pallas kernels: none -> 100 us  [call(): pl.pallas_call(fn, out_shape=tuple((jax.ShapeDtypeStruct(s, d) for s, d i...]
    all_to_all x11 -> x12, waiting for transfers between devices: 74.4 us -> 161 us  [exchange(): return lax.all_to_all(v, axes, 0, 0, tiled=True)]
    unnamed x74 -> x56, local copies, waits for them, and re-layouts: 53.9 us -> 3.44 us
    dot_general x22 -> x2, matrix products: 48.1 us -> 3.56 us  [the longest x1 1.8 us: shards(): jnp.einsum('rp,dp->rd', out_all, spread, preferred_element_type=F32)]
  transfers between devices with their start and end apart: 17 -> 12, of which waited for: 16 -> 10; matrix products, arithmetic and copies ran while one was open for 15% -> 5% of each run, Pallas kernels for 0% -> 11%
where the time goes in v1:
time: 546 us; the launch traced here: 543 us
  blocking collectives  167 us (31%)
  waiting for transfers between devices  161 us (29%)
  Pallas kernels  100 us (18%)
  starting transfers between devices  67.6 us (12%)
  local copies, waits for them, and re-layouts  30.5 us (6%)
  other arithmetic  12 us (2%)
    all_to_all x6, blocking collectives, exchange(): return lax.all_to_all(v, axes, 0, 0, tiled=True)  167 us
    all_to_all x12, waiting for transfers between devices, exchange(): return lax.all_to_all(v, axes, 0, 0, tiled=True)  161 us
    pallas_call x13, Pallas kernels, call(): pl.pallas_call(fn, out_shape=tuple((jax.ShapeDtypeStruct(s, d) for s, d i...  100 us
    all_to_all x12, starting transfers between devices, exchange(): return lax.all_to_all(v, axes, 0, 0, tiled=True)  67.6 us
  transfers between devices with their start and end apart: 12, of which 10 were waited for; matrix products, arithmetic and copies ran while one was open for 5% of the time, Pallas kernels for 11%

profile of v1, /device:TPU:1, one launch (start us, length us, event | category | flops | bytes accessed | tf_op | source)
XLA Modules:
  0.0 543.4 jit_solution(10861042952475925864)
XLA Ops:
  4.4 9.2 %all-to-all-start = ((bf16[32,32,1600]{2,1,0:T(8,128)(2,1)}), bf16[32,32,1600]{2,1,0:T(8,128)(2,1)S(1)}, u32[]{:S(2)}, u32[]{:S(2)}) async-start(bf16[32,32,1600]{2,1,0:T(8,128)(2,1)} %broadcast_in_dim.41), calls=%async_computation | async-start | bytes 6815744 | tf_op jit(solution)/shard_map/all_to_all | solution.py:64
  24.9 6.6 %concatenate.24 = bf16[96,640]{1,0:T(8,128)(2,1)} concatenate(bf16[30,640]{1,0:T(8,128)(2,1)S(1)} %copy-done.12, bf16[1,640]{1,0:T(2,128)(2,1)} %pad.14, bf16[1,640]{1,0:T(2,128)(2,1)} %broadcast_in_dim.43, bf16[30,640]{1,0:T(8,128)(2,1)S(1)} %copy-done.13, bf16[2,640]{1,0:T(2,128)(2,1)} %broadcast.218, bf16[30,640]{1,0:T(8,128)(2,1)} %bitcast.31, bf16[2,640]{1,0:T(2,128)(2,1)} %broadcast.218), dimensions={0} | concatenate | bytes 245760 | tf_op jit(solution)/shard_map/concatenate | solution.py:389
  35.2 19.8 %all-to-all-done.w = bf16[32,32,1600]{2,1,0:T(8,128)(2,1)S(1)} async-done(((bf16[32,32,1600]{2,1,0:T(8,128)(2,1)}), bf16[32,32,1600]{2,1,0:T(8,128)(2,1)S(1)}, u32[]{:S(2)}, u32[]{:S(2)}) %all-to-all-start) | async-done | bytes 3276832 | tf_op jit(solution)/shard_map/all_to_all | solution.py:64
  56.7 4.3 shard_map.204
  61.0 11.6 %all-to-all-start.1 = ((bf16[64,80,128]{2,1,0:T(8,128)(2,1)}), bf16[64,80,128]{2,1,0:T(8,128)(2,1)S(1)}, u32[]{:S(2)}, u32[]{:S(2)}) async-start(bf16[64,80,128]{2,1,0:T(8,128)(2,1)} %get-tuple-element.39), calls=%async_computation.1 | async-start | bytes 2621440 | tf_op jit(solution)/shard_map/all_to_all | solution.py:64
  73.1 21.6 %all-to-all-done.1.recv = bf16[64,80,128]{2,1,0:T(8,128)(2,1)S(1)} async-done(((bf16[64,80,128]{2,1,0:T(8,128)(2,1)}), bf16[64,80,128]{2,1,0:T(8,128)(2,1)S(1)}, u32[]{:S(2)}, u32[]{:S(2)}) %all-to-all-start.1) | async-done | bytes 1310752 | tf_op jit(solution)/shard_map/all_to_all | solution.py:64
  95.9 20.9 %shard_map.205 = (bf16[64,16,128]{2,1,0:T(8,128)(2,1)}, f32[8,64,256]{2,1,0:T(8,128)}, f32[8,8,256]{2,1,0:T(8,128)}) custom-call(bf16[64,80,128]{2,1,0:T(8,128)(2,1)} %copy-done.2, s32[1,256]{1,0:T(1,128)} %fusion.18.qpos), custom_call_target="tpu_custom_call" | custom-call | tf_op jit(solution)/shard_map/pallas_call | solution.py:54
  116.7 4.5 all-to-all-start.2
  121.2 11.4 %all-to-all-done.2.recv = bf16[64,16,128]{2,1,0:T(8,128)(2,1)S(1)} async-done(((bf16[64,16,128]{2,1,0:T(8,128)(2,1)}), bf16[64,16,128]{2,1,0:T(8,128)(2,1)S(1)}, u32[]{:S(2)}, u32[]{:S(2)}) %all-to-all-start.2) | async-done | bytes 262176 | tf_op jit(solution)/shard_map/all_to_all | solution.py:64
  132.9 31.0 %all_to_all.90.w = bf16[32,32,1024]{2,1,0:T(8,128)(2,1)} all-to-all(bf16[32,32,1024]{2,1,0:T(8,128)(2,1)S(1)} %broadcast_in_dim.45), channel_id=1, replica_groups=mesh['shard'=2,'context'=16,'tensor'=4] {'shard','context'}, dimensions={0} | all-to-all | bytes 4194304 | tf_op jit(solution)/shard_map/all_to_all | solution.py:64
  164.2 50.6 %all_to_all.91.w = bf16[32,96,640]{2,1,0:T(8,128)(2,1)} all-to-all(bf16[32,96,640]{2,1,0:T(8,128)(2,1)S(1)} %broadcast_in_dim.44), channel_id=1, replica_groups=mesh['shard'=2,'context'=16,'tensor'=4] {'shard','context'}, dimensions={0} | all-to-all | bytes 7864320 | tf_op jit(solution)/shard_map/all_to_all | solution.py:64
  216.0 6.6 %all-to-all-start.6 = ((bf16[4,128,1024]{2,1,0:T(8,128)(2,1)}), bf16[4,128,1024]{2,1,0:T(8,128)(2,1)S(1)}, u32[]{:S(2)}, u32[]{:S(2)}) async-start(bf16[4,128,1024]{2,1,0:T(8,128)(2,1)} %broadcast_in_dim.47), calls=%async_computation.6 | async-start | bytes 2097152 | tf_op jit(solution)/shard_map/all_to_all | solution.py:64
  228.3 9.4 %all-to-all-done.6.dy = bf16[4,128,1024]{2,1,0:T(8,128)(2,1)S(1)} async-done(((bf16[4,128,1024]{2,1,0:T(8,128)(2,1)}), bf16[4,128,1024]{2,1,0:T(8,128)(2,1)S(1)}, u32[]{:S(2)}, u32[]{:S(2)}) %all-to-all-start.6) | async-done | bytes 1048608 | tf_op jit(solution)/shard_map/all_to_all | solution.py:64
  238.9 18.9 %all_to_all.92.h2 = bf16[4,128,1024]{2,1,0:T(8,128)(2,1)} all-to-all(bf16[4,128,1024]{2,1,0:T(8,128)(2,1)S(1)} %broadcast_in_dim.46), channel_id=1, replica_groups=mesh['shard'=2,'context'=16,'tensor'=4] {'tensor'}, dimensions={0} | all-to-all | bytes 2097152 | tf_op jit(solution)/shard_map/all_to_all | solution.py:64
  257.8 11.7 %shard_map.207 = (bf16[4,128,1024]{2,1,0:T(8,128)(2,1)}, bf16[4,128,1024]{2,1,0:T(8,128)(2,1)}, bf16[4,128,640]{2,1,0:T(8,128)(2,1)}, bf16[4,128,640]{2,1,0:T(8,128)(2,1)}, bf16[4,128,640]{2,1,0:T(8,128)(2,1)}) custom-call(bf16[4,128,1024]{2,1,0:T(8,128)(2,1)} %all_to_all.92.h2, bf16[4,128,1024]{2,1,0:T(8,128)(2,1)} %copy-done.3, ...), custom_call_target="tpu_custom_call" | custom-call | tf_op jit(solution)/shard_map/pallas_call | solution.py:54
  269.6 20.4 %all_to_all.93.parts = bf16[4,128,1024]{2,1,0:T(8,128)(2,1)} all-to-all(bf16[4,128,1024]{2,1,0:T(8,128)(2,1)} %get-tuple-element.47), channel_id=1, replica_groups=mesh['shard'=2,'context'=16,'tensor'=4] {'tensor'}, dimensions={0} | all-to-all | bytes 2097152 | tf_op jit(solution)/shard_map/all_to_all | solution.py:64
  290.0 5.3 shard_map.209
  295.4 17.3 %all_to_all.94.drecv = bf16[64,16,128]{2,1,0:T(8,128)(2,1)} all-to-all(bf16[64,16,128]{2,1,0:T(8,128)(2,1)} %get-tuple-element.48), channel_id=1, replica_groups=mesh['shard'=2,'context'=16,'tensor'=4] {'context','tensor'}, dimensions={0} | all-to-all | bytes 524288 | tf_op jit(solution)/shard_map/all_to_all | solution.py:64
  317.7 22.4 %shard_map.210 = bf16[64,80,128]{2,1,0:T(8,128)(2,1)} custom-call(bf16[64,80,128]{2,1,0:T(8,128)(2,1)} %copy-done.2, s32[1,256]{1,0:T(1,128)} %fusion.18.qpos, bf16[64,16,128]{2,1,0:T(8,128)(2,1)} %all_to_all.94.drecv, f32[8,64,256]{2,1,0:T(8,128)} %get-tuple-element.49.o_in, f32[8,8,256]{2,1,0:T(8,128)} %get-tuple-element.50.lse_in), custom_call_target="tpu_custom_call" | custom-call | tf_op jit(solution)/shard_map/pallas_call | solution.py:54
  340.1 29.1 %all_to_all.95.recv = bf16[64,80,128]{2,1,0:T(8,128)(2,1)} all-to-all(bf16[64,80,128]{2,1,0:T(8,128)(2,1)} %shard_map.210), channel_id=1, replica_groups=mesh['shard'=2,'context'=16,'tensor'=4] {'context','tensor'}, dimensions={0} | all-to-all | bytes 2621440 | tf_op jit(solution)/shard_map/all_to_all | solution.py:64
  378.0 10.2 %all-to-all-done.7.parts = bf16[4,128,1024]{2,1,0:T(8,128)(2,1)S(1)} async-done(((bf16[4,128,1024]{2,1,0:T(8,128)(2,1)}), bf16[4,128,1024]{2,1,0:T(8,128)(2,1)S(1)}, u32[]{:S(2)}, u32[]{:S(2)}) %all-to-all-start.7) | async-done | bytes 1048608 | tf_op jit(solution)/shard_map/all_to_all | solution.py:64
  388.2 4.3 all-to-all-start.12
  395.7 5.6 %all-to-all-done.12 = bf16[4,128,448]{1,2,0:T(8,128)(2,1)S(1)} async-done(((bf16[4,128,448]{1,2,0:T(8,128)(2,1)}), bf16[4,128,448]{1,2,0:T(8,128)(2,1)S(1)}, u32[]{:S(2)}, u32[]{:S(2)}) %all-to-all-start.12) | async-done | bytes 458784 | tf_op jit(solution)/shard_map/all_to_all | solution.py:64
  402.1 4.3 all-to-all-start.15
  406.5 9.1 %shard_map.212 = (f32[128,960]{1,0:T(8,128)}, f32[1,1024]{1,0:T(1,128)}) custom-call(bf16[128,1792]{1,0:T(8,128)(2,1)} %get-tuple-element.51.full, bf16[32,32,1600]{2,1,0:T(8,128)(2,1)} %copy-done.1, bf16[128,1024]{1,0:T(8,128)(2,1)} %get-tuple-element.37.xp, f32[1,1024]{1,0:T(1,128)} %reshape.233.gain, f32[128,1024]{1,0:T(8,128)} %get-tuple-element.52.dx1, ...), custom_call_target="tpu_custom_call" | custom-call | tf_op jit(solution)/shard_map/pallas_call | solution.py:54
  421.4 15.1 %all-to-all-done.15 = bf16[128,32,256]{2,1,0:T(8,128)(2,1)S(1)} async-done(((bf16[128,32,256]{2,1,0:T(8,128)(2,1)}), bf16[128,32,256]{2,1,0:T(8,128)(2,1)S(1)}, u32[]{:S(2)}, u32[]{:S(2)}) %all-to-all-start.15) | async-done | bytes 2097184 | tf_op jit(solution)/shard_map/all_to_all | solution.py:64
  440.8 14.4 %all-to-all-done.13 = bf16[32,32,448]{2,1,0:T(8,128)(2,1)S(1)} async-done(((bf16[32,32,448]{2,1,0:T(8,128)(2,1)}), bf16[32,32,448]{2,1,0:T(8,128)(2,1)S(1)}, u32[]{:S(2)}, u32[]{:S(2)}) %all-to-all-start.13) | async-done | bytes 917536 | tf_op jit(solution)/shard_map/all_to_all | solution.py:64
  455.9 6.2 %all-to-all-start.16 = ((bf16[4,32,256]{2,1,0:T(8,128)(2,1)}), bf16[4,32,256]{2,1,0:T(8,128)(2,1)S(1)}, u32[]{:S(2)}, u32[]{:S(2)}) async-start(bf16[4,32,256]{2,1,0:T(8,128)(2,1)} %broadcast_in_dim.50), calls=%async_computation.16 | async-start | bytes 131072 | tf_op jit(solution)/shard_map/all_to_all | solution.py:64
  462.2 4.6 all-to-all-done.16
  471.6 6.6 %shard_map.215 = bf16[32,96,640]{2,1,0:T(8,128)(2,1)} custom-call(bf16[4,128,1024]{2,1,0:T(8,128)(2,1)} %all_to_all.92.h2, bf16[4,128,1024]{2,1,0:T(8,128)(2,1)} %copy-done.3, bf16[4,128,640]{2,1,0:T(8,128)(2,1)} %get-tuple-element.60.act, bf16[4,128,640]{2,1,0:T(8,128)(2,1)} %get-tuple-element.61.dgate, bf16[4,128,640]{2,1,0:T(8,128)(2,1)} %get-tuple-element.62.dup), custom_call_target="tpu_custom_call" | custom-call | tf_op jit(solution)/shard_map/pallas_call | solution.py:54
  478.3 5.1 all-to-all-start.17
  491.4 48.6 %all-to-all-done.17 = bf16[32,96,640]{2,1,0:T(8,128)(2,1)} async-done(((bf16[32,96,640]{2,1,0:T(8,128)(2,1)}), bf16[32,96,640]{2,1,0:T(8,128)(2,1)}, u32[]{:S(2)}, u32[]{:S(2)}) %all-to-all-start.17) | async-done | bytes 3932192 | tf_op jit(solution)/shard_map/all_to_all | solution.py:64
  (120 shorter events, 75.4 us)
Async XLA Ops:
  0.6 32.7 %copy-start = (bf16[30,960]{1,0:T(8,128)(2,1)S(1)}, bf16[30,960]{1,0:T(8,128)(2,1)}, u32[]{:S(2)}) copy-start(bf16[30,960]{1,0:T(8,128)(2,1)} %param.19) | copy-start | bytes 172804
  4.4 50.6 %all-to-all-start = ((bf16[32,32,1600]{2,1,0:T(8,128)(2,1)}), bf16[32,32,1600]{2,1,0:T(8,128)(2,1)S(1)}, u32[]{:S(2)}, u32[]{:S(2)}) async-start(bf16[32,32,1600]{2,1,0:T(8,128)(2,1)} %broadcast_in_dim.41), calls=%async_computation | async-start | bytes 6815744 | tf_op jit(solution)/shard_map/all_to_all | solution.py:64
  13.6 11.3 %copy-start.12 = (bf16[30,640]{1,0:T(8,128)(2,1)S(1)}, bf16[30,640]{1,0:T(8,128)(2,1)}, u32[]{:S(2)}) copy-start(bf16[30,640]{1,0:T(8,128)(2,1)} %param.21) | copy-start | bytes 115204
  13.6 11.3 %copy-start.13 = (bf16[30,640]{1,0:T(8,128)(2,1)S(1)}, bf16[30,640]{1,0:T(8,128)(2,1)}, u32[]{:S(2)}) copy-start(bf16[30,640]{1,0:T(8,128)(2,1)} %param.22) | copy-start | bytes 115204
  17.4 3.2 copy-start.22
  17.4 3.2 copy-start.24
  61.0 33.8 %all-to-all-start.1 = ((bf16[64,80,128]{2,1,0:T(8,128)(2,1)}), bf16[64,80,128]{2,1,0:T(8,128)(2,1)S(1)}, u32[]{:S(2)}, u32[]{:S(2)}) async-start(bf16[64,80,128]{2,1,0:T(8,128)(2,1)} %get-tuple-element.39), calls=%async_computation.1 | async-start | bytes 2621440 | tf_op jit(solution)/shard_map/all_to_all | solution.py:64
  73.1 90.8 %copy-start.10 = (bf16[96,640]{1,0:T(8,128)(2,1)S(1)}, bf16[96,640]{1,0:T(8,128)(2,1)}, u32[]{:S(2)}) copy-start(bf16[96,640]{1,0:T(8,128)(2,1)} %concatenate.24) | copy-start | bytes 368644
  116.7 15.9 %all-to-all-start.2 = ((bf16[64,16,128]{2,1,0:T(8,128)(2,1)}), bf16[64,16,128]{2,1,0:T(8,128)(2,1)S(1)}, u32[]{:S(2)}, u32[]{:S(2)}) async-start(bf16[64,16,128]{2,1,0:T(8,128)(2,1)} %get-tuple-element.40), calls=%async_computation.2 | async-start | bytes 524288 | tf_op jit(solution)/shard_map/all_to_all | solution.py:64
  132.6 31.6 %copy-start.9 = (bf16[64,16,128]{2,1,0:T(8,128)(2,1)}, bf16[64,16,128]{2,1,0:T(8,128)(2,1)S(1)}, u32[]{:S(2)}) copy-start(bf16[64,16,128]{2,1,0:T(8,128)(2,1)S(1)} %all-to-all-done.2.recv) | copy-start | bytes 786436
  164.2 50.6 %copy-start.8 = (bf16[128,1024]{1,0:T(8,128)(2,1)S(1)}, bf16[128,1024]{1,0:T(8,128)(2,1)}, u32[]{:S(2)}) copy-start(bf16[128,1024]{1,0:T(8,128)(2,1)} %get-tuple-element.44.dyp) | copy-start | bytes 786436
  216.0 21.7 %all-to-all-start.6 = ((bf16[4,128,1024]{2,1,0:T(8,128)(2,1)}), bf16[4,128,1024]{2,1,0:T(8,128)(2,1)S(1)}, u32[]{:S(2)}, u32[]{:S(2)}) async-start(bf16[4,128,1024]{2,1,0:T(8,128)(2,1)} %broadcast_in_dim.47), calls=%async_computation.6 | async-start | bytes 2097152 | tf_op jit(solution)/shard_map/all_to_all | solution.py:64
  237.7 20.2 %copy-start.3 = (bf16[4,128,1024]{2,1,0:T(8,128)(2,1)}, bf16[4,128,1024]{2,1,0:T(8,128)(2,1)S(1)}, u32[]{:S(2)}) copy-start(bf16[4,128,1024]{2,1,0:T(8,128)(2,1)S(1)} %all-to-all-done.6.dy) | copy-start | bytes 3145732
  269.6 43.1 %copy-start.11 = (bf16[128,1024]{1,0:T(8,128)(2,1)S(1)}, bf16[128,1024]{1,0:T(8,128)(2,1)}, u32[]{:S(2)}) copy-start(bf16[128,1024]{1,0:T(8,128)(2,1)} %get-tuple-element.54) | copy-start | bytes 786436
  313.8 26.3 %all-to-all-start.11 = ((bf16[4,128,1024]{2,1,0:T(8,128)(2,1)}), bf16[4,128,1024]{2,1,0:T(8,128)(2,1)S(1)}, u32[]{:S(2)}, u32[]{:S(2)}) async-start(bf16[4,128,1024]{2,1,0:T(8,128)(2,1)} %broadcast_in_dim.48), calls=%async_computation.11 | async-start | bytes 2097152 | tf_op jit(solution)/shard_map/all_to_all | solution.py:64
  340.1 48.1 %copy-start.5 = (bf16[4,128,1024]{2,1,0:T(8,128)(2,1)}, bf16[4,128,1024]{2,1,0:T(8,128)(2,1)S(1)}, u32[]{:S(2)}) copy-start(bf16[4,128,1024]{2,1,0:T(8,128)(2,1)S(1)} %all-to-all-done.11.h1) | copy-start | bytes 3145732
  369.2 19.0 %all-to-all-start.7 = ((bf16[4,128,1024]{2,1,0:T(8,128)(2,1)}), bf16[4,128,1024]{2,1,0:T(8,128)(2,1)S(1)}, u32[]{:S(2)}, u32[]{:S(2)}) async-start(bf16[4,128,1024]{2,1,0:T(8,128)(2,1)} %get-tuple-element.45), calls=%async_computation.7 | async-start | bytes 2097152 | tf_op jit(solution)/shard_map/all_to_all | solution.py:64
  378.0 28.4 %copy-start.26 = (f32[1,1024]{1,0:T(1,128)S(1)}, f32[1,1024]{1,0:T(1,128)}, u32[]{:S(2)}) copy-start(f32[1,1024]{1,0:T(1,128)} %get-tuple-element.57) | copy-start | bytes 12292
  388.2 13.1 %copy-start.4 = (bf16[4,128,1024]{2,1,0:T(8,128)(2,1)}, bf16[4,128,1024]{2,1,0:T(8,128)(2,1)S(1)}, u32[]{:S(2)}) copy-start(bf16[4,128,1024]{2,1,0:T(8,128)(2,1)S(1)} %all-to-all-done.7.parts) | copy-start | bytes 3145732
  388.2 13.1 %all-to-all-start.12 = ((bf16[4,128,448]{1,2,0:T(8,128)(2,1)}), bf16[4,128,448]{1,2,0:T(8,128)(2,1)S(1)}, u32[]{:S(2)}, u32[]{:S(2)}) async-start(bf16[4,128,448]{1,2,0:T(8,128)(2,1)} %copy.34), calls=%async_computation.12 | async-start | bytes 917504 | tf_op jit(solution)/shard_map/all_to_all | solution.py:64
  402.1 34.4 %all-to-all-start.15 = ((bf16[128,32,256]{2,1,0:T(8,128)(2,1)}), bf16[128,32,256]{2,1,0:T(8,128)(2,1)S(1)}, u32[]{:S(2)}, u32[]{:S(2)}) async-start(bf16[128,32,256]{2,1,0:T(8,128)(2,1)} %bitcast.24), calls=%async_computation.15 | async-start | bytes 4194304 | tf_op jit(solution)/shard_map/all_to_all | solution.py:64
  406.4 10.8 %copy-start.7 = (bf16[4,128,448]{1,2,0:T(8,128)(2,1)S(1)}, bf16[4,128,448]{1,2,0:T(8,128)(2,1)}, u32[]{:S(2)}) copy-start(bf16[4,128,448]{1,2,0:T(8,128)(2,1)} %copy-done.6) | copy-start | bytes 1376260
  436.5 18.7 %all-to-all-start.13 = ((bf16[32,32,448]{2,1,0:T(8,128)(2,1)}), bf16[32,32,448]{2,1,0:T(8,128)(2,1)S(1)}, u32[]{:S(2)}, u32[]{:S(2)}) async-start(bf16[32,32,448]{2,1,0:T(8,128)(2,1)} %shard_map.213), calls=%async_computation.13 | async-start | bytes 2097152 | tf_op jit(solution)/shard_map/all_to_all | solution.py:64
  455.9 10.9 %all-to-all-start.16 = ((bf16[4,32,256]{2,1,0:T(8,128)(2,1)}), bf16[4,32,256]{2,1,0:T(8,128)(2,1)S(1)}, u32[]{:S(2)}, u32[]{:S(2)}) async-start(bf16[4,32,256]{2,1,0:T(8,128)(2,1)} %broadcast_in_dim.50), calls=%async_computation.16 | async-start | bytes 131072 | tf_op jit(solution)/shard_map/all_to_all | solution.py:64
  467.5 10.8 %all-to-all-start.14 = ((bf16[4,32,448]{2,1,0:T(8,128)(2,1)}), bf16[4,32,448]{2,1,0:T(8,128)(2,1)S(1)}, u32[]{:S(2)}, u32[]{:S(2)}) async-start(bf16[4,32,448]{2,1,0:T(8,128)(2,1)} %broadcast_in_dim.49), calls=%async_computation.14 | async-start | bytes 262144 | tf_op jit(solution)/shard_map/all_to_all | solution.py:64
  478.3 61.7 %all-to-all-start.17 = ((bf16[32,96,640]{2,1,0:T(8,128)(2,1)}), bf16[32,96,640]{2,1,0:T(8,128)(2,1)}, u32[]{:S(2)}, u32[]{:S(2)}) async-start(bf16[32,96,640]{2,1,0:T(8,128)(2,1)} %shard_map.215), calls=%async_computation.17 | async-start | bytes 7864320 | tf_op jit(solution)/shard_map/all_to_all | solution.py:64
  483.4 3.7 copy-start.15
  483.4 3.7 copy-start.17
  483.4 3.7 copy-start.19
  483.4 3.7 copy-start.21
  483.4 3.7 copy-start.23
  483.4 3.7 copy-start.25
  (7 other events, 13.6 us)

commit v2 on v1

--- a/solution.py
+++ b/solution.py
@@ -18,7 +18,8 @@
 WP = NB * PADB
 QKV = 1600
 FFS = 640
-QUART = 448
+QUART = 640
+HALF = 832
 T = 128
 EPSILON = 1e-05
 ROPE_BASE = 100000.0
@@ -27,6 +28,7 @@
 BF16 = jnp.bfloat16
 HIGHEST = lax.Precision.HIGHEST
 SC = ("shard", "context")
+CS = ("context", "shard")
 CT = ("context", "tensor")
 ALL = ("shard", "context", "tensor")
 QB = 8
@@ -50,13 +52,15 @@
     return lax.dot_general(a, b, (((0,), (0,)), ((), ())), preferred_element_type=F32)
 
 
-def call(fn, outs, *args, scratch=(), name=None):
+def call(fn, outs, *args, scratch=(), specs=None):
+    whole = pl.BlockSpec(memory_space=pltpu.VMEM)
     return pl.pallas_call(
         fn,
+        in_specs=[(specs or {}).get(k, whole) for k in range(len(args))],
+        out_specs=tuple(whole for _ in outs),
         out_shape=tuple(jax.ShapeDtypeStruct(s, d) for s, d in outs),
         scratch_shapes=list(scratch),
         compiler_params=pltpu.CompilerParams(vmem_limit_bytes=56 * 1024 * 1024),
-        name=name,
     )(*args)
 
 
@@ -67,6 +71,33 @@
 def to_all(v, axes):
     n = math.prod(lax.axis_size(a) for a in ((axes,) if isinstance(axes, str) else axes))
     return exchange(jnp.broadcast_to(v, (n, *v.shape)), axes)
+
+
+def swap(v, axis, bit):
+    pairs = [(i, i ^ bit) for i in range(lax.axis_size(axis))]
+    return lax.ppermute(v, axis, pairs)
+
+
+def from_tensor(v):
+    near = jnp.stack([v, swap(v, "tensor", 2)])
+    return near, swap(near, "tensor", 1)
+
+
+def gathered(v):
+    mine = lax.axis_index("shard") == 0
+    other = swap(v, "shard", 1)
+    pair = jnp.concatenate([jnp.where(mine, v, other), jnp.where(mine, other, v)], axis=0)
+    return lax.all_gather(pair, "context", axis=0, tiled=True).reshape(NB, *v.shape)
+
+
+def scattered(v):
+    n = v.shape[1]
+    flat = v.reshape(NB * n, v.shape[2])
+    part = lax.psum_scatter(flat, "context", scatter_dimension=0, tiled=True)
+    mine = lax.axis_index("shard") == 0
+    keep = jnp.where(mine, part[:n], part[n:])
+    away = jnp.where(mine, part[n:], part[:n])
+    return keep.astype(F32) + swap(away, "shard", 1).astype(F32)
 
 
 def normed(x):
@@ -108,19 +139,46 @@
         dst[row + 16 : row + 32, col : col + D] = part[:, D:]
 
 
+def first_kernel(wq, wk, wv, gain, core, out):
+    zero = jnp.zeros((BLK, 64), BF16)
+    low = wq[:, :HALF]
+    high = jnp.concatenate([wq[:, HALF:], wk[...], wv[...], zero], axis=1)
+    half = jnp.where(core[...] == 0, low.astype(F32), high.astype(F32)).astype(BF16)
+    tail = jnp.concatenate([gain[...], jnp.zeros((1, HALF), BF16)], axis=0)
+    block = jnp.concatenate([half, tail], axis=0)
+    for b in range(NB):
+        out[b] = block
+
+
+def shard_kernel(wg, wu, wd, wo, gain, e, mlp, out):
+    zero = jnp.zeros((2, FFS), BF16)
+    i = lax.broadcasted_iota(jnp.int32, (PADB, BLK), 0)
+    j = lax.broadcasted_iota(jnp.int32, (PADB, BLK), 1)
+    eye = (i == j).astype(F32).astype(BF16)
+    mlp[0:32, :] = dot(eye, wg[...]).astype(BF16)
+    mlp[30:31, :] = gain[...]
+    mlp[32:64, :] = dot(eye, wu[...]).astype(BF16)
+    mlp[64:96, :] = dot_t(eye, wd[...]).astype(BF16)
+    out[...] = dot(eye, dot(wo[...], e[...]).astype(BF16)).astype(BF16)
+
+
 def pad_kernel(x, dy, e, xp, dyp):
     xp[...] = dot(x[...], e[...]).astype(BF16)
     dyp[...] = dot(dy[...], e[...]).astype(BF16)
 
 
-def project_kernel(xp, gain, w, cos, sin, send, h1_out, rows):
+def project_kernel(xp, gain, wa, wb, core, cos, sin, send, h1_out, rows):
     n1, _ = normed(xp[...].astype(F32))
     h1 = (n1 * gain[...]).astype(BF16)
     h1_out[...] = h1
-    qkv = dot(h1, w[...].reshape(WP, QKV))
+    ya = dot(h1, wa[...].reshape(WP, HALF))
+    yb = dot(h1, wb[...].reshape(WP, HALF))
+    first = core[...] == 0
+    low = jnp.where(first, ya, yb)
+    high = jnp.where(first, yb, ya)
+    qkv = jnp.concatenate([low, high[:, : QKV - HALF]], axis=1)
     for j in range(10):
         part = turn(qkv[:, 128 * j : 128 * j + 128], cos[...], sin[...])
-        lane = lax.broadcasted_iota(jnp.int32, part.shape, 1) + 128 * j
         rows[:, 128 * j : 128 * j + 128] = part
     send[60:64] = jnp.zeros((4, 80, 128), BF16)
     for unit, row, col in units():
@@ -266,64 +324,63 @@
     h2_out[...] = (n2 * gain[...]).astype(BF16)
 
 
-def mlp_kernel(h2, dy, w, part, dh2, act, dgate, dup):
+def mlp_kernel(near, far, dnear, dfar, w, part, part_far, dh2, dh2_far, act, dgate, dup):
     wg = w[:, 0:32, :].reshape(WP, FFS)
     wu = w[:, 32:64, :].reshape(WP, FFS)
     wd = w[:, 64:96, :].reshape(WP, FFS)
     for i in range(4):
-        h = h2[i]
+        h = near[i] if i < 2 else far[i - 2]
+        dy = dnear[i] if i < 2 else dfar[i - 2]
         gate = dot(h, wg)
         up = dot(h, wu)
         sig = jax.nn.sigmoid(gate)
         silu = gate * sig
         a = (silu * up).astype(BF16)
         act[i] = a
-        part[i] = dot_t(a, wd).astype(BF16)
-        dact = dot(dy[i], wd)
+        y = dot_t(a, wd).astype(BF16)
+        dact = dot(dy, wd)
         dg = (dact * up * sig * (1.0 + gate * (1.0 - sig))).astype(BF16)
         du = (dact * silu).astype(BF16)
         dgate[i] = dg
         dup[i] = du
-        dh2[i] = (dot_t(dg, wg) + dot_t(du, wu)).astype(BF16)
-
-
-def mlp_grad_kernel(h2, dy, act, dgate, dup, out):
-    h = h2[...].reshape(4 * T, WP)
+        back = (dot_t(dg, wg) + dot_t(du, wu)).astype(BF16)
+        if i < 2:
+            part[i] = y
+            dh2[i] = back
+        else:
+            part_far[i - 2] = y
+            dh2_far[i - 2] = back
+
+
+def mlp_grad_kernel(near, far, dnear, dfar, act, dgate, dup, out):
+    h = jnp.concatenate([near[...].reshape(2 * T, WP), far[...].reshape(2 * T, WP)], axis=0)
+    d = jnp.concatenate([dnear[...].reshape(2 * T, WP), dfar[...].reshape(2 * T, WP)], axis=0)
     out[:, 0:32, :] = tdot(h, dgate[...].reshape(4 * T, FFS)).astype(BF16).reshape(NB, 32, FFS)
     out[:, 32:64, :] = tdot(h, dup[...].reshape(4 * T, FFS)).astype(BF16).reshape(NB, 32, FFS)
-    d = dy[...].reshape(4 * T, WP)
     out[:, 64:96, :] = tdot(d, act[...].reshape(4 * T, FFS)).astype(BF16).reshape(NB, 32, FFS)
 
 
-def mixed_kernel(parts, x1, e, out):
-    total = jnp.sum(parts[...].astype(F32), axis=0)
+def mixed_kernel(own, away, x1, e, out):
+    total = own[0].astype(F32) + away[...].astype(F32)
     out[...] = dot_t((x1[...] + total).astype(BF16), e[...]).astype(BF16)
 
 
-def mid_back_kernel(parts, x1, gain, dyp, w, e, dx1_out, da_out, send, gain_part, dol):
-    dh2 = jnp.sum(parts[...].astype(F32), axis=0)
+def mid_back_kernel(own, away, x1, gain, dyp, w, e, dx1_out, da_out, send, gain_part, dol):
+    dh2 = own[0].astype(F32) + away[...].astype(F32)
     n2, r2 = normed(x1[...])
     gain_part[...] = jnp.sum(dh2 * n2, axis=0, keepdims=True)
     dx1 = dyp[...].astype(F32) + norm_back(dh2 * gain[...], n2, r2)
     dx1_out[...] = dx1
     da = dx1.astype(BF16)
-    da_out[...] = da
+    da_out[...] = dot_t(da, e[...]).astype(BF16)
     wide = dot_t(da, w[...].reshape(WP, WP)).astype(BF16)
     dol[...] = dot_t(wide, e[...]).astype(BF16)
     send[60:64] = jnp.zeros((4, 16, 128), BF16)
     pack_rows(dol, send, 0)
 
 
-def out_grad_kernel(olp, da, out):
-    for t in range(4):
-        out[:, t] = (
-            tdot(olp[...], da[:, 256 * t : 256 * t + 256]).astype(BF16).reshape(NB, 32, 256)
-        )
-
-
-def unpack_back_kernel(recv, cos, sin, full, send, rows):
+def unpack_back_kernel(recv, cos, sin, da, full, send, rows):
     unpack_rows(recv, rows, 64)
-    full[:, QKV:] = jnp.zeros((T, 4 * QUART - QKV), BF16)
     for s in range(2):
         for g in range(KH):
             total = recv[s * 30 + g * 6, 0:64, :].astype(F32)
@@ -336,32 +393,41 @@
             rows[:, 128 * j : 128 * j + 128], cos[...], -sin[...]
         ).astype(BF16)
     for t in range(4):
-        send[t] = full[:, QUART * t : QUART * t + QUART]
-
-
-def tokens_back_kernel(full, w, xp, gain, dx1, e, tokens_grad, gain_part):
-    dh1 = dot_t(full[:, :QKV], w[...].reshape(WP, QKV))
+        first = QUART * t
+        inside = min(max(QKV - first, 0), QUART)
+        if inside:
+            send[t, :, :inside] = full[:, first : first + inside]
+        if inside < QUART:
+            start = first + inside - QKV
+            send[t, :, inside:] = da[:, start : start + QUART - inside]
+
+
+def tokens_back_kernel(full, wa, wb, core, xp, gain, dx1, e, tokens_grad, gain_part):
+    low = full[:, :HALF].astype(F32)
+    high = jnp.concatenate([full[:, HALF:], jnp.zeros((T, 64), BF16)], axis=1).astype(F32)
+    first = core[...] == 0
+    ga = jnp.where(first, low, high).astype(BF16)
+    gb = jnp.where(first, high, low).astype(BF16)
+    dh1 = dot_t(ga, wa[...].reshape(WP, HALF)) + dot_t(gb, wb[...].reshape(WP, HALF))
     n1, r1 = normed(xp[...].astype(F32))
     gain_part[...] = jnp.sum(dh1 * n1, axis=0, keepdims=True)
     grad = dx1[...] + norm_back(dh1 * gain[...], n1, r1)
-    tokens_grad[...] = dot_t(grad, e[...].astype(F32), HIGHEST)
-
-
-def proj_grad_kernel(h1, dq, gains, out):
-    out[...] = (
-        tdot(h1[...].reshape(4 * T, WP), dq[...].reshape(4 * T, QUART))
-        .astype(BF16)
-        .reshape(NB, 32, QUART)
-    )
+    high_part = grad.astype(BF16)
+    rest = grad - high_part.astype(F32)
+    mid_part = rest.astype(BF16)
+    low_part = (rest - mid_part.astype(F32)).astype(BF16)
+    tokens_grad[...] = dot_t(high_part, e[...]) + (
+        dot_t(mid_part, e[...]) + dot_t(low_part, e[...])
+    )
+
+
+def proj_grad_kernel(h_near, h_far, o_near, o_far, grads_in, order, edge, gains, out):
+    h1 = jnp.concatenate([h_near[...].reshape(2 * T, WP), h_far[...].reshape(2 * T, WP)], axis=0)
+    ol = jnp.concatenate([o_near[...].reshape(2 * T, WP), o_far[...].reshape(2 * T, WP)], axis=0)
+    grads = jnp.concatenate([grads_in[order[k]] for k in range(4)], axis=0)
+    total = jnp.where(edge[...] < QKV, tdot(h1, grads), tdot(ol, grads))
+    out[...] = total.astype(BF16).reshape(NB, 32, QUART)
     out[:, 30:31, :] = gains[...]
-
-
-def pad_rows(w, extra=None):
-    rows = [w]
-    if extra is not None:
-        rows.append(jnp.pad(extra[None, :], ((0, 0), (0, w.shape[1] - extra.shape[0]))))
-    rows.append(jnp.zeros((PADB - BLK - (extra is not None), w.shape[1]), w.dtype))
-    return jnp.concatenate(rows, axis=0)
 
 
 def shards(
@@ -380,18 +446,28 @@
 ):
     i = lax.broadcasted_iota(jnp.int32, (WIDTH, WP), 0)
     j = lax.broadcasted_iota(jnp.int32, (WIDTH, WP), 1)
-    spread = (j == (i // BLK) * PADB + i % BLK).astype(BF16)
-
-    w1 = to_all(pad_rows(jnp.concatenate([w_query, key_weight, value_weight], axis=1), attn_gain), SC)
-    gain1 = w1[:, 30, :PADB].reshape(1, WP).astype(F32)
-
-    own_out = jnp.dot(w_out, spread, preferred_element_type=F32).astype(BF16)
-    own_mlp = jnp.concatenate(
-        [pad_rows(w_gate, mlp_gain), pad_rows(w_up), pad_rows(w_down.T)], axis=0
-    )
-    own_out, own_mlp, w1 = lax.optimization_barrier((own_out, own_mlp, w1))
-    w2 = to_all(pad_rows(own_out), SC)
-    w3 = to_all(own_mlp, SC)
+    block = i // BLK
+    place = (block % 16) * 2 + block // 16
+    spread = (j == place * PADB + i % BLK).astype(BF16)
+    tensor = lax.axis_index("tensor")
+    core = (tensor % 2).reshape(1, 1).astype(jnp.int32)
+
+    def gain_row(gain, width):
+        return jnp.pad(gain, (0, width - BLK)).reshape(1, width)
+
+    (w1_send,) = call(
+        first_kernel, [((NB, PADB, HALF), BF16)],
+        w_query, key_weight, value_weight, gain_row(attn_gain, HALF), core,
+    )
+    w1a = exchange(w1_send, CS)
+    w1b = swap(w1a, "tensor", 1)
+    gain1 = w1a[:, 30, :PADB].reshape(1, WP).astype(F32)
+    own_mlp, own_out = call(
+        shard_kernel, [((96, FFS), BF16), ((PADB, WP), BF16)],
+        w_gate, w_up, w_down, w_out, gain_row(mlp_gain, FFS), spread,
+    )
+    w2 = gathered(own_out)
+    w3 = gathered(own_mlp)
     gain2 = w3[:, 30, :PADB].reshape(1, WP).astype(F32)
 
     half = D // 2
@@ -408,16 +484,15 @@
         out_grad.reshape(T, WIDTH),
         spread,
     )
-    dy_all = to_all(dyp, "tensor").reshape(4, T, WP)
+    dy_near, dy_far = from_tensor(dyp)
 
     send, h1 = call(
         project_kernel,
         [((64, 80, 128), BF16), ((T, WP), BF16)],
-        xp, gain1, w1, cos, sin,
+        xp, gain1, w1a, w1b, core, cos, sin,
         scratch=[pltpu.VMEM((T, 1280), F32)],
     )
     recv = exchange(send, CT)
-    h1_all = to_all(h1, "tensor").reshape(4, T, WP)
 
     lane = jnp.arange(QN, dtype=jnp.int32)
     qpos = (
@@ -440,31 +515,36 @@
         o_recv, xp, spread, gain2, w2,
         scratch=[pltpu.VMEM((T, WIDTH), BF16)],
     )
-    h2_all = to_all(h2, "tensor").reshape(4, T, WP)
-
-    part, dh2_part, act, dgate, dup = call(
-        mlp_kernel,
-        [((4, T, WP), BF16), ((4, T, WP), BF16)] + [((4, T, FFS), BF16)] * 3,
-        h2_all, dy_all, w3,
-    )
-    dh2_recv = exchange(dh2_part, "tensor")
+    h2_near, h2_far = from_tensor(h2)
+    h1_near, h1_far = from_tensor(h1)
+    ol_near, ol_far = from_tensor(olp)
+
+    tiles = [((2, T, WP), BF16)] * 4 + [((4, T, FFS), BF16)] * 3
+    part, part_far, dh2, dh2_far, act, dgate, dup = call(
+        mlp_kernel, tiles, h2_near, h2_far, dy_near, dy_far, w3
+    )
+
+    def summed(own, far):
+        return (own.astype(F32) + swap(far, "tensor", 1).astype(F32)).astype(BF16)
+
+    dh2 = summed(dh2, dh2_far)
+    dh2_away = swap(dh2[1], "tensor", 2)
     (mlp_grad,) = call(
-        mlp_grad_kernel, [((NB, 96, FFS), BF16)], h2_all, dy_all, act, dgate, dup
+        mlp_grad_kernel, [((NB, 96, FFS), BF16)],
+        h2_near, h2_far, dy_near, dy_far, act, dgate, dup,
     )
 
     dx1, da, d_send, gain2_part = call(
         mid_back_kernel,
-        [((T, WP), F32), ((T, WP), BF16), ((64, 16, 128), BF16), ((1, WP), F32)],
-        dh2_recv, x1, gain2, dyp, w2, spread,
+        [((T, WP), F32), ((T, WIDTH), BF16), ((64, 16, 128), BF16), ((1, WP), F32)],
+        dh2, dh2_away, x1, gain2, dyp, w2, spread,
         scratch=[pltpu.VMEM((T, WIDTH), BF16)],
     )
     d_recv = exchange(d_send, CT)
-    part_recv = exchange(part, "tensor")
-    mlp_recv = exchange(mlp_grad, SC)
-
-    (mixed,) = call(mixed_kernel, [((T, WIDTH), BF16)], part_recv, x1, spread)
-    (out_w_grad,) = call(out_grad_kernel, [((NB, 4, 32, 256), BF16)], olp, da)
-    out_recv = exchange(out_w_grad.reshape(NB * 4, 32, 256), ALL)
+    mlp_sum = scattered(mlp_grad)
+    part = summed(part, part_far)
+    part_away = swap(part[1], "tensor", 2)
+    (mixed,) = call(mixed_kernel, [((T, WIDTH), BF16)], part, part_away, x1, spread)
 
     (back_send,) = call(
         attend_back_kernel,
@@ -476,34 +556,39 @@
 
     full, dq_send = call(
         unpack_back_kernel,
-        [((T, 4 * QUART), BF16), ((4, T, QUART), BF16)],
-        back_recv, cos, sin,
+        [((T, QKV), BF16), ((4, T, QUART), BF16)],
+        back_recv, cos, sin, da,
         scratch=[pltpu.VMEM((T, 1280), F32)],
     )
     dq_recv = exchange(dq_send, "tensor")
     tokens_grad, gain1_part = call(
         tokens_back_kernel,
         [((T, WIDTH), F32), ((1, WP), F32)],
-        full, w1, xp, gain1, dx1, spread,
+        full, w1a, w1b, core, xp, gain1, dx1, spread,
     )
     gains = jnp.concatenate(
         [gain1_part.reshape(NB, PADB), gain2_part.reshape(NB, PADB)], axis=1
     ).astype(BF16)
     gains = jnp.pad(gains, ((0, 0), (0, QUART - 2 * PADB))).reshape(NB, 1, QUART)
+    order = jnp.bitwise_xor(tensor, jnp.array([0, 2, 1, 3], jnp.int32))
+    edge = (tensor * QUART + jnp.arange(QUART, dtype=jnp.int32)).reshape(1, QUART)
     (proj_grad,) = call(
-        proj_grad_kernel, [((NB, 32, QUART), BF16)], h1_all, dq_recv, gains
-    )
-    proj_sum = jnp.sum(exchange(proj_grad, SC).astype(F32), axis=0)
-
-    mlp_sum = jnp.sum(mlp_recv.astype(F32), axis=0)
-    out_sum = jnp.sum(out_recv.astype(F32), axis=0)
-    out_all = to_all(out_sum.astype(BF16), "tensor")
-    out_all = jnp.moveaxis(out_all, 0, 1).reshape(32, WP)[:BLK].astype(BF16)
-    wout_grad = jnp.einsum("rp,dp->rd", out_all, spread, preferred_element_type=F32)
-
-    proj_all = to_all(proj_sum.astype(BF16), "tensor").astype(F32)
-    gain_sums = jnp.sum(proj_all[:, 30, : 2 * PADB], axis=0)
-    proj_full = jnp.moveaxis(proj_all[:, :BLK], 0, 1).reshape(BLK, 4 * QUART)
+        proj_grad_kernel, [((NB, 32, QUART), BF16)],
+        h1_near, h1_far, ol_near, ol_far, dq_recv, order, edge, gains,
+        specs={5: pl.BlockSpec(memory_space=pltpu.SMEM)},
+    )
+    proj_sum = jnp.sum(exchange(proj_grad, CS).astype(F32), axis=0)
+
+    near, far = from_tensor(proj_sum.astype(BF16))
+    quads = jnp.concatenate([near, far], axis=0)
+    gain_sums = jnp.sum(quads[:, 30, : 2 * PADB].astype(F32), axis=0)
+    quarters = []
+    for q in range(4):
+        apart = jnp.bitwise_xor(tensor, q)
+        at = (apart % 2) * 2 + apart // 2
+        quarters.append(lax.dynamic_index_in_dim(quads, at, 0, keepdims=False)[:BLK])
+    proj_full = jnp.concatenate(quarters, axis=1).astype(F32)
+    wout_grad = proj_full[:, QKV:]
     return (
         mixed.reshape(tokens.shape),
         tokens_grad.reshape(tokens.shape),

time: 546 us -> 367 us (0.67)
  blocking collectives: 167 us -> 21.5 us
  waiting for transfers between devices: 161 us -> 122 us
  local copies, waits for them, and re-layouts: 30.5 us -> 14.8 us
  between operations: 1.06 us -> 14.1 us
  starting transfers between devices: 67.6 us -> 74.5 us
    all_to_all x6 -> x1, blocking collectives: 167 us -> 21.5 us  [exchange(): return lax.all_to_all(v, axes, 0, 0, tiled=True)]
    all_to_all x12 -> x6, waiting for transfers between devices: 161 us -> 60.2 us  [exchange(): return lax.all_to_all(v, axes, 0, 0, tiled=True)]
    ppermute x0 -> x18, waiting for transfers between devices: none -> 49.2 us  [swap(): return lax.ppermute(v, axis, pairs)]
    ppermute x0 -> x18, starting transfers between devices: none -> 38.3 us  [swap(): return lax.ppermute(v, axis, pairs)]
    all_to_all x12 -> x6, starting transfers between devices: 67.6 us -> 36.1 us  [exchange(): return lax.all_to_all(v, axes, 0, 0, tiled=True)]
    all_gather x0 -> x2, waiting for transfers between devices: none -> 12.7 us  [gathered(): lax.all_gather(pair, 'context', axis=0, tiled=True).reshape(NB, *v.shape)]
    broadcast_in_dim x9 -> x0, local copies, waits for them, and re-layouts: 7.84 us -> none  [the longest x8 7.26 us: to_all(): return exchange(jnp.broadcast_to(v, (n, *v.shape)), axes)]
    concatenate x4 -> x0, local copies, waits for them, and re-layouts: 7.66 us -> none  [the longest x1 6.63 us: shards(): jnp.concatenate([pad_rows(w_gate, mlp_gain), pad_rows(w_up), pad_rows(w_d...]
  transfers between devices with their start and end apart: 12 -> 27, of which waited for: 10 -> 16; matrix products, arithmetic and copies ran while one was open for 5% -> 3% of each run, Pallas kernels for 11% -> 22%
where the time goes in v2:
time: 367 us; the launch traced here: 366 us
  waiting for transfers between devices  122 us (33%)
  Pallas kernels  103 us (28%)
  starting transfers between devices  74.5 us (20%)
  blocking collectives  21.5 us (6%)
  other arithmetic  15.5 us (4%)
  local copies, waits for them, and re-layouts  14.8 us (4%)
  between operations  14.1 us (4%)
    pallas_call x14, Pallas kernels, call(): pl.pallas_call(fn, in_specs=[(specs or {}).get(k, whole) for k in range(l...  103 us
    all_to_all x6, waiting for transfers between devices, exchange(): return lax.all_to_all(v, axes, 0, 0, tiled=True)  60.2 us
    ppermute x18, waiting for transfers between devices, swap(): return lax.ppermute(v, axis, pairs)  49.2 us
    ppermute x18, starting transfers between devices, swap(): return lax.ppermute(v, axis, pairs)  38.3 us
    all_to_all x6, starting transfers between devices, exchange(): return lax.all_to_all(v, axes, 0, 0, tiled=True)  36.1 us
    all_to_all x1, blocking collectives, exchange(): return lax.all_to_all(v, axes, 0, 0, tiled=True)  21.5 us
    all_gather x2, waiting for transfers between devices, gathered(): lax.all_gather(pair, 'context', axis=0, tiled=True).reshape(NB, *v.shape)  12.7 us
    unnamed x55, local copies, waits for them, and re-layouts  8.69 us
  transfers between devices with their start and end apart: 27, of which 16 were waited for; matrix products, arithmetic and copies ran while one was open for 3% of the time, Pallas kernels for 22%

profile of v2, /device:TPU:1, one launch (start us, length us, event | category | flops | bytes accessed | tf_op | source)
XLA Modules:
  0.0 365.7 jit_solution(1055374948337767854)
XLA Ops:
  10.1 3.2 fusion.9.e
  18.9 3.2 collective-permute-done.1
  26.8 7.9 %all-to-all-start = ((bf16[32,32,832]{2,1,0:T(8,128)(2,1)}), bf16[32,32,832]{2,1,0:T(8,128)(2,1)S(1)}, u32[]{:S(2)}, u32[]{:S(2)}) async-start(bf16[32,32,832]{2,1,0:T(8,128)(2,1)} %shard_map.213), calls=%async_computation | async-start | bytes 3670016 | tf_op jit(solution)/shard_map/all_to_all | solution.py:68
  39.7 20.7 %all-to-all-done.wa = bf16[32,32,832]{2,1,0:T(8,128)(2,1)S(1)} async-done(((bf16[32,32,832]{2,1,0:T(8,128)(2,1)}), bf16[32,32,832]{2,1,0:T(8,128)(2,1)S(1)}, u32[]{:S(2)}, u32[]{:S(2)}) %all-to-all-start) | async-done | bytes 1703968 | tf_op jit(solution)/shard_map/all_to_all | solution.py:68
  60.3 4.6 %collective-permute-start = (bf16[32,32,832]{2,1,0:T(8,128)(2,1)S(1)}, bf16[32,32,832]{2,1,0:T(8,128)(2,1)}, u32[]{:S(2)}, u32[]{:S(2)}) collective-permute-start(bf16[32,32,832]{2,1,0:T(8,128)(2,1)S(1)} %all-to-all-done.wa), channel_id=1, source_target_pairs={{0,1},{1,0},{2,3},{3,2},{4,5},{5,4},{6,7},{7,6},{8,9},{9,8},{10,11... | collective-permute-start | bytes 5111816 | tf_op jit(solution)/shard_map/ppermute | solution.py:78
  65.0 3.2 shard_map.212
  70.0 4.6 %shard_map.214 = (bf16[64,80,128]{2,1,0:T(8,128)(2,1)}, bf16[128,1024]{1,0:T(8,128)(2,1)}) custom-call(bf16[128,1024]{1,0:T(8,128)(2,1)} %get-tuple-element.38.xp, f32[1,1024]{1,0:T(1,128)} %reshape.260.gain, bf16[32,32,832]{2,1,0:T(8,128)(2,1)} %copy-done, bf16[32,32,832]{2,1,0:T(8,128)(2,1)} %collective-permute-done.wb, s32[1,1]{1,0:T(1,128)} %bitcast.2.core, ...), custom_call_target="tpu_custom_call" | custom-call | tf_op jit(solution)/shard_map/pallas_call | solution.py:57
  74.6 8.0 %all-to-all-start.1 = ((bf16[64,80,128]{2,1,0:T(8,128)(2,1)}), bf16[64,80,128]{2,1,0:T(8,128)(2,1)S(1)}, u32[]{:S(2)}, u32[]{:S(2)}) async-start(bf16[64,80,128]{2,1,0:T(8,128)(2,1)} %get-tuple-element.39), calls=%async_computation.1 | async-start | bytes 2621440 | tf_op jit(solution)/shard_map/all_to_all | solution.py:68
  83.2 26.3 %all-to-all-done.1.recv = bf16[64,80,128]{2,1,0:T(8,128)(2,1)S(1)} async-done(((bf16[64,80,128]{2,1,0:T(8,128)(2,1)}), bf16[64,80,128]{2,1,0:T(8,128)(2,1)S(1)}, u32[]{:S(2)}, u32[]{:S(2)}) %all-to-all-start.1) | async-done | bytes 1310752 | tf_op jit(solution)/shard_map/all_to_all | solution.py:68
  110.6 20.9 %shard_map.215 = (bf16[64,16,128]{2,1,0:T(8,128)(2,1)}, f32[8,64,256]{2,1,0:T(8,128)}, f32[8,8,256]{2,1,0:T(8,128)}) custom-call(bf16[64,80,128]{2,1,0:T(8,128)(2,1)} %copy-done.1, s32[1,256]{1,0:T(1,128)} %fusion.24.qpos), custom_call_target="tpu_custom_call" | custom-call | tf_op jit(solution)/shard_map/pallas_call | solution.py:57
  131.5 4.3 %all-to-all-start.2 = ((bf16[64,16,128]{2,1,0:T(8,128)(2,1)}), bf16[64,16,128]{2,1,0:T(8,128)(2,1)S(1)}, u32[]{:S(2)}, u32[]{:S(2)}) async-start(bf16[64,16,128]{2,1,0:T(8,128)(2,1)} %get-tuple-element.40), calls=%async_computation.2 | async-start | bytes 524288 | tf_op jit(solution)/shard_map/all_to_all | solution.py:68
  140.4 12.7 %all-gather.5.cloned.1.call-done = bf16[1024,1024]{1,0:T(8,128)(2,1)} async-done(((bf16[64,1024]{1,0:T(8,128)(2,1)}), bf16[1024,1024]{1,0:T(8,128)(2,1)}) %all-gather.5.cloned.1.call-update) | async-done | bytes 2097168 | tf_op jit(solution)/shard_map/all_gather | solution.py:90
  153.9 4.1 %shard_map.217 = (bf16[128,1024]{1,0:T(8,128)(2,1)}, f32[128,1024]{1,0:T(8,128)}, bf16[128,1024]{1,0:T(8,128)(2,1)}) custom-call(bf16[64,16,128]{2,1,0:T(8,128)(2,1)} %copy-done.13, bf16[128,1024]{1,0:T(8,128)(2,1)} %get-tuple-element.38.xp, bf16[960,1024]{1,0:T(8,128)(2,1)} %fusion.9.e, f32[1,1024]{1,0:T(1,128)} %reshape.261.gain, ...), custom_call_target="tpu_custom_call" | custom-call | tf_op jit(solution)/shard_map/pallas_call | solution.py:57
  162.7 3.3 collective-permute-done.3
  172.0 11.5 %shard_map.218 = (bf16[2,128,1024]{2,1,0:T(8,128)(2,1)}, bf16[2,128,1024]{2,1,0:T(8,128)(2,1)}, bf16[2,128,1024]{2,1,0:T(8,128)(2,1)}, bf16[2,128,1024]{2,1,0:T(...) custom-call(bf16[2,128,1024]{2,1,0:T(8,128)(2,1)} %copy-done.4, ...), custom_call_target="tpu_custom_call" | custom-call | tf_op jit(solution)/shard_map/pallas_call | solution.py:57
  183.6 6.7 %shard_map.225 = bf16[32,96,640]{2,1,0:T(8,128)(2,1)} custom-call(bf16[2,128,1024]{2,1,0:T(8,128)(2,1)} %copy-done.4, bf16[2,128,1024]{2,1,0:T(8,128)(2,1)} %copy-done.11, bf16[2,128,1024]{2,1,0:T(8,128)(2,1)} %copy-done.3, bf16[2,128,1024]{2,1,0:T(8,128)(2,1)} %copy-done.10, bf16[4,128,640]{2,1,0:T(8,128)(2,1)} %get-tuple-element.62.act, ...), custom_call_target="tpu_custom_call" | custom-call | tf_op jit(solution)/shard_map/pallas_call | solution.py:57
  196.3 6.3 %collective-permute-done.10.away = bf16[128,1024]{1,0:T(8,128)(2,1)S(1)} collective-permute-done((bf16[128,1024]{1,0:T(8,128)(2,1)S(1)}, bf16[128,1024]{1,0:T(8,128)(2,1)S(1)}, u32[]{:S(2)}, u32[]{:S(2)}) %collective-permute-start.10) | collective-permute-done | bytes 262176 | tf_op jit(solution)/shard_map/ppermute | solution.py:78
  203.3 5.8 %shard_map.220 = (f32[128,1024]{1,0:T(8,128)}, bf16[128,960]{1,0:T(8,128)(2,1)}, bf16[64,16,128]{2,1,0:T(8,128)(2,1)}, f32[1,1024]{1,0:T(1,128)}) custom-call(bf16[2,128,1024]{2,1,0:T(8,128)(2,1)} %copy-done.6, bf16[128,1024]{1,0:T(8,128)(2,1)} %copy-done.18, f32[128,1024]{1,0:T(8,128)} %get-tuple-element.47.x1, f32[1,1024]{1,0:T(1,128)} %reshape.261.gain, ...), custom_call_target="tpu_custom_call" | custom-call | tf_op jit(solution)/shard_map/pallas_call | solution.py:57
  209.1 21.5 %all_to_all.35.drecv = bf16[64,16,128]{2,1,0:T(8,128)(2,1)} all-to-all(bf16[64,16,128]{2,1,0:T(8,128)(2,1)} %get-tuple-element.50), channel_id=1, replica_groups=mesh['shard'=2,'context'=16,'tensor'=4] {'context','tensor'}, dimensions={0} | all-to-all | bytes 524288 | tf_op jit(solution)/shard_map/all_to_all | solution.py:68
  230.6 22.4 %shard_map.221 = bf16[64,80,128]{2,1,0:T(8,128)(2,1)} custom-call(bf16[64,80,128]{2,1,0:T(8,128)(2,1)} %copy-done.1, s32[1,256]{1,0:T(1,128)} %fusion.24.qpos, bf16[64,16,128]{2,1,0:T(8,128)(2,1)} %all_to_all.35.drecv, f32[8,64,256]{2,1,0:T(8,128)} %get-tuple-element.51.o_in, f32[8,8,256]{2,1,0:T(8,128)} %get-tuple-element.52.lse_in), custom_call_target="tpu_custom_call" | custom-call | tf_op jit(solution)/shard_map/pallas_call | solution.py:57
  253.0 4.8 %all-to-all-start.4 = ((bf16[64,80,128]{2,1,0:T(8,128)(2,1)}), bf16[64,80,128]{2,1,0:T(8,128)(2,1)S(1)}, u32[]{:S(2)}, u32[]{:S(2)}) async-start(bf16[64,80,128]{2,1,0:T(8,128)(2,1)} %shard_map.221), calls=%async_computation.4 | async-start | bytes 2621440 | tf_op jit(solution)/shard_map/all_to_all | solution.py:68
  260.9 19.1 %collective-permute-done.11 = bf16[128,1024]{1,0:T(8,128)(2,1)S(1)} collective-permute-done((bf16[128,1024]{1,0:T(8,128)(2,1)S(1)}, bf16[128,1024]{1,0:T(8,128)(2,1)S(1)}, u32[]{:S(2)}, u32[]{:S(2)}) %collective-permute-start.11) | collective-permute-done | bytes 262176 | tf_op jit(solution)/shard_map/ppermute | solution.py:78
  282.5 4.0 %collective-permute-done.13 = bf16[128,1024]{1,0:T(8,128)(2,1)S(1)} collective-permute-done((bf16[128,1024]{1,0:T(8,128)(2,1)S(1)}, bf16[128,1024]{1,0:T(8,128)(2,1)S(1)}, u32[]{:S(2)}, u32[]{:S(2)}) %collective-permute-start.13) | collective-permute-done | bytes 262176 | tf_op jit(solution)/shard_map/ppermute | solution.py:78
  291.7 3.5 all-to-all-start.5
  296.5 7.2 %shard_map.223 = (f32[128,960]{1,0:T(8,128)}, f32[1,1024]{1,0:T(1,128)}) custom-call(bf16[128,1600]{1,0:T(8,128)(2,1)} %get-tuple-element.54.full, bf16[32,32,832]{2,1,0:T(8,128)(2,1)} %copy-done, bf16[32,32,832]{2,1,0:T(8,128)(2,1)} %collective-permute-done.wb, s32[1,1]{1,0:T(1,128)} %bitcast.2.core, bf16[128,1024]{1,0:T(8,128)(2,1)} %get-tuple-element.38.xp, ...), custom_call_target="tpu_custom_call" | custom-call | tf_op jit(solution)/shard_map/pallas_call | solution.py:57
  307.0 4.8 %shard_map.224 = bf16[32,32,640]{2,1,0:T(8,128)(2,1)} custom-call(bf16[2,128,1024]{2,1,0:T(8,128)(2,1)} %copy-done.8, bf16[2,128,1024]{2,1,0:T(8,128)(2,1)} %copy-done.15, bf16[2,128,1024]{2,1,0:T(8,128)(2,1)} %copy-done.9, bf16[2,128,1024]{2,1,0:T(8,128)(2,1)} %collective-permute-done.14.o_far, bf16[4,128,640]{2,1,0:T(8,128)(2,1)} %copy-done.7, ...), custom_call_target="tpu_custom_call" | custom-call | tf_op jit(solution)/shard_map/pallas_call | solution.py:57
  311.8 7.5 %all-to-all-start.6 = ((bf16[32,32,640]{2,1,0:T(8,128)(2,1)}), bf16[32,32,640]{2,1,0:T(8,128)(2,1)S(1)}, u32[]{:S(2)}, u32[]{:S(2)}) async-start(bf16[32,32,640]{2,1,0:T(8,128)(2,1)} %shard_map.224), calls=%async_computation.6 | async-start | bytes 2621440 | tf_op jit(solution)/shard_map/all_to_all | solution.py:68
  322.6 3.1 collective-permute-start.8
  325.6 12.5 %all-to-all-done.6 = bf16[32,32,640]{2,1,0:T(8,128)(2,1)S(1)} async-done(((bf16[32,32,640]{2,1,0:T(8,128)(2,1)}), bf16[32,32,640]{2,1,0:T(8,128)(2,1)S(1)}, u32[]{:S(2)}, u32[]{:S(2)}) %all-to-all-start.6) | async-done | bytes 1310752 | tf_op jit(solution)/shard_map/all_to_all | solution.py:68
  338.3 3.9 %collective-permute-start.15 = (bf16[32,640]{1,0:T(8,128)(2,1)S(1)}, bf16[32,640]{1,0:T(8,128)(2,1)S(1)}, u32[]{:S(2)}, u32[]{:S(2)}) collective-permute-start(bf16[32,640]{1,0:T(8,128)(2,1)S(1)} %reduce_sum.21), channel_id=1, source_target_pairs={{0,2},{1,3},{2,0},{3,1},{4,6},{5,7},{6,4},{7,5},{8,10},{9,11},{10,... | collective-permute-start | bytes 122888 | tf_op jit(solution)/shard_map/ppermute | solution.py:78
  342.2 3.2 collective-permute-done.15
  347.4 3.4 shard_map.219
  (146 shorter events, 73.3 us)
Async XLA Ops:
  7.2 131.7 %all-gather.3.cloned.1.call-start = ((), (), s32[]{:S(2)}) async-start(), calls=%async_computation.8 | async-start | bytes 4177920 | tf_op jit(solution)/shard_map/all_gather | solution.py:90
  16.4 48.5 %copy-start.23 = (s32[2,64]{1,0:T(2,128)S(1)}, s32[2,64]{1,0:T(2,128)}, u32[]{:S(2)}) copy-start(s32[2,64]{1,0:T(2,128)} %param.14) | copy-start | bytes 1540
  16.4 5.7 %collective-permute-start.1 = (bf16[96,640]{1,0:T(8,128)(2,1)}, bf16[96,640]{1,0:T(8,128)(2,1)S(1)}, u32[]{:S(2)}, u32[]{:S(2)}) collective-permute-start(bf16[96,640]{1,0:T(8,128)(2,1)} %get-tuple-element.41), channel_id=1, source_target_pairs={{0,64},{64,0},{1,65},{65,1},{2,66},{66,2},{3,67},{67,3},{4,68},{68... | collective-permute-start | bytes 368648 | tf_op jit(solution)/shard_map/ppermute | solution.py:78
  26.8 33.6 %all-to-all-start = ((bf16[32,32,832]{2,1,0:T(8,128)(2,1)}), bf16[32,32,832]{2,1,0:T(8,128)(2,1)S(1)}, u32[]{:S(2)}, u32[]{:S(2)}) async-start(bf16[32,32,832]{2,1,0:T(8,128)(2,1)} %shard_map.213), calls=%async_computation | async-start | bytes 3670016 | tf_op jit(solution)/shard_map/all_to_all | solution.py:68
  34.7 118.5 %all-gather.5.cloned.1.call-start = ((), (), s32[]{:S(2)}) async-start(), calls=%async_computation.9 | async-start | bytes 2228224 | tf_op jit(solution)/shard_map/all_gather | solution.py:90
  34.7 4.2 %collective-permute-start.2 = (bf16[32,1024]{1,0:T(8,128)(2,1)S(1)}, bf16[32,1024]{1,0:T(8,128)(2,1)S(1)}, u32[]{:S(2)}, u32[]{:S(2)}) collective-permute-start(bf16[32,1024]{1,0:T(8,128)(2,1)S(1)} %copy-done.21), channel_id=1, source_target_pairs={{0,64},{64,0},{1,65},{65,1},{2,66},{66,2},{3,67},{67,3},{4,68},{68... | collective-permute-start | bytes 196616 | tf_op jit(solution)/shard_map/ppermute | solution.py:78
  60.3 9.7 %collective-permute-start = (bf16[32,32,832]{2,1,0:T(8,128)(2,1)S(1)}, bf16[32,32,832]{2,1,0:T(8,128)(2,1)}, u32[]{:S(2)}, u32[]{:S(2)}) collective-permute-start(bf16[32,32,832]{2,1,0:T(8,128)(2,1)S(1)} %all-to-all-done.wa), channel_id=1, source_target_pairs={{0,1},{1,0},{2,3},{3,2},{4,5},{5,4},{6,7},{7,6},{8,9},{9,8},{10,11... | collective-permute-start | bytes 5111816 | tf_op jit(solution)/shard_map/ppermute | solution.py:78
  70.0 65.8 %copy-start.12 = (bf16[128,1024]{1,0:T(8,128)(2,1)S(1)}, bf16[128,1024]{1,0:T(8,128)(2,1)}, u32[]{:S(2)}) copy-start(bf16[128,1024]{1,0:T(8,128)(2,1)} %get-tuple-element.44.dyp) | copy-start | bytes 786436
  74.6 34.8 %all-to-all-start.1 = ((bf16[64,80,128]{2,1,0:T(8,128)(2,1)}), bf16[64,80,128]{2,1,0:T(8,128)(2,1)S(1)}, u32[]{:S(2)}, u32[]{:S(2)}) async-start(bf16[64,80,128]{2,1,0:T(8,128)(2,1)} %get-tuple-element.39), calls=%async_computation.1 | async-start | bytes 2621440 | tf_op jit(solution)/shard_map/all_to_all | solution.py:68
  131.5 21.7 %all-to-all-start.2 = ((bf16[64,16,128]{2,1,0:T(8,128)(2,1)}), bf16[64,16,128]{2,1,0:T(8,128)(2,1)S(1)}, u32[]{:S(2)}, u32[]{:S(2)}) async-start(bf16[64,16,128]{2,1,0:T(8,128)(2,1)} %get-tuple-element.40), calls=%async_computation.2 | async-start | bytes 524288 | tf_op jit(solution)/shard_map/all_to_all | solution.py:68
  135.8 215.8 %reduce-scatter.2.cloned.1.call-start = ((), (), s32[]{:S(2)}) async-start(), calls=%async_computation.10 | async-start | bytes 4177920 | tf_op jit(solution)/shard_map/reduce_scatter | solution.py:96
  135.9 24.9 %collective-permute-start.5 = (bf16[128,1024]{1,0:T(8,128)(2,1)S(1)}, bf16[128,1024]{1,0:T(8,128)(2,1)S(1)}, u32[]{:S(2)}, u32[]{:S(2)}) collective-permute-start(bf16[128,1024]{1,0:T(8,128)(2,1)S(1)} %copy-done.12), channel_id=1, source_target_pairs={{0,2},{1,3},{2,0},{3,1},{4,6},{5,7},{6,4},{7,5},{8,10},{9,11},{10,... | collective-permute-start | bytes 786440 | tf_op jit(solution)/shard_map/ppermute | solution.py:78
  158.0 8.0 %collective-permute-start.3 = (bf16[128,1024]{1,0:T(8,128)(2,1)}, bf16[128,1024]{1,0:T(8,128)(2,1)S(1)}, u32[]{:S(2)}, u32[]{:S(2)}) collective-permute-start(bf16[128,1024]{1,0:T(8,128)(2,1)} %get-tuple-element.43), channel_id=1, source_target_pairs={{0,2},{1,3},{2,0},{3,1},{4,6},{5,7},{6,4},{7,5},{8,10},{9,11},{10,... | collective-permute-start | bytes 786440 | tf_op jit(solution)/shard_map/ppermute | solution.py:78
  160.8 8.9 %collective-permute-start.6 = (bf16[2,128,1024]{2,1,0:T(8,128)(2,1)S(1)}, bf16[2,128,1024]{2,1,0:T(8,128)(2,1)S(1)}, u32[]{:S(2)}, u32[]{:S(2)}) collective-permute-start(bf16[2,128,1024]{2,1,0:T(8,128)(2,1)S(1)} %pad_maximum_fusion.1.dnear), channel_id=1, source_target_pairs={{0,1},{1,0},{2,3},{3,2},{4,5},{5,4},{6,7},{7,6},{8,9},{9,8},{10,11... | collective-permute-start | bytes 1572872 | tf_op jit(solution)/shard_map/ppermute | solution.py:78
  167.0 4.2 %collective-permute-start.4 = (bf16[2,128,1024]{2,1,0:T(8,128)(2,1)S(1)}, bf16[2,128,1024]{2,1,0:T(8,128)(2,1)S(1)}, u32[]{:S(2)}, u32[]{:S(2)}) collective-permute-start(bf16[2,128,1024]{2,1,0:T(8,128)(2,1)S(1)} %pad_maximum_fusion.near), channel_id=1, source_target_pairs={{0,1},{1,0},{2,3},{3,2},{4,5},{5,4},{6,7},{7,6},{8,9},{9,8},{10,11... | collective-permute-start | bytes 1572872 | tf_op jit(solution)/shard_map/ppermute | solution.py:78
  191.3 1.9 collective-permute-start.9
  193.5 9.1 %collective-permute-start.10 = (bf16[128,1024]{1,0:T(8,128)(2,1)S(1)}, bf16[128,1024]{1,0:T(8,128)(2,1)S(1)}, u32[]{:S(2)}, u32[]{:S(2)}) collective-permute-start(bf16[128,1024]{1,0:T(8,128)(2,1)S(1)} %slice_bitcast_fusion), channel_id=1, source_target_pairs={{0,2},{1,3},{2,0},{3,1},{4,6},{5,7},{6,4},{7,5},{8,10},{9,11},{10,... | collective-permute-start | bytes 786440 | tf_op jit(solution)/shard_map/ppermute | solution.py:78
  209.1 48.7 %copy-start.19 = (bf16[128,1024]{1,0:T(8,128)(2,1)S(1)}, bf16[128,1024]{1,0:T(8,128)(2,1)}, u32[]{:S(2)}) copy-start(bf16[128,1024]{1,0:T(8,128)(2,1)} %get-tuple-element.57) | copy-start | bytes 786436
  209.1 51.7 %copy-start.20 = (bf16[128,1024]{1,0:T(8,128)(2,1)S(1)}, bf16[128,1024]{1,0:T(8,128)(2,1)}, u32[]{:S(2)}) copy-start(bf16[128,1024]{1,0:T(8,128)(2,1)} %get-tuple-element.58) | copy-start | bytes 786436
  253.0 43.4 %copy-start.22 = (f32[1,1024]{1,0:T(1,128)S(1)}, f32[1,1024]{1,0:T(1,128)}, u32[]{:S(2)}) copy-start(f32[1,1024]{1,0:T(1,128)} %get-tuple-element.61) | copy-start | bytes 12292
  253.0 34.6 %all-to-all-start.4 = ((bf16[64,80,128]{2,1,0:T(8,128)(2,1)}), bf16[64,80,128]{2,1,0:T(8,128)(2,1)S(1)}, u32[]{:S(2)}, u32[]{:S(2)}) async-start(bf16[64,80,128]{2,1,0:T(8,128)(2,1)} %shard_map.221), calls=%async_computation.4 | async-start | bytes 2621440 | tf_op jit(solution)/shard_map/all_to_all | solution.py:68
  257.8 22.2 %collective-permute-start.11 = (bf16[128,1024]{1,0:T(8,128)(2,1)S(1)}, bf16[128,1024]{1,0:T(8,128)(2,1)S(1)}, u32[]{:S(2)}, u32[]{:S(2)}) collective-permute-start(bf16[128,1024]{1,0:T(8,128)(2,1)S(1)} %copy-done.19), channel_id=1, source_target_pairs={{0,2},{1,3},{2,0},{3,1},{4,6},{5,7},{6,4},{7,5},{8,10},{9,11},{10,... | collective-permute-start | bytes 786440 | tf_op jit(solution)/shard_map/ppermute | solution.py:78
  260.8 25.8 %collective-permute-start.13 = (bf16[128,1024]{1,0:T(8,128)(2,1)S(1)}, bf16[128,1024]{1,0:T(8,128)(2,1)S(1)}, u32[]{:S(2)}, u32[]{:S(2)}) collective-permute-start(bf16[128,1024]{1,0:T(8,128)(2,1)S(1)} %copy-done.20), channel_id=1, source_target_pairs={{0,2},{1,3},{2,0},{3,1},{4,6},{5,7},{6,4},{7,5},{8,10},{9,11},{10,... | collective-permute-start | bytes 786440 | tf_op jit(solution)/shard_map/ppermute | solution.py:78
  280.0 25.3 %collective-permute-start.12 = (bf16[2,128,1024]{2,1,0:T(8,128)(2,1)S(1)}, bf16[2,128,1024]{2,1,0:T(8,128)(2,1)S(1)}, u32[]{:S(2)}, u32[]{:S(2)}) collective-permute-start(bf16[2,128,1024]{2,1,0:T(8,128)(2,1)S(1)} %pad_maximum_fusion.2.h_near), channel_id=1, source_target_pairs={{0,1},{1,0},{2,3},{3,2},{4,5},{5,4},{6,7},{7,6},{8,9},{9,8},{10,11... | collective-permute-start | bytes 1572872 | tf_op jit(solution)/shard_map/ppermute | solution.py:78
  286.6 18.8 %collective-permute-start.14 = (bf16[2,128,1024]{2,1,0:T(8,128)(2,1)S(1)}, bf16[2,128,1024]{2,1,0:T(8,128)(2,1)}, u32[]{:S(2)}, u32[]{:S(2)}) collective-permute-start(bf16[2,128,1024]{2,1,0:T(8,128)(2,1)S(1)} %pad_maximum_fusion.3.o_near), channel_id=1, source_target_pairs={{0,1},{1,0},{2,3},{3,2},{4,5},{5,4},{6,7},{7,6},{8,9},{9,8},{10,11... | collective-permute-start | bytes 1572872 | tf_op jit(solution)/shard_map/ppermute | solution.py:78
  291.7 14.4 %all-to-all-start.5 = ((bf16[4,128,640]{2,1,0:T(8,128)(2,1)}), bf16[4,128,640]{2,1,0:T(8,128)(2,1)S(1)}, u32[]{:S(2)}, u32[]{:S(2)}) async-start(bf16[4,128,640]{2,1,0:T(8,128)(2,1)} %get-tuple-element.59), calls=%async_computation.5 | async-start | bytes 1310720 | tf_op jit(solution)/shard_map/all_to_all | solution.py:68
  311.8 26.3 %all-to-all-start.6 = ((bf16[32,32,640]{2,1,0:T(8,128)(2,1)}), bf16[32,32,640]{2,1,0:T(8,128)(2,1)S(1)}, u32[]{:S(2)}, u32[]{:S(2)}) async-start(bf16[32,32,640]{2,1,0:T(8,128)(2,1)} %shard_map.224), calls=%async_computation.6 | async-start | bytes 2621440 | tf_op jit(solution)/shard_map/all_to_all | solution.py:68
  319.3 3.0 collective-permute-start.7
  322.6 24.2 %collective-permute-start.8 = (bf16[128,1024]{1,0:T(8,128)(2,1)S(1)}, bf16[128,1024]{1,0:T(8,128)(2,1)S(1)}, u32[]{:S(2)}, u32[]{:S(2)}) collective-permute-start(bf16[128,1024]{1,0:T(8,128)(2,1)S(1)} %slice_bitcast_fusion.1), channel_id=1, source_target_pairs={{0,2},{1,3},{2,0},{3,1},{4,6},{5,7},{6,4},{7,5},{8,10},{9,11},{10,... | collective-permute-start | bytes 786440 | tf_op jit(solution)/shard_map/ppermute | solution.py:78
  338.3 7.2 %collective-permute-start.15 = (bf16[32,640]{1,0:T(8,128)(2,1)S(1)}, bf16[32,640]{1,0:T(8,128)(2,1)S(1)}, u32[]{:S(2)}, u32[]{:S(2)}) collective-permute-start(bf16[32,640]{1,0:T(8,128)(2,1)S(1)} %reduce_sum.21), channel_id=1, source_target_pairs={{0,2},{1,3},{2,0},{3,1},{4,6},{5,7},{6,4},{7,5},{8,10},{9,11},{10,... | collective-permute-start | bytes 122888 | tf_op jit(solution)/shard_map/ppermute | solution.py:78
  345.5 5.4 %collective-permute-start.16 = (bf16[2,32,640]{2,1,0:T(8,128)(2,1)S(1)}, bf16[2,32,640]{2,1,0:T(8,128)(2,1)S(1)}, u32[]{:S(2)}, u32[]{:S(2)}) collective-permute-start(bf16[2,32,640]{2,1,0:T(8,128)(2,1)S(1)} %pad_maximum_fusion.7), channel_id=1, source_target_pairs={{0,1},{1,0},{2,3},{3,2},{4,5},{5,4},{6,7},{7,6},{8,9},{9,8},{10,11... | collective-permute-start | bytes 245768 | tf_op jit(solution)/shard_map/ppermute | solution.py:78
  352.6 4.9 %collective-permute-start.17 = (bf16[96,640]{1,0:T(8,128)(2,1)S(1)}, bf16[96,640]{1,0:T(8,128)(2,1)S(1)}, u32[]{:S(2)}, u32[]{:S(2)}) collective-permute-start(bf16[96,640]{1,0:T(8,128)(2,1)S(1)} %broadcast_select_fusion), channel_id=1, source_target_pairs={{0,64},{64,0},{1,65},{65,1},{2,66},{66,2},{3,67},{67,3},{4,68},{68... | collective-permute-start | bytes 368648 | tf_op jit(solution)/shard_map/ppermute | solution.py:78
  (22 other events, 209.3 us)
Sparse Core Ops, SparseCore 0:
  23.9 75.9 all-gather.2
  102.6 50.5 all-gather.4
  190.4 83.6 reduce-scatter.1

commit v3 on v2

--- a/solution.py
+++ b/solution.py
@@ -78,8 +78,12 @@
     return lax.ppermute(v, axis, pairs)
 
 
+def from_pair(v):
+    return jnp.stack([v, swap(v, "tensor", 2)])
+
+
 def from_tensor(v):
-    near = jnp.stack([v, swap(v, "tensor", 2)])
+    near = from_pair(v)
     return near, swap(near, "tensor", 1)
 
 
@@ -144,22 +148,26 @@
     low = wq[:, :HALF]
     high = jnp.concatenate([wq[:, HALF:], wk[...], wv[...], zero], axis=1)
     half = jnp.where(core[...] == 0, low.astype(F32), high.astype(F32)).astype(BF16)
-    tail = jnp.concatenate([gain[...], jnp.zeros((1, HALF), BF16)], axis=0)
+    tail = jnp.concatenate(
+        [gain[...].astype(F32), jnp.zeros((1, HALF - BLK), F32)], axis=1
+    )
+    tail = jnp.concatenate([tail, jnp.zeros_like(tail)], axis=0).astype(BF16)
     block = jnp.concatenate([half, tail], axis=0)
     for b in range(NB):
         out[b] = block
 
 
-def shard_kernel(wg, wu, wd, wo, gain, e, mlp, out):
-    zero = jnp.zeros((2, FFS), BF16)
+def shard_kernel(wg, wu, wd, wo, gain, e, out):
     i = lax.broadcasted_iota(jnp.int32, (PADB, BLK), 0)
     j = lax.broadcasted_iota(jnp.int32, (PADB, BLK), 1)
     eye = (i == j).astype(F32).astype(BF16)
-    mlp[0:32, :] = dot(eye, wg[...]).astype(BF16)
-    mlp[30:31, :] = gain[...]
-    mlp[32:64, :] = dot(eye, wu[...]).astype(BF16)
-    mlp[64:96, :] = dot_t(eye, wd[...]).astype(BF16)
-    out[...] = dot(eye, dot(wo[...], e[...]).astype(BF16)).astype(BF16)
+    out[:, 0:FFS] = dot(eye, wg[...]).astype(BF16)
+    out[:, FFS : 2 * FFS] = dot(eye, wu[...]).astype(BF16)
+    out[:, 2 * FFS : 3 * FFS] = dot(eye, wd[...]).astype(BF16)
+    row = lax.broadcasted_iota(jnp.int32, (PADB, WP), 0)
+    tail = jnp.concatenate([gain[...].astype(F32), jnp.zeros((1, WP - BLK), F32)], axis=1)
+    own = dot(eye, dot(wo[...], e[...]).astype(BF16))
+    out[:, 3 * FFS :] = jnp.where(row == BLK, tail, own).astype(BF16)
 
 
 def pad_kernel(x, dy, e, xp, dyp):
@@ -180,9 +188,9 @@
     for j in range(10):
         part = turn(qkv[:, 128 * j : 128 * j + 128], cos[...], sin[...])
         rows[:, 128 * j : 128 * j + 128] = part
-    send[60:64] = jnp.zeros((4, 80, 128), BF16)
+    send[60:64] = jnp.zeros((4, 48, 128), BF16)
     for unit, row, col in units():
-        send[unit, 64:80, :] = (
+        send[unit, 32:48, :] = (
             jnp.concatenate(
                 [rows[row : row + 16, col : col + D], rows[row + 16 : row + 32, col : col + D]],
                 axis=1,
@@ -199,7 +207,7 @@
                 axis=1,
             ).astype(BF16)
             for u in range(6):
-                send[s * 30 + g * 6 + u, 0:64, :] = both
+                send[s * 30 + g * 6 + u, 0:32, :] = both[32 * (u % 2) : 32 * (u % 2) + 32]
 
 
 def low_pair(block):
@@ -227,7 +235,7 @@
 
 
 def load_pair(ref, qb, first):
-    return ref[pl.ds(qb * 8, 8), first : first + 16, :].reshape(T, 128).astype(F32)
+    return ref[qb * 8 : qb * 8 + 8, first : first + 16, :].reshape(T, 128).astype(F32)
 
 
 def unpair(cols):
@@ -235,121 +243,115 @@
     return jnp.concatenate([flat[:T], flat[T:]], axis=1).astype(BF16).reshape(8, 16, 128)
 
 
-def attend_kernel(recv, qpos, send, o_out, lse_out, kv_t, scores):
+def key_block(recv, peer, kb):
+    own = recv[kb * 8 : kb * 8 + 8, 0:32, :].reshape(KB // 2, 128)
+    other = peer[kb * 8 : kb * 8 + 8].reshape(KB // 2, 128)
+    return jnp.concatenate([own, other], axis=0)
+
+
+def masked(raw, kpos, qpos):
+    return jnp.where(kpos[...] <= qpos[...], raw, MASKED)
+
+
+def attend_kernel(recv, peer, kpos, qpos, send, o_out, lse_out, kv_t, scores):
     for kb in range(QB):
-        block = recv[kb * 8 : kb * 8 + 8, 0:64, :].reshape(KB, 128)
-        kv_t[kb] = block.astype(F32).T.astype(BF16)
-
-    def key_block(kb):
-        return recv[pl.ds(kb * 8, 8), 0:64, :].reshape(KB, 128)
-
-    def one(qb, carry):
-        q = low_pair(load_pair(recv, qb, 64))
-
-        def first(kb, top):
-            raw = dot_t(key_block(kb), q)
+        kv_t[kb] = key_block(recv, peer, kb).astype(F32).T.astype(BF16)
+    for qb in range(QB):
+        q = low_pair(load_pair(recv, qb, 32))
+        top = jnp.full((8, QN), MASKED, F32)
+        for kb in range(qb + 1):
+            raw = dot_t(key_block(recv, peer, kb), q)
+            if kb == qb:
+                raw = masked(raw, kpos, qpos)
             scores[kb] = raw
-            return jnp.maximum(top, jnp.max(raw.reshape(KB // 8, 8, QN), axis=0))
-
-        top = lax.fori_loop(0, qb, first, jnp.full((8, QN), MASKED, F32))
-        raw = dot_t(key_block(qb), q)
-        kpos = lax.broadcasted_iota(jnp.int32, (KB, QN), 0)
-        raw = jnp.where(kpos <= qpos[...], raw, MASKED)
-        scores[qb] = raw
-        top = jnp.maximum(top, jnp.max(raw.reshape(KB // 8, 8, QN), axis=0))
+            top = jnp.maximum(top, jnp.max(raw.reshape(KB // 8, 8, QN), axis=0))
         top = jnp.max(top, axis=0, keepdims=True)
-
-        def second(kb, carry):
-            mass, acc = carry
+        mass = jnp.zeros((8, QN), F32)
+        acc = jnp.zeros((D, QN), F32)
+        for kb in range(qb + 1):
             p = jnp.exp(scores[kb] - top)
             mass = mass + jnp.sum(p.reshape(KB // 8, 8, QN), axis=0)
             acc = acc + dot(kv_t[kb, D:, :], p.astype(BF16))
-            return mass, acc
-
-        mass, acc = lax.fori_loop(
-            0, qb + 1, second, (jnp.zeros((8, QN), F32), jnp.zeros((D, QN), F32))
-        )
         mass = jnp.sum(mass, axis=0, keepdims=True)
         acc = acc / mass
         o_out[qb] = acc
         lse_out[qb] = jnp.broadcast_to(top + jnp.log(mass), (8, QN))
-        send[pl.ds(qb * 8, 8)] = unpair(acc)
-        return carry
-
-    lax.fori_loop(0, QB, one, 0)
-
-
-def attend_back_kernel(recv, qpos, drecv, o_in, lse_in, send, kv_t, dkv):
+        send[qb * 8 : qb * 8 + 8] = unpair(acc)
+
+
+def attend_back_kernel(recv, peer, kpos, qpos, core, drecv, o_in, lse_in, send, kv_t, dkv):
     for kb in range(QB):
-        block = recv[kb * 8 : kb * 8 + 8, 0:64, :].reshape(KB, 128)
-        kv_t[kb] = block[:, :D].astype(F32).T.astype(BF16)
+        kv_t[kb] = key_block(recv, peer, kb)[:, :D].astype(F32).T.astype(BF16)
     dkv[...] = jnp.zeros_like(dkv)
-
-    def one(qb, carry):
-        q = low_pair(load_pair(recv, qb, 64))
+    for qb in range(QB):
+        q = low_pair(load_pair(recv, qb, 32))
         pair = load_pair(drecv, qb, 0)
         dz = high_pair(pair)
         flat = jnp.concatenate([pair[:, :D], pair[:, D:]], axis=0)
         delta = jnp.sum(flat.T * o_in[qb], axis=0, keepdims=True)
         lse = lse_in[qb][0:1]
-
-        def tile(kb, acc, diagonal):
-            block = recv[pl.ds(kb * 8, 8), 0:64, :].reshape(KB, 128)
+        acc = jnp.zeros((D, QN), F32)
+        for kb in range(qb + 1):
+            block = key_block(recv, peer, kb)
             raw = dot_t(block, q)
-            if diagonal:
-                kpos = lax.broadcasted_iota(jnp.int32, (KB, QN), 0)
-                raw = jnp.where(kpos <= qpos[...], raw, MASKED)
+            if kb == qb:
+                raw = masked(raw, kpos, qpos)
             p = jnp.exp(raw - lse)
             ds = (p * (dot_t(block, dz) - delta)).astype(BF16)
             dkv[kb] += dot(ds, q) + dot(p.astype(BF16), dz)
-            return acc + dot(kv_t[kb], ds)
-
-        acc = lax.fori_loop(0, qb, lambda kb, a: tile(kb, a, False), jnp.zeros((D, QN), F32))
-        acc = tile(qb, acc, True)
-        send[pl.ds(qb * 8, 8), 64:80, :] = unpair(acc * 0.125)
-        return carry
-
-    lax.fori_loop(0, QB, one, 0)
+            acc = acc + dot(kv_t[kb], ds)
+        send[qb * 8 : qb * 8 + 8, 64:80, :] = unpair(acc * 0.125)
     for kb in range(QB):
-        send[kb * 8 : kb * 8 + 8, 0:64, :] = dkv[kb].astype(BF16).reshape(8, 64, 128)
+        own = dkv[kb, : KB // 2, :]
+        other = dkv[kb, KB // 2 :, :]
+        low = jnp.where(core[...] == 0, own, other)
+        high = jnp.where(core[...] == 0, other, own)
+        send[kb * 8 : kb * 8 + 8, 0:32, :] = low.astype(BF16).reshape(8, 32, 128)
+        send[kb * 8 : kb * 8 + 8, 32:64, :] = high.astype(BF16).reshape(8, 32, 128)
 
 
 def out_kernel(recv, xp, e, gain, w, olp_out, x1_out, h2_out, ol):
     unpack_rows(recv, ol, 0)
     olp = dot(ol[...], e[...]).astype(BF16)
     olp_out[...] = olp
-    x1 = xp[...].astype(F32) + dot(olp, w[...].reshape(WP, WP))
+    x1 = xp[...].astype(F32) + dot(olp, w[:, :, 3 * FFS :].reshape(WP, WP))
     x1_out[...] = x1
     n2, _ = normed(x1)
     h2_out[...] = (n2 * gain[...]).astype(BF16)
 
 
-def mlp_kernel(near, far, dnear, dfar, w, part, part_far, dh2, dh2_far, act, dgate, dup):
-    wg = w[:, 0:32, :].reshape(WP, FFS)
-    wu = w[:, 32:64, :].reshape(WP, FFS)
-    wd = w[:, 64:96, :].reshape(WP, FFS)
-    for i in range(4):
+def mlp_kernel(near, far, dnear, dfar, w, dh2, dh2_far, act, dgate, dup):
+    wg = w[:, :, 0:FFS].reshape(WP, FFS)
+    wu = w[:, :, FFS : 2 * FFS].reshape(WP, FFS)
+    wd = w[:, :, 2 * FFS : 3 * FFS].reshape(WP, FFS)
+    for i in (2, 3, 0, 1):
         h = near[i] if i < 2 else far[i - 2]
         dy = dnear[i] if i < 2 else dfar[i - 2]
         gate = dot(h, wg)
         up = dot(h, wu)
+        dact = dot(dy, wd)
         sig = jax.nn.sigmoid(gate)
         silu = gate * sig
-        a = (silu * up).astype(BF16)
-        act[i] = a
-        y = dot_t(a, wd).astype(BF16)
-        dact = dot(dy, wd)
+        act[i] = (silu * up).astype(BF16)
         dg = (dact * up * sig * (1.0 + gate * (1.0 - sig))).astype(BF16)
         du = (dact * silu).astype(BF16)
         dgate[i] = dg
         dup[i] = du
         back = (dot_t(dg, wg) + dot_t(du, wu)).astype(BF16)
         if i < 2:
-            part[i] = y
             dh2[i] = back
         else:
+            dh2_far[i - 2] = back
+
+
+def mlp_part_kernel(act, w, part, part_far):
+    wd = w[:, :, 2 * FFS : 3 * FFS].reshape(WP, FFS)
+    for i in range(4):
+        y = dot_t(act[i], wd).astype(BF16)
+        if i < 2:
+            part[i] = y
+        else:
             part_far[i - 2] = y
-            dh2_far[i - 2] = back
 
 
 def mlp_grad_kernel(near, far, dnear, dfar, act, dgate, dup, out):
@@ -373,7 +375,7 @@
     dx1_out[...] = dx1
     da = dx1.astype(BF16)
     da_out[...] = dot_t(da, e[...]).astype(BF16)
-    wide = dot_t(da, w[...].reshape(WP, WP)).astype(BF16)
+    wide = dot_t(da, w[:, :, 3 * FFS :].reshape(WP, WP)).astype(BF16)
     dol[...] = dot_t(wide, e[...]).astype(BF16)
     send[60:64] = jnp.zeros((4, 16, 128), BF16)
     pack_rows(dol, send, 0)
@@ -452,23 +454,22 @@
     tensor = lax.axis_index("tensor")
     core = (tensor % 2).reshape(1, 1).astype(jnp.int32)
 
-    def gain_row(gain, width):
-        return jnp.pad(gain, (0, width - BLK)).reshape(1, width)
-
     (w1_send,) = call(
         first_kernel, [((NB, PADB, HALF), BF16)],
-        w_query, key_weight, value_weight, gain_row(attn_gain, HALF), core,
+        w_query, key_weight, value_weight, attn_gain.reshape(1, BLK), core,
     )
     w1a = exchange(w1_send, CS)
-    w1b = swap(w1a, "tensor", 1)
     gain1 = w1a[:, 30, :PADB].reshape(1, WP).astype(F32)
-    own_mlp, own_out = call(
-        shard_kernel, [((96, FFS), BF16), ((PADB, WP), BF16)],
-        w_gate, w_up, w_down, w_out, gain_row(mlp_gain, FFS), spread,
-    )
-    w2 = gathered(own_out)
-    w3 = gathered(own_mlp)
-    gain2 = w3[:, 30, :PADB].reshape(1, WP).astype(F32)
+    w_gate, w_up, w_down, w_out, mlp_gain, tokens, w1_send = lax.optimization_barrier(
+        (w_gate, w_up, w_down, w_out, mlp_gain, tokens, w1_send)
+    )
+    (own,) = call(
+        shard_kernel, [((PADB, 3 * FFS + WP), BF16)],
+        w_gate, w_up, w_down.T, w_out, mlp_gain.reshape(1, BLK), spread,
+    )
+    own, w1a = lax.optimization_barrier((own, w1a))
+    w2 = gathered(own)
+    gain2 = w2[:, 30, 3 * FFS : 3 * FFS + PADB].reshape(1, WP).astype(F32)
 
     half = D // 2
     freq = ROPE_BASE ** (-2.0 * jnp.arange(half, dtype=F32) / D)
@@ -485,14 +486,25 @@
         spread,
     )
     dy_near, dy_far = from_tensor(dyp)
+    held, xp = lax.optimization_barrier((w1a, xp))
+    w1b = swap(held, "tensor", 1)
 
     send, h1 = call(
         project_kernel,
-        [((64, 80, 128), BF16), ((T, WP), BF16)],
+        [((64, 48, 128), BF16), ((T, WP), BF16)],
         xp, gain1, w1a, w1b, core, cos, sin,
         scratch=[pltpu.VMEM((T, 1280), F32)],
     )
     recv = exchange(send, CT)
+    peer = swap(recv[:, :32, :], "tensor", 1)
+    h1, peer = lax.optimization_barrier((h1, peer))
+    h1_near = from_pair(h1)
+    row = jnp.arange(KB, dtype=jnp.int32)
+    kpos = (
+        64 * ((row % (KB // 2)) // 32)
+        + 32 * jnp.bitwise_xor(tensor % 2, row // (KB // 2))
+        + row % 32
+    ).reshape(KB, 1)
 
     lane = jnp.arange(QN, dtype=jnp.int32)
     qpos = (
@@ -504,9 +516,11 @@
     o_send, o_cols, lse = call(
         attend_kernel,
         [((64, 16, 128), BF16), ((QB, D, QN), F32), ((QB, 8, QN), F32)],
-        recv, qpos,
+        recv, peer, kpos, qpos,
         scratch=[pltpu.VMEM((QB, 128, KB), BF16), pltpu.VMEM((QB, KB, QN), F32)],
     )
+    o_send, h1_near = lax.optimization_barrier((o_send, h1_near))
+    h1_far = swap(h1_near, "tensor", 1)
     o_recv = exchange(o_send, CT)
 
     olp, x1, h2 = call(
@@ -516,23 +530,22 @@
         scratch=[pltpu.VMEM((T, WIDTH), BF16)],
     )
     h2_near, h2_far = from_tensor(h2)
-    h1_near, h1_far = from_tensor(h1)
-    ol_near, ol_far = from_tensor(olp)
-
-    tiles = [((2, T, WP), BF16)] * 4 + [((4, T, FFS), BF16)] * 3
-    part, part_far, dh2, dh2_far, act, dgate, dup = call(
-        mlp_kernel, tiles, h2_near, h2_far, dy_near, dy_far, w3
-    )
+    olp, h2_far = lax.optimization_barrier((olp, h2_far))
+    ol_near = from_pair(olp)
+
+    tiles = [((2, T, WP), BF16)] * 2 + [((4, T, FFS), BF16)] * 3
+    dh2, dh2_far, act, dgate, dup = call(
+        mlp_kernel, tiles, h2_near, h2_far, dy_near, dy_far, w2
+    )
+    part, part_far = call(mlp_part_kernel, [((2, T, WP), BF16)] * 2, act, w2)
 
     def summed(own, far):
         return (own.astype(F32) + swap(far, "tensor", 1).astype(F32)).astype(BF16)
 
     dh2 = summed(dh2, dh2_far)
+    dh2, ol_near = lax.optimization_barrier((dh2, ol_near))
     dh2_away = swap(dh2[1], "tensor", 2)
-    (mlp_grad,) = call(
-        mlp_grad_kernel, [((NB, 96, FFS), BF16)],
-        h2_near, h2_far, dy_near, dy_far, act, dgate, dup,
-    )
+    ol_far = swap(ol_near, "tensor", 1)
 
     dx1, da, d_send, gain2_part = call(
         mid_back_kernel,
@@ -540,19 +553,26 @@
         dh2, dh2_away, x1, gain2, dyp, w2, spread,
         scratch=[pltpu.VMEM((T, WIDTH), BF16)],
     )
+    act, dgate, dup, d_send = lax.optimization_barrier((act, dgate, dup, d_send))
     d_recv = exchange(d_send, CT)
+    (mlp_grad,) = call(
+        mlp_grad_kernel, [((NB, 96, FFS), BF16)],
+        h2_near, h2_far, dy_near, dy_far, act, dgate, dup,
+    )
     mlp_sum = scattered(mlp_grad)
     part = summed(part, part_far)
+    part, d_recv = lax.optimization_barrier((part, d_recv))
     part_away = swap(part[1], "tensor", 2)
-    (mixed,) = call(mixed_kernel, [((T, WIDTH), BF16)], part, part_away, x1, spread)
-
     (back_send,) = call(
         attend_back_kernel,
         [((64, 80, 128), BF16)],
-        recv, qpos, d_recv, o_cols, lse,
+        recv, peer, kpos, qpos, core, d_recv, o_cols, lse,
         scratch=[pltpu.VMEM((QB, D, KB), BF16), pltpu.VMEM((QB, KB, 128), F32)],
     )
+    back_send, part_away = lax.optimization_barrier((back_send, part_away))
     back_recv = exchange(back_send, CT)
+    (mixed,) = call(mixed_kernel, [((T, WIDTH), BF16)], part, part_away, x1, spread)
+    back_recv, mixed = lax.optimization_barrier((back_recv, mixed))
 
     full, dq_send = call(
         unpack_back_kernel,

time: 367 us -> 344 us (0.937); the launches traced: 366 us -> 338 us
  blocking collectives: 21.5 us -> 47.5 us
  waiting for transfers between devices: 122 us -> 100 us
  starting transfers between devices: 74.5 us -> 55.2 us
  Pallas kernels: 103 us -> 93.3 us
  local copies, waits for them, and re-layouts: 14.8 us -> 9.65 us
    all_to_all x1 -> x2, blocking collectives: 21.5 us -> 47.5 us  [exchange(): return lax.all_to_all(v, axes, 0, 0, tiled=True)]
    ppermute x18, starting transfers between devices: 38.3 us -> 21.8 us  [swap(): return lax.ppermute(v, axis, pairs)]
    ppermute x18, waiting for transfers between devices: 49.2 us -> 38.8 us  [swap(): return lax.ppermute(v, axis, pairs)]
    pallas_call x14 -> x15, Pallas kernels: 103 us -> 93.3 us  [call(): pl.pallas_call(fn, in_specs=[(specs or {}).get(k, whole) for k in range(l...]
    all_to_all x6 -> x5, waiting for transfers between devices: 60.2 us -> 51.2 us  [exchange(): return lax.all_to_all(v, axes, 0, 0, tiled=True)]
    unnamed x55 -> x48, local copies, waits for them, and re-layouts: 8.69 us -> 5.31 us
    all_to_all x6 -> x5, starting transfers between devices: 36.1 us -> 33.3 us  [exchange(): return lax.all_to_all(v, axes, 0, 0, tiled=True)]
    all_gather x2 -> x1, waiting for transfers between devices: 12.7 us -> 10.1 us  [gathered(): lax.all_gather(pair, 'context', axis=0, tiled=True).reshape(NB, *v.shape)]
  transfers between devices with their start and end apart: 27 -> 25, of which waited for: 16 -> 17; matrix products, arithmetic and copies ran while one was open for 3% -> 5% of each run, Pallas kernels for 22% -> 18%
where the time goes in v3:
time: 344 us; the launch traced here: 338 us
  waiting for transfers between devices  100 us (29%)
  Pallas kernels  93.3 us (27%)
  starting transfers between devices  55.2 us (16%)
  blocking collectives  47.5 us (14%)
  other arithmetic  17.9 us (5%)
  between operations  14.8 us (4%)
  local copies, waits for them, and re-layouts  9.65 us (3%)
    pallas_call x15, Pallas kernels, call(): pl.pallas_call(fn, in_specs=[(specs or {}).get(k, whole) for k in range(l...  93.3 us
    all_to_all x5, waiting for transfers between devices, exchange(): return lax.all_to_all(v, axes, 0, 0, tiled=True)  51.2 us
    all_to_all x2, blocking collectives, exchange(): return lax.all_to_all(v, axes, 0, 0, tiled=True)  47.5 us
    ppermute x18, waiting for transfers between devices, swap(): return lax.ppermute(v, axis, pairs)  38.8 us
    all_to_all x5, starting transfers between devices, exchange(): return lax.all_to_all(v, axes, 0, 0, tiled=True)  33.3 us
    ppermute x18, starting transfers between devices, swap(): return lax.ppermute(v, axis, pairs)  21.8 us
    all_gather x1, waiting for transfers between devices, gathered(): lax.all_gather(pair, 'context', axis=0, tiled=True).reshape(NB, *v.shape)  10.1 us
  transfers between devices with their start and end apart: 25, of which 17 were waited for; matrix products, arithmetic and copies ran while one was open for 5% of the time, Pallas kernels for 18%

profile of v3, /device:TPU:1, one launch (start us, length us, event | category | flops | bytes accessed | tf_op | source)
XLA Modules:
  0.0 338.5 jit_solution(1844784675815358420)
XLA Ops:
  9.6 9.2 %all-to-all-start = ((bf16[32,32,832]{2,1,0:T(8,128)(2,1)}), bf16[32,32,832]{2,1,0:T(8,128)(2,1)S(1)}, u32[]{:S(2)}, u32[]{:S(2)}) async-start(bf16[32,32,832]{2,1,0:T(8,128)(2,1)} %shard_map.212), calls=%async_computation | async-start | bytes 3670016 | tf_op jit(solution)/shard_map/all_to_all | solution.py:68
  18.9 3.2 fusion.9.e
  22.1 3.0 shard_map.213
  25.1 18.5 %all-to-all-done.wa = bf16[32,32,832]{2,1,0:T(8,128)(2,1)S(1)} async-done(((bf16[32,32,832]{2,1,0:T(8,128)(2,1)}), bf16[32,32,832]{2,1,0:T(8,128)(2,1)S(1)}, u32[]{:S(2)}, u32[]{:S(2)}) %all-to-all-start) | async-done | bytes 1703968 | tf_op jit(solution)/shard_map/all_to_all | solution.py:68
  43.9 4.3 %collective-permute-done.3 = bf16[32,2944]{1,0:T(8,128)(2,1)S(1)} collective-permute-done((bf16[32,2944]{1,0:T(8,128)(2,1)}, bf16[32,2944]{1,0:T(8,128)(2,1)S(1)}, u32[]{:S(2)}, u32[]{:S(2)}) %collective-permute-start.3) | collective-permute-done | bytes 188448 | tf_op jit(solution)/shard_map/ppermute | solution.py:78
  50.0 3.2 shard_map.214
  53.2 2.9 collective-permute-start
  59.7 4.5 %shard_map.215 = (bf16[64,48,128]{2,1,0:T(8,128)(2,1)}, bf16[128,1024]{1,0:T(8,128)(2,1)}) custom-call(bf16[128,1024]{1,0:T(8,128)(2,1)} %get-tuple-element.72.xp, f32[1,1024]{1,0:T(1,128)} %reshape.387.gain, bf16[32,32,832]{2,1,0:T(8,128)(2,1)} %copy-done, bf16[32,32,832]{2,1,0:T(8,128)(2,1)} %collective-permute-done.wb, s32[1,1]{1,0:T(1,128)} %bitcast.1.core, ...), custom_call_target="tpu_custom_call" | custom-call | tf_op jit(solution)/shard_map/pallas_call | solution.py:57
  64.2 24.4 %all_to_all.35.recv = bf16[64,48,128]{2,1,0:T(8,128)(2,1)S(1)} all-to-all(bf16[64,48,128]{2,1,0:T(8,128)(2,1)} %get-tuple-element.74), channel_id=1, replica_groups=mesh['shard'=2,'context'=16,'tensor'=4] {'context','tensor'}, dimensions={0} | all-to-all | bytes 1572864 | tf_op jit(solution)/shard_map/all_to_all | solution.py:68
  92.4 10.4 %shard_map.216 = (bf16[64,16,128]{2,1,0:T(8,128)(2,1)}, f32[8,64,256]{2,1,0:T(8,128)}, f32[8,8,256]{2,1,0:T(8,128)}) custom-call(bf16[64,48,128]{2,1,0:T(8,128)(2,1)} %copy-done.1, bf16[64,32,128]{2,1,0:T(8,128)(2,1)} %copy-done.10, s32[512,1]{1,0:T(8,128)} %fusion.13.kpos, s32[1,256]{1,0:T(1,128)} %fusion.40.qpos), custom_call_target="tpu_custom_call" | custom-call | tf_op jit(solution)/shard_map/pallas_call | solution.py:57
  102.9 7.3 %all-to-all-start.2 = ((bf16[64,16,128]{2,1,0:T(8,128)(2,1)}), bf16[64,16,128]{2,1,0:T(8,128)(2,1)S(1)}, u32[]{:S(2)}, u32[]{:S(2)}) async-start(bf16[64,16,128]{2,1,0:T(8,128)(2,1)} %get-tuple-element.79), calls=%async_computation.2 | async-start | bytes 524288 | tf_op jit(solution)/shard_map/all_to_all | solution.py:68
  110.3 10.1 %all-gather.2.cloned.1.call-done = bf16[1024,2944]{1,0:T(8,128)(2,1)} async-done(((bf16[64,2944]{1,0:T(8,128)(2,1)}), bf16[1024,2944]{1,0:T(8,128)(2,1)}) %all-gather.2.cloned.1.call-update) | async-done | bytes 6029328 | tf_op jit(solution)/shard_map/all_gather | solution.py:94
  125.1 5.2 %shard_map.217 = (bf16[128,1024]{1,0:T(8,128)(2,1)}, f32[128,1024]{1,0:T(8,128)}, bf16[128,1024]{1,0:T(8,128)(2,1)}) custom-call(bf16[64,16,128]{2,1,0:T(8,128)(2,1)} %copy-done.15, bf16[128,1024]{1,0:T(8,128)(2,1)} %get-tuple-element.72.xp, bf16[960,1024]{1,0:T(8,128)(2,1)} %fusion.9.e, f32[1,1024]{1,0:T(1,128)} %reshape.388.gain, ...), custom_call_target="tpu_custom_call" | custom-call | tf_op jit(solution)/shard_map/pallas_call | solution.py:57
  133.3 6.3 %collective-permute-done.4 = bf16[128,1024]{1,0:T(8,128)(2,1)S(1)} collective-permute-done((bf16[128,1024]{1,0:T(8,128)(2,1)}, bf16[128,1024]{1,0:T(8,128)(2,1)S(1)}, u32[]{:S(2)}, u32[]{:S(2)}) %collective-permute-start.4) | collective-permute-done | bytes 262176 | tf_op jit(solution)/shard_map/ppermute | solution.py:78
  149.1 10.2 %shard_map.218 = (bf16[2,128,1024]{2,1,0:T(8,128)(2,1)}, bf16[2,128,1024]{2,1,0:T(8,128)(2,1)}, bf16[4,128,640]{2,1,0:T(8,128)(2,1)}, bf16[4,128,640]{2,1,0:T(8,128)(2,1)}, bf16[4,128,640]{2,1,0:T(8,128)(2,1)}) custom-call(bf16[2,128,1024]{2,1,0:T(8,128)(2,1)} %copy-done.3, bf16[2,128,1024]{2,1,0:T(8,128)(2,1)} %copy-done.11, ...), custom_call_target="tpu_custom_call" | custom-call | tf_op jit(solution)/shard_map/pallas_call | solution.py:57
  160.1 8.8 %collective-permute-done.10 = bf16[128,1024]{1,0:T(8,128)(2,1)S(1)} collective-permute-done((bf16[128,1024]{1,0:T(8,128)(2,1)S(1)}, bf16[128,1024]{1,0:T(8,128)(2,1)S(1)}, u32[]{:S(2)}, u32[]{:S(2)}) %collective-permute-start.10) | collective-permute-done | bytes 262176 | tf_op jit(solution)/shard_map/ppermute | solution.py:78
  171.1 7.8 %collective-permute-done.11.away = bf16[128,1024]{1,0:T(8,128)(2,1)S(1)} collective-permute-done((bf16[128,1024]{1,0:T(8,128)(2,1)S(1)}, bf16[128,1024]{1,0:T(8,128)(2,1)S(1)}, u32[]{:S(2)}, u32[]{:S(2)}) %collective-permute-start.11) | collective-permute-done | bytes 262176 | tf_op jit(solution)/shard_map/ppermute | solution.py:78
  179.6 6.9 %shard_map.220 = (f32[128,1024]{1,0:T(8,128)}, bf16[128,960]{1,0:T(8,128)(2,1)}, bf16[64,16,128]{2,1,0:T(8,128)(2,1)}, f32[1,1024]{1,0:T(1,128)}) custom-call(bf16[2,128,1024]{2,1,0:T(8,128)(2,1)} %copy-done.6, bf16[128,1024]{1,0:T(8,128)(2,1)} %copy-done.18, f32[128,1024]{1,0:T(8,128)} %get-tuple-element.94.x1, f32[1,1024]{1,0:T(1,128)} %reshape.388.gain, ...), custom_call_target="tpu_custom_call" | custom-call | tf_op jit(solution)/shard_map/pallas_call | solution.py:57
  186.5 6.8 %shard_map.226 = bf16[32,96,640]{2,1,0:T(8,128)(2,1)} custom-call(bf16[2,128,1024]{2,1,0:T(8,128)(2,1)} %copy-done.3, bf16[2,128,1024]{2,1,0:T(8,128)(2,1)} %copy-done.11, bf16[2,128,1024]{2,1,0:T(8,128)(2,1)} %copy-done.4, bf16[2,128,1024]{2,1,0:T(8,128)(2,1)} %copy-done.12, bf16[4,128,640]{2,1,0:T(8,128)(2,1)} %get-tuple-element.114.act, ...), custom_call_target="tpu_custom_call" | custom-call | tf_op jit(solution)/shard_map/pallas_call | solution.py:57
  193.3 5.5 %shard_map.219 = (bf16[2,128,1024]{2,1,0:T(8,128)(2,1)}, bf16[2,128,1024]{2,1,0:T(8,128)(2,1)}) custom-call(bf16[4,128,640]{2,1,0:T(8,128)(2,1)} %get-tuple-element.114.act, bf16[32,32,2944]{2,1,0:T(8,128)(2,1)} %bitcast.40), custom_call_target="tpu_custom_call" | custom-call | tf_op jit(solution)/shard_map/pallas_call | solution.py:57
  200.6 6.2 %all-to-all-start.3 = ((bf16[64,16,128]{2,1,0:T(8,128)(2,1)}), bf16[64,16,128]{2,1,0:T(8,128)(2,1)S(1)}, u32[]{:S(2)}, u32[]{:S(2)}) async-start(bf16[64,16,128]{2,1,0:T(8,128)(2,1)} %get-tuple-element.96), calls=%async_computation.3 | async-start | bytes 524288 | tf_op jit(solution)/shard_map/all_to_all | solution.py:68
  208.0 11.3 %all-to-all-done.3.drecv = bf16[64,16,128]{2,1,0:T(8,128)(2,1)S(1)} async-done(((bf16[64,16,128]{2,1,0:T(8,128)(2,1)}), bf16[64,16,128]{2,1,0:T(8,128)(2,1)S(1)}, u32[]{:S(2)}, u32[]{:S(2)}) %all-to-all-start.3) | async-done | bytes 262176 | tf_op jit(solution)/shard_map/all_to_all | solution.py:68
  220.0 16.8 %shard_map.221 = bf16[64,80,128]{2,1,0:T(8,128)(2,1)} custom-call(bf16[64,48,128]{2,1,0:T(8,128)(2,1)} %copy-done.1, bf16[64,32,128]{2,1,0:T(8,128)(2,1)} %copy-done.10, s32[512,1]{1,0:T(8,128)} %fusion.13.kpos, s32[1,256]{1,0:T(1,128)} %fusion.40.qpos, s32[1,1]{1,0:T(1,128)} %bitcast.1.core, bf16[64,16,128]{2,1,0:T(8,128)(2,1)} %copy-done.13, ...), custom_call_target="tpu_custom_call" | custom-call | tf_op jit(solution)/shard_map/pallas_call | solution.py:57
  237.5 6.8 %all-to-all-start.4 = ((bf16[64,80,128]{2,1,0:T(8,128)(2,1)}), bf16[64,80,128]{2,1,0:T(8,128)(2,1)S(1)}, u32[]{:S(2)}, u32[]{:S(2)}) async-start(bf16[64,80,128]{2,1,0:T(8,128)(2,1)} %shard_map.221), calls=%async_computation.4 | async-start | bytes 2621440 | tf_op jit(solution)/shard_map/all_to_all | solution.py:68
  245.0 3.4 %shard_map.222 = bf16[128,960]{1,0:T(8,128)(2,1)} custom-call(bf16[2,128,1024]{2,1,0:T(8,128)(2,1)} %copy-done.5, bf16[128,1024]{1,0:T(8,128)(2,1)} %copy-done.17, f32[128,1024]{1,0:T(8,128)} %get-tuple-element.94.x1, bf16[960,1024]{1,0:T(8,128)(2,1)} %fusion.9.e), custom_call_target="tpu_custom_call" | custom-call | tf_op jit(solution)/shard_map/pallas_call | solution.py:57
  248.4 18.1 %all-to-all-done.4.recv = bf16[64,80,128]{2,1,0:T(8,128)(2,1)S(1)} async-done(((bf16[64,80,128]{2,1,0:T(8,128)(2,1)}), bf16[64,80,128]{2,1,0:T(8,128)(2,1)S(1)}, u32[]{:S(2)}, u32[]{:S(2)}) %all-to-all-start.4) | async-done | bytes 1310752 | tf_op jit(solution)/shard_map/all_to_all | solution.py:68
  267.6 3.0 shard_map.223
  270.7 3.8 %all-to-all-start.5 = ((bf16[4,128,640]{2,1,0:T(8,128)(2,1)}), bf16[4,128,640]{2,1,0:T(8,128)(2,1)S(1)}, u32[]{:S(2)}, u32[]{:S(2)}) async-start(bf16[4,128,640]{2,1,0:T(8,128)(2,1)} %get-tuple-element.111), calls=%async_computation.5 | async-start | bytes 1310720 | tf_op jit(solution)/shard_map/all_to_all | solution.py:68
  275.7 7.3 %shard_map.224 = (f32[128,960]{1,0:T(8,128)}, f32[1,1024]{1,0:T(1,128)}) custom-call(bf16[128,1600]{1,0:T(8,128)(2,1)} %get-tuple-element.106.full, bf16[32,32,832]{2,1,0:T(8,128)(2,1)} %copy-done, bf16[32,32,832]{2,1,0:T(8,128)(2,1)} %collective-permute-done.wb, s32[1,1]{1,0:T(1,128)} %bitcast.1.core, bf16[128,1024]{1,0:T(8,128)(2,1)} %get-tuple-element.72.xp, ...), custom_call_target="tpu_custom_call" | custom-call | tf_op jit(solution)/shard_map/pallas_call | solution.py:57
  286.3 4.8 %shard_map.225 = bf16[32,32,640]{2,1,0:T(8,128)(2,1)} custom-call(bf16[2,128,1024]{2,1,0:T(8,128)(2,1)} %copy-done.8, bf16[2,128,1024]{2,1,0:T(8,128)(2,1)} %copy-done.16, bf16[2,128,1024]{2,1,0:T(8,128)(2,1)} %copy-done.9, bf16[2,128,1024]{2,1,0:T(8,128)(2,1)} %collective-permute-done.14.o_far, bf16[4,128,640]{2,1,0:T(8,128)(2,1)} %copy-done.7, ...), custom_call_target="tpu_custom_call" | custom-call | tf_op jit(solution)/shard_map/pallas_call | solution.py:57
  291.1 23.1 %all_to_all.36 = bf16[32,32,640]{2,1,0:T(8,128)(2,1)S(1)} all-to-all(bf16[32,32,640]{2,1,0:T(8,128)(2,1)} %shard_map.225), channel_id=1, replica_groups=mesh['shard'=2,'context'=16,'tensor'=4] {'context','shard'}, dimensions={0} | all-to-all | bytes 2621440 | tf_op jit(solution)/shard_map/all_to_all | solution.py:68
  314.3 3.6 %collective-permute-start.15 = (bf16[32,640]{1,0:T(8,128)(2,1)S(1)}, bf16[32,640]{1,0:T(8,128)(2,1)S(1)}, u32[]{:S(2)}, u32[]{:S(2)}) collective-permute-start(bf16[32,640]{1,0:T(8,128)(2,1)S(1)} %reduce_sum.21), channel_id=1, source_target_pairs={{0,2},{1,3},{2,0},{3,1},{4,6},{5,7},{6,4},{7,5},{8,10},{9,11},{10,... | collective-permute-start | bytes 122888 | tf_op jit(solution)/shard_map/ppermute | solution.py:78
  (132 shorter events, 56.8 us)
Async XLA Ops:
  9.6 34.0 %all-to-all-start = ((bf16[32,32,832]{2,1,0:T(8,128)(2,1)}), bf16[32,32,832]{2,1,0:T(8,128)(2,1)S(1)}, u32[]{:S(2)}, u32[]{:S(2)}) async-start(bf16[32,32,832]{2,1,0:T(8,128)(2,1)} %shard_map.212), calls=%async_computation | async-start | bytes 3670016 | tf_op jit(solution)/shard_map/all_to_all | solution.py:68
  18.8 101.6 %all-gather.2.cloned.1.call-start = ((), (), s32[]{:S(2)}) async-start(), calls=%async_computation.8 | async-start | bytes 6406144 | tf_op jit(solution)/shard_map/all_gather | solution.py:94
  18.9 37.2 %copy-start.22 = (s32[2,64]{1,0:T(2,128)S(1)}, s32[2,64]{1,0:T(2,128)}, u32[]{:S(2)}) copy-start(s32[2,64]{1,0:T(2,128)} %param.14) | copy-start | bytes 1540
  43.6 4.6 %collective-permute-start.3 = (bf16[32,2944]{1,0:T(8,128)(2,1)}, bf16[32,2944]{1,0:T(8,128)(2,1)S(1)}, u32[]{:S(2)}, u32[]{:S(2)}) collective-permute-start(bf16[32,2944]{1,0:T(8,128)(2,1)} %shard_map.213), channel_id=1, source_target_pairs={{0,64},{64,0},{1,65},{65,1},{2,66},{66,2},{3,67},{67,3},{4,68},{68... | collective-permute-start | bytes 565256 | tf_op jit(solution)/shard_map/ppermute | solution.py:78
  53.2 6.5 %collective-permute-start = (bf16[32,32,832]{2,1,0:T(8,128)(2,1)S(1)}, bf16[32,32,832]{2,1,0:T(8,128)(2,1)}, u32[]{:S(2)}, u32[]{:S(2)}) collective-permute-start(bf16[32,32,832]{2,1,0:T(8,128)(2,1)S(1)} %all-to-all-done.wa), channel_id=1, source_target_pairs={{0,1},{1,0},{2,3},{3,2},{4,5},{5,4},{6,7},{7,6},{8,9},{9,8},{10,11... | collective-permute-start | bytes 5111816 | tf_op jit(solution)/shard_map/ppermute | solution.py:78
  64.2 38.7 %copy-start.20 = (bf16[128,1024]{1,0:T(8,128)(2,1)S(1)}, bf16[128,1024]{1,0:T(8,128)(2,1)}, u32[]{:S(2)}) copy-start(bf16[128,1024]{1,0:T(8,128)(2,1)} %get-tuple-element.78) | copy-start | bytes 786436
  88.6 2.0 collective-permute-start.1
  90.6 12.3 %collective-permute-start.2 = (bf16[128,1024]{1,0:T(8,128)(2,1)}, bf16[128,1024]{1,0:T(8,128)(2,1)S(1)}, u32[]{:S(2)}, u32[]{:S(2)}) collective-permute-start(bf16[128,1024]{1,0:T(8,128)(2,1)} %get-tuple-element.78), channel_id=1, source_target_pairs={{0,2},{1,3},{2,0},{3,1},{4,6},{5,7},{6,4},{7,5},{8,10},{9,11},{10,... | collective-permute-start | bytes 786440 | tf_op jit(solution)/shard_map/ppermute | solution.py:78
  102.9 141.4 %copy-start.8 = (bf16[2,128,1024]{2,1,0:T(8,128)(2,1)}, bf16[2,128,1024]{2,1,0:T(8,128)(2,1)S(1)}, u32[]{:S(2)}) copy-start(bf16[2,128,1024]{2,1,0:T(8,128)(2,1)S(1)} %pad_maximum_fusion.h_near) | copy-start | bytes 1572868
  102.9 21.5 %all-to-all-start.2 = ((bf16[64,16,128]{2,1,0:T(8,128)(2,1)}), bf16[64,16,128]{2,1,0:T(8,128)(2,1)S(1)}, u32[]{:S(2)}, u32[]{:S(2)}) async-start(bf16[64,16,128]{2,1,0:T(8,128)(2,1)} %get-tuple-element.79), calls=%async_computation.2 | async-start | bytes 524288 | tf_op jit(solution)/shard_map/all_to_all | solution.py:68
  110.2 213.6 %reduce-scatter.2.cloned.1.call-start = ((), (), s32[]{:S(2)}) async-start(), calls=%async_computation.9 | async-start | bytes 4177920 | tf_op jit(solution)/shard_map/reduce_scatter | solution.py:100
  130.3 9.3 %collective-permute-start.4 = (bf16[128,1024]{1,0:T(8,128)(2,1)}, bf16[128,1024]{1,0:T(8,128)(2,1)S(1)}, u32[]{:S(2)}, u32[]{:S(2)}) collective-permute-start(bf16[128,1024]{1,0:T(8,128)(2,1)} %get-tuple-element.81), channel_id=1, source_target_pairs={{0,2},{1,3},{2,0},{3,1},{4,6},{5,7},{6,4},{7,5},{8,10},{9,11},{10,... | collective-permute-start | bytes 786440 | tf_op jit(solution)/shard_map/ppermute | solution.py:78
  130.7 14.6 %collective-permute-start.6 = (bf16[128,1024]{1,0:T(8,128)(2,1)S(1)}, bf16[128,1024]{1,0:T(8,128)(2,1)S(1)}, u32[]{:S(2)}, u32[]{:S(2)}) collective-permute-start(bf16[128,1024]{1,0:T(8,128)(2,1)S(1)} %copy-done.14), channel_id=1, source_target_pairs={{0,2},{1,3},{2,0},{3,1},{4,6},{5,7},{6,4},{7,5},{8,10},{9,11},{10,... | collective-permute-start | bytes 786440 | tf_op jit(solution)/shard_map/ppermute | solution.py:78
  140.7 6.0 %collective-permute-start.5 = (bf16[2,128,1024]{2,1,0:T(8,128)(2,1)S(1)}, bf16[2,128,1024]{2,1,0:T(8,128)(2,1)S(1)}, u32[]{:S(2)}, u32[]{:S(2)}) collective-permute-start(bf16[2,128,1024]{2,1,0:T(8,128)(2,1)S(1)} %pad_maximum_fusion.1.near), channel_id=1, source_target_pairs={{0,1},{1,0},{2,3},{3,2},{4,5},{5,4},{6,7},{7,6},{8,9},{9,8},{10,11... | collective-permute-start | bytes 1572872 | tf_op jit(solution)/shard_map/ppermute | solution.py:78
  145.3 2.9 collective-permute-start.7
  159.3 9.7 %collective-permute-start.9 = (bf16[2,128,1024]{2,1,0:T(8,128)(2,1)}, bf16[2,128,1024]{2,1,0:T(8,128)(2,1)S(1)}, u32[]{:S(2)}, u32[]{:S(2)}) collective-permute-start(bf16[2,128,1024]{2,1,0:T(8,128)(2,1)} %get-tuple-element.91), channel_id=1, source_target_pairs={{0,1},{1,0},{2,3},{3,2},{4,5},{5,4},{6,7},{7,6},{8,9},{9,8},{10,11... | collective-permute-start | bytes 1572872 | tf_op jit(solution)/shard_map/ppermute | solution.py:78
  159.7 9.3 %collective-permute-start.10 = (bf16[128,1024]{1,0:T(8,128)(2,1)S(1)}, bf16[128,1024]{1,0:T(8,128)(2,1)S(1)}, u32[]{:S(2)}, u32[]{:S(2)}) collective-permute-start(bf16[128,1024]{1,0:T(8,128)(2,1)S(1)} %copy-done.19), channel_id=1, source_target_pairs={{0,2},{1,3},{2,0},{3,1},{4,6},{5,7},{6,4},{7,5},{8,10},{9,11},{10,... | collective-permute-start | bytes 786440 | tf_op jit(solution)/shard_map/ppermute | solution.py:78
  169.0 75.9 %copy-start.9 = (bf16[2,128,1024]{2,1,0:T(8,128)(2,1)}, bf16[2,128,1024]{2,1,0:T(8,128)(2,1)S(1)}, u32[]{:S(2)}) copy-start(bf16[2,128,1024]{2,1,0:T(8,128)(2,1)S(1)} %pad_maximum_fusion.3.o_near) | copy-start | bytes 1572868
  170.5 8.4 %collective-permute-start.11 = (bf16[128,1024]{1,0:T(8,128)(2,1)S(1)}, bf16[128,1024]{1,0:T(8,128)(2,1)S(1)}, u32[]{:S(2)}, u32[]{:S(2)}) collective-permute-start(bf16[128,1024]{1,0:T(8,128)(2,1)S(1)} %slice_bitcast_fusion.1), channel_id=1, source_target_pairs={{0,2},{1,3},{2,0},{3,1},{4,6},{5,7},{6,4},{7,5},{8,10},{9,11},{10,... | collective-permute-start | bytes 786440 | tf_op jit(solution)/shard_map/ppermute | solution.py:78
  198.7 8.0 %collective-permute-start.8 = (bf16[2,128,1024]{2,1,0:T(8,128)(2,1)}, bf16[2,128,1024]{2,1,0:T(8,128)(2,1)S(1)}, u32[]{:S(2)}, u32[]{:S(2)}) collective-permute-start(bf16[2,128,1024]{2,1,0:T(8,128)(2,1)} %get-tuple-element.87), channel_id=1, source_target_pairs={{0,1},{1,0},{2,3},{3,2},{4,5},{5,4},{6,7},{7,6},{8,9},{9,8},{10,11... | collective-permute-start | bytes 1572872 | tf_op jit(solution)/shard_map/ppermute | solution.py:78
  200.6 18.7 %all-to-all-start.3 = ((bf16[64,16,128]{2,1,0:T(8,128)(2,1)}), bf16[64,16,128]{2,1,0:T(8,128)(2,1)S(1)}, u32[]{:S(2)}, u32[]{:S(2)}) async-start(bf16[64,16,128]{2,1,0:T(8,128)(2,1)} %get-tuple-element.96), calls=%async_computation.3 | async-start | bytes 524288 | tf_op jit(solution)/shard_map/all_to_all | solution.py:68
  208.0 36.9 %copy-start.5 = (bf16[2,128,1024]{2,1,0:T(8,128)(2,1)}, bf16[2,128,1024]{2,1,0:T(8,128)(2,1)S(1)}, u32[]{:S(2)}) copy-start(bf16[2,128,1024]{2,1,0:T(8,128)(2,1)S(1)} %add_convert_fusion.1.own) | copy-start | bytes 1572868
  219.4 17.4 %collective-permute-start.12 = (bf16[128,1024]{1,0:T(8,128)(2,1)S(1)}, bf16[128,1024]{1,0:T(8,128)(2,1)S(1)}, u32[]{:S(2)}, u32[]{:S(2)}) collective-permute-start(bf16[128,1024]{1,0:T(8,128)(2,1)S(1)} %slice_bitcast_fusion), channel_id=1, source_target_pairs={{0,2},{1,3},{2,0},{3,1},{4,6},{5,7},{6,4},{7,5},{8,10},{9,11},{10,... | collective-permute-start | bytes 786440 | tf_op jit(solution)/shard_map/ppermute | solution.py:78
  237.5 29.0 %all-to-all-start.4 = ((bf16[64,80,128]{2,1,0:T(8,128)(2,1)}), bf16[64,80,128]{2,1,0:T(8,128)(2,1)S(1)}, u32[]{:S(2)}, u32[]{:S(2)}) async-start(bf16[64,80,128]{2,1,0:T(8,128)(2,1)} %shard_map.221), calls=%async_computation.4 | async-start | bytes 2621440 | tf_op jit(solution)/shard_map/all_to_all | solution.py:68
  244.3 30.2 %copy-start.23 = (s32[4]{0:T(128)S(1)}, s32[4]{0:T(128)}, u32[]{:S(2)}) copy-start(s32[4]{0:T(128)} %constant.237.clone) | copy-start | bytes 52
  244.3 31.3 %copy-start.21 = (f32[1,1024]{1,0:T(1,128)S(1)}, f32[1,1024]{1,0:T(1,128)}, u32[]{:S(2)}) copy-start(f32[1,1024]{1,0:T(1,128)} %get-tuple-element.113) | copy-start | bytes 12292
  244.3 40.2 %collective-permute-start.13 = (bf16[2,128,1024]{2,1,0:T(8,128)(2,1)S(1)}, bf16[2,128,1024]{2,1,0:T(8,128)(2,1)S(1)}, u32[]{:S(2)}, u32[]{:S(2)}) collective-permute-start(bf16[2,128,1024]{2,1,0:T(8,128)(2,1)S(1)} %pad_maximum_fusion.h_near), channel_id=1, source_target_pairs={{0,1},{1,0},{2,3},{3,2},{4,5},{5,4},{6,7},{7,6},{8,9},{9,8},{10,11... | collective-permute-start | bytes 1572872 | tf_op jit(solution)/shard_map/ppermute | solution.py:78
  244.9 39.7 %collective-permute-start.14 = (bf16[2,128,1024]{2,1,0:T(8,128)(2,1)S(1)}, bf16[2,128,1024]{2,1,0:T(8,128)(2,1)}, u32[]{:S(2)}, u32[]{:S(2)}) collective-permute-start(bf16[2,128,1024]{2,1,0:T(8,128)(2,1)S(1)} %pad_maximum_fusion.3.o_near), channel_id=1, source_target_pairs={{0,1},{1,0},{2,3},{3,2},{4,5},{5,4},{6,7},{7,6},{8,9},{9,8},{10,11... | collective-permute-start | bytes 1572872 | tf_op jit(solution)/shard_map/ppermute | solution.py:78
  270.7 14.7 %all-to-all-start.5 = ((bf16[4,128,640]{2,1,0:T(8,128)(2,1)}), bf16[4,128,640]{2,1,0:T(8,128)(2,1)S(1)}, u32[]{:S(2)}, u32[]{:S(2)}) async-start(bf16[4,128,640]{2,1,0:T(8,128)(2,1)} %get-tuple-element.111), calls=%async_computation.5 | async-start | bytes 1310720 | tf_op jit(solution)/shard_map/all_to_all | solution.py:68
  314.3 5.0 %collective-permute-start.15 = (bf16[32,640]{1,0:T(8,128)(2,1)S(1)}, bf16[32,640]{1,0:T(8,128)(2,1)S(1)}, u32[]{:S(2)}, u32[]{:S(2)}) collective-permute-start(bf16[32,640]{1,0:T(8,128)(2,1)S(1)} %reduce_sum.21), channel_id=1, source_target_pairs={{0,2},{1,3},{2,0},{3,1},{4,6},{5,7},{6,4},{7,5},{8,10},{9,11},{10,... | collective-permute-start | bytes 122888 | tf_op jit(solution)/shard_map/ppermute | solution.py:78
  319.4 3.7 %collective-permute-start.16 = (bf16[2,32,640]{2,1,0:T(8,128)(2,1)S(1)}, bf16[2,32,640]{2,1,0:T(8,128)(2,1)S(1)}, u32[]{:S(2)}, u32[]{:S(2)}) collective-permute-start(bf16[2,32,640]{2,1,0:T(8,128)(2,1)S(1)} %pad_maximum_fusion.6), channel_id=1, source_target_pairs={{0,1},{1,0},{2,3},{3,2},{4,5},{5,4},{6,7},{7,6},{8,9},{9,8},{10,11... | collective-permute-start | bytes 245768 | tf_op jit(solution)/shard_map/ppermute | solution.py:78
  324.8 4.6 %collective-permute-start.17 = (bf16[96,640]{1,0:T(8,128)(2,1)S(1)}, bf16[96,640]{1,0:T(8,128)(2,1)S(1)}, u32[]{:S(2)}, u32[]{:S(2)}) collective-permute-start(bf16[96,640]{1,0:T(8,128)(2,1)S(1)} %broadcast_select_fusion.2), channel_id=1, source_target_pairs={{0,64},{64,0},{1,65},{65,1},{2,66},{66,2},{3,67},{67,3},{4,68},{68... | collective-permute-start | bytes 368648 | tf_op jit(solution)/shard_map/ppermute | solution.py:78
  (17 other events, 70.5 us)
Sparse Core Ops, SparseCore 0:
  50.1 70.1 all-gather.1
  193.4 83.2 reduce-scatter.1

commit v4 on v3

--- a/solution.py
+++ b/solution.py
@@ -2,6 +2,7 @@
 
 import jax
 import jax.numpy as jnp
+import numpy as np
 from jax import lax
 from jax.experimental import pallas as pl
 from jax.experimental.pallas import tpu as pltpu
@@ -87,17 +88,24 @@
     return near, swap(near, "tensor", 1)
 
 
-def gathered(v):
+def paired(v):
     mine = lax.axis_index("shard") == 0
     other = swap(v, "shard", 1)
-    pair = jnp.concatenate([jnp.where(mine, v, other), jnp.where(mine, other, v)], axis=0)
-    return lax.all_gather(pair, "context", axis=0, tiled=True).reshape(NB, *v.shape)
+    return jnp.concatenate([jnp.where(mine, v, other), jnp.where(mine, other, v)], axis=0)
+
+
+def from_each(pieces):
+    return [pieces[0]] + [swap(pieces[k], "tensor", k) for k in range(1, 4)]
 
 
 def scattered(v):
     n = v.shape[1]
     flat = v.reshape(NB * n, v.shape[2])
-    part = lax.psum_scatter(flat, "context", scatter_dimension=0, tiled=True)
+    return lax.psum_scatter(flat, "context", scatter_dimension=0, tiled=True)
+
+
+def over_shard(part):
+    n = part.shape[0] // 2
     mine = lax.axis_index("shard") == 0
     keep = jnp.where(mine, part[:n], part[n:])
     away = jnp.where(mine, part[n:], part[:n])
@@ -157,7 +165,7 @@
         out[b] = block
 
 
-def shard_kernel(wg, wu, wd, wo, gain, e, out):
+def prep_kernel(wg, wu, wd, wo, gain, x, dy, e, out, xd):
     i = lax.broadcasted_iota(jnp.int32, (PADB, BLK), 0)
     j = lax.broadcasted_iota(jnp.int32, (PADB, BLK), 1)
     eye = (i == j).astype(F32).astype(BF16)
@@ -168,17 +176,13 @@
     tail = jnp.concatenate([gain[...].astype(F32), jnp.zeros((1, WP - BLK), F32)], axis=1)
     own = dot(eye, dot(wo[...], e[...]).astype(BF16))
     out[:, 3 * FFS :] = jnp.where(row == BLK, tail, own).astype(BF16)
-
-
-def pad_kernel(x, dy, e, xp, dyp):
-    xp[...] = dot(x[...], e[...]).astype(BF16)
-    dyp[...] = dot(dy[...], e[...]).astype(BF16)
-
-
-def project_kernel(xp, gain, wa, wb, core, cos, sin, send, h1_out, rows):
-    n1, _ = normed(xp[...].astype(F32))
+    xd[0] = dot(x[...], e[...]).astype(BF16)
+    xd[1] = dot(dy[...], e[...]).astype(BF16)
+
+
+def project_kernel(xd, gain, wa, wb, core, cos, sin, send, rows):
+    n1, _ = normed(xd[0].astype(F32))
     h1 = (n1 * gain[...]).astype(BF16)
-    h1_out[...] = h1
     ya = dot(h1, wa[...].reshape(WP, HALF))
     yb = dot(h1, wb[...].reshape(WP, HALF))
     first = core[...] == 0
@@ -210,6 +214,12 @@
                 send[s * 30 + g * 6 + u, 0:32, :] = both[32 * (u % 2) : 32 * (u % 2) + 32]
 
 
+def hidden_kernel(x0, x1, x2, x3, gain, out):
+    for k, x in enumerate((x0, x1, x2, x3)):
+        n1, _ = normed(x[0].astype(F32))
+        out[T * k : T * k + T, :] = (n1 * gain[...]).astype(BF16)
+
+
 def low_pair(block):
     lane = lax.broadcasted_iota(jnp.int32, block.shape, 1)
     zero = jnp.zeros_like(block)
@@ -310,26 +320,25 @@
         send[kb * 8 : kb * 8 + 8, 32:64, :] = high.astype(BF16).reshape(8, 32, 128)
 
 
-def out_kernel(recv, xp, e, gain, w, olp_out, x1_out, h2_out, ol):
+def out_kernel(recv, xd, e, gain, w, olp_out, x1_out, h2_out, ol):
     unpack_rows(recv, ol, 0)
     olp = dot(ol[...], e[...]).astype(BF16)
     olp_out[...] = olp
-    x1 = xp[...].astype(F32) + dot(olp, w[:, :, 3 * FFS :].reshape(WP, WP))
+    x1 = xd[0].astype(F32) + dot(olp, w[:, :, 3 * FFS :].reshape(WP, WP))
     x1_out[...] = x1
     n2, _ = normed(x1)
     h2_out[...] = (n2 * gain[...]).astype(BF16)
 
 
-def mlp_kernel(near, far, dnear, dfar, w, dh2, dh2_far, act, dgate, dup):
+def mlp_kernel(h_a, h_b, dy_a, dy_b, w, back_a, back_b, act, dgate, dup):
     wg = w[:, :, 0:FFS].reshape(WP, FFS)
     wu = w[:, :, FFS : 2 * FFS].reshape(WP, FFS)
     wd = w[:, :, 2 * FFS : 3 * FFS].reshape(WP, FFS)
-    for i in (2, 3, 0, 1):
-        h = near[i] if i < 2 else far[i - 2]
-        dy = dnear[i] if i < 2 else dfar[i - 2]
+    for i, (h_in, dy_in, back) in enumerate(((h_a, dy_a, back_a), (h_b, dy_b, back_b))):
+        h = h_in[...]
         gate = dot(h, wg)
         up = dot(h, wu)
-        dact = dot(dy, wd)
+        dact = dot(dy_in[1], wd)
         sig = jax.nn.sigmoid(gate)
         silu = gate * sig
         act[i] = (silu * up).astype(BF16)
@@ -337,29 +346,27 @@
         du = (dact * silu).astype(BF16)
         dgate[i] = dg
         dup[i] = du
-        back = (dot_t(dg, wg) + dot_t(du, wu)).astype(BF16)
-        if i < 2:
-            dh2[i] = back
-        else:
-            dh2_far[i - 2] = back
-
-
-def mlp_part_kernel(act, w, part, part_far):
+        back[...] = (dot_t(dg, wg) + dot_t(du, wu)).astype(BF16)
+
+
+def mlp_part_kernel(near, far, w, part, part_far):
     wd = w[:, :, 2 * FFS : 3 * FFS].reshape(WP, FFS)
-    for i in range(4):
-        y = dot_t(act[i], wd).astype(BF16)
-        if i < 2:
-            part[i] = y
-        else:
-            part_far[i - 2] = y
-
-
-def mlp_grad_kernel(near, far, dnear, dfar, act, dgate, dup, out):
-    h = jnp.concatenate([near[...].reshape(2 * T, WP), far[...].reshape(2 * T, WP)], axis=0)
-    d = jnp.concatenate([dnear[...].reshape(2 * T, WP), dfar[...].reshape(2 * T, WP)], axis=0)
-    out[:, 0:32, :] = tdot(h, dgate[...].reshape(4 * T, FFS)).astype(BF16).reshape(NB, 32, FFS)
-    out[:, 32:64, :] = tdot(h, dup[...].reshape(4 * T, FFS)).astype(BF16).reshape(NB, 32, FFS)
-    out[:, 64:96, :] = tdot(d, act[...].reshape(4 * T, FFS)).astype(BF16).reshape(NB, 32, FFS)
+    part[0] = dot_t(near[0], wd).astype(BF16)
+    part[1] = dot_t(far[0], wd).astype(BF16)
+    part_far[0] = dot_t(near[1], wd).astype(BF16)
+    part_far[1] = dot_t(far[1], wd).astype(BF16)
+
+
+def mlp_grad_kernel(
+    h0, h1, h2, h3, d0, d1, d2, d3, act_n, act_f, gate_n, gate_f, up_n, up_f, out
+):
+    h = jnp.concatenate([h0[...], h1[...], h2[...], h3[...]], axis=0)
+    d = jnp.concatenate([d0[1], d1[1], d2[1], d3[1]], axis=0)
+    for k, (left, near, far) in enumerate(((h, gate_n, gate_f), (h, up_n, up_f), (d, act_n, act_f))):
+        right = jnp.concatenate(
+            [near[...].reshape(2 * T, FFS), far[...].reshape(2 * T, FFS)], axis=0
+        )
+        out[:, 32 * k : 32 * k + 32, :] = tdot(left, right).astype(BF16).reshape(NB, 32, FFS)
 
 
 def mixed_kernel(own, away, x1, e, out):
@@ -367,11 +374,15 @@
     out[...] = dot_t((x1[...] + total).astype(BF16), e[...]).astype(BF16)
 
 
-def mid_back_kernel(own, away, x1, gain, dyp, w, e, dx1_out, da_out, send, gain_part, dol):
-    dh2 = own[0].astype(F32) + away[...].astype(F32)
+def mid_back_kernel(
+    b0, b1, b2, b3, x1, gain, xd, w, e, dx1_out, da_out, send, gain_part, dol
+):
+    dh2 = (b0[...].astype(F32) + b1[...].astype(F32)) + (
+        b2[...].astype(F32) + b3[...].astype(F32)
+    )
     n2, r2 = normed(x1[...])
     gain_part[...] = jnp.sum(dh2 * n2, axis=0, keepdims=True)
-    dx1 = dyp[...].astype(F32) + norm_back(dh2 * gain[...], n2, r2)
+    dx1 = xd[1].astype(F32) + norm_back(dh2 * gain[...], n2, r2)
     dx1_out[...] = dx1
     da = dx1.astype(BF16)
     da_out[...] = dot_t(da, e[...]).astype(BF16)
@@ -381,7 +392,7 @@
     pack_rows(dol, send, 0)
 
 
-def unpack_back_kernel(recv, cos, sin, da, full, send, rows):
+def unpack_back_kernel(recv, cos, sin, da, slot, full, s0, s1, s2, s3, rows, held):
     unpack_rows(recv, rows, 64)
     for s in range(2):
         for g in range(KH):
@@ -398,20 +409,22 @@
         first = QUART * t
         inside = min(max(QKV - first, 0), QUART)
         if inside:
-            send[t, :, :inside] = full[:, first : first + inside]
+            held[t, :, :inside] = full[:, first : first + inside]
         if inside < QUART:
             start = first + inside - QKV
-            send[t, :, inside:] = da[:, start : start + QUART - inside]
-
-
-def tokens_back_kernel(full, wa, wb, core, xp, gain, dx1, e, tokens_grad, gain_part):
+            held[t, :, inside:] = da[:, start : start + QUART - inside]
+    for k, out in enumerate((s0, s1, s2, s3)):
+        out[...] = held[slot[k]]
+
+
+def tokens_back_kernel(full, wa, wb, core, xd, gain, dx1, e, tokens_grad, gain_part):
     low = full[:, :HALF].astype(F32)
     high = jnp.concatenate([full[:, HALF:], jnp.zeros((T, 64), BF16)], axis=1).astype(F32)
     first = core[...] == 0
     ga = jnp.where(first, low, high).astype(BF16)
     gb = jnp.where(first, high, low).astype(BF16)
     dh1 = dot_t(ga, wa[...].reshape(WP, HALF)) + dot_t(gb, wb[...].reshape(WP, HALF))
-    n1, r1 = normed(xp[...].astype(F32))
+    n1, r1 = normed(xd[0].astype(F32))
     gain_part[...] = jnp.sum(dh1 * n1, axis=0, keepdims=True)
     grad = dx1[...] + norm_back(dh1 * gain[...], n1, r1)
     high_part = grad.astype(BF16)
@@ -423,13 +436,30 @@
     )
 
 
-def proj_grad_kernel(h_near, h_far, o_near, o_far, grads_in, order, edge, gains, out):
-    h1 = jnp.concatenate([h_near[...].reshape(2 * T, WP), h_far[...].reshape(2 * T, WP)], axis=0)
-    ol = jnp.concatenate([o_near[...].reshape(2 * T, WP), o_far[...].reshape(2 * T, WP)], axis=0)
-    grads = jnp.concatenate([grads_in[order[k]] for k in range(4)], axis=0)
-    total = jnp.where(edge[...] < QKV, tdot(h1, grads), tdot(ol, grads))
+def proj_grad_kernel(h1_all, o_near, o_far, g0, g1, g2, g3, edge, gains, out):
+    ol = jnp.concatenate([o_near[0], o_far[0], o_near[1], o_far[1]], axis=0)
+    grads = jnp.concatenate([g0[...], g1[...], g2[...], g3[...]], axis=0)
+    total = jnp.where(edge[...] < QKV, tdot(h1_all[...], grads), tdot(ol, grads))
     out[...] = total.astype(BF16).reshape(NB, 32, QUART)
     out[:, 30:31, :] = gains[...]
+
+
+def total_kernel(pieces, out):
+    total = pieces[0].astype(F32)
+    for b in range(1, NB):
+        total = total + pieces[b].astype(F32)
+    out[...] = total.astype(BF16)
+
+
+def last_kernel(p0, p1, p2, p3, slot, wq, wk, wv, wo, gains, held):
+    for k, p in enumerate((p0, p1, p2, p3)):
+        held[k] = p[...].astype(F32)
+    gains[...] = held[0, 30:31, :] + held[1, 30:31, :] + held[2, 30:31, :] + held[3, 30:31, :]
+    full = jnp.concatenate([held[slot[q], :BLK, :] for q in range(4)], axis=1)
+    wq[...] = full[:, :960]
+    wk[...] = full[:, 960:1280]
+    wv[...] = full[:, 1280:QKV]
+    wo[...] = full[:, QKV:]
 
 
 def shards(
@@ -446,11 +476,11 @@
     w_up,
     w_down,
 ):
-    i = lax.broadcasted_iota(jnp.int32, (WIDTH, WP), 0)
-    j = lax.broadcasted_iota(jnp.int32, (WIDTH, WP), 1)
-    block = i // BLK
-    place = (block % 16) * 2 + block // 16
-    spread = (j == place * PADB + i % BLK).astype(BF16)
+    at = np.arange(WIDTH)
+    block = at // BLK
+    table = np.zeros((WIDTH, WP), np.float32)
+    table[at, ((block % 16) * 2 + block // 16) * PADB + at % BLK] = 1.0
+    spread = jnp.asarray(table, BF16)
     tensor = lax.axis_index("tensor")
     core = (tensor % 2).reshape(1, 1).astype(jnp.int32)
 
@@ -459,18 +489,15 @@
         w_query, key_weight, value_weight, attn_gain.reshape(1, BLK), core,
     )
     w1a = exchange(w1_send, CS)
-    gain1 = w1a[:, 30, :PADB].reshape(1, WP).astype(F32)
-    w_gate, w_up, w_down, w_out, mlp_gain, tokens, w1_send = lax.optimization_barrier(
-        (w_gate, w_up, w_down, w_out, mlp_gain, tokens, w1_send)
-    )
-    (own,) = call(
-        shard_kernel, [((PADB, 3 * FFS + WP), BF16)],
-        w_gate, w_up, w_down.T, w_out, mlp_gain.reshape(1, BLK), spread,
-    )
-    own, w1a = lax.optimization_barrier((own, w1a))
-    w2 = gathered(own)
-    gain2 = w2[:, 30, 3 * FFS : 3 * FFS + PADB].reshape(1, WP).astype(F32)
-
+    w_gate, w_up, w_down, w_out, mlp_gain, w1_send = lax.optimization_barrier(
+        (w_gate, w_up, w_down, w_out, mlp_gain, w1_send)
+    )
+    own, xd = call(
+        prep_kernel,
+        [((PADB, 3 * FFS + WP), BF16), ((2, T, WP), BF16)],
+        w_gate, w_up, w_down.T, w_out, mlp_gain.reshape(1, BLK),
+        tokens.reshape(T, WIDTH), out_grad.reshape(T, WIDTH), spread,
+    )
     half = D // 2
     freq = ROPE_BASE ** (-2.0 * jnp.arange(half, dtype=F32) / D)
     theta = positions.reshape(T).astype(F32)[:, None] * freq
@@ -478,27 +505,20 @@
     cos = jnp.concatenate([c, c, c, c], axis=1)
     sin = jnp.concatenate([-s, s, -s, s], axis=1)
 
-    xp, dyp = call(
-        pad_kernel,
-        [((T, WP), BF16), ((T, WP), BF16)],
-        tokens.reshape(T, WIDTH),
-        out_grad.reshape(T, WIDTH),
-        spread,
-    )
-    dy_near, dy_far = from_tensor(dyp)
-    held, xp = lax.optimization_barrier((w1a, xp))
-    w1b = swap(held, "tensor", 1)
-
-    send, h1 = call(
+    w1a, own, xd, cos, sin = lax.optimization_barrier((w1a, own, xd, cos, sin))
+    w1b = swap(w1a, "tensor", 1)
+    w2 = lax.all_gather(paired(own), "context", axis=0, tiled=True).reshape(NB, *own.shape)
+    gain2 = w2[:, 30, 3 * FFS : 3 * FFS + PADB].reshape(1, WP).astype(F32)
+    gain1 = w1a[:, 30, :PADB].reshape(1, WP).astype(F32)
+
+    (send,) = call(
         project_kernel,
-        [((64, 48, 128), BF16), ((T, WP), BF16)],
-        xp, gain1, w1a, w1b, core, cos, sin,
+        [((64, 48, 128), BF16)],
+        xd, gain1, w1a, w1b, core, cos, sin,
         scratch=[pltpu.VMEM((T, 1280), F32)],
     )
     recv = exchange(send, CT)
     peer = swap(recv[:, :32, :], "tensor", 1)
-    h1, peer = lax.optimization_barrier((h1, peer))
-    h1_near = from_pair(h1)
     row = jnp.arange(KB, dtype=jnp.int32)
     kpos = (
         64 * ((row % (KB // 2)) // 32)
@@ -519,104 +539,110 @@
         recv, peer, kpos, qpos,
         scratch=[pltpu.VMEM((QB, 128, KB), BF16), pltpu.VMEM((QB, KB, QN), F32)],
     )
-    o_send, h1_near = lax.optimization_barrier((o_send, h1_near))
-    h1_far = swap(h1_near, "tensor", 1)
     o_recv = exchange(o_send, CT)
+    xd, o_send = lax.optimization_barrier((xd, o_send))
+    xd_one, xd_two = swap(xd, "tensor", 1), swap(xd, "tensor", 2)
 
     olp, x1, h2 = call(
         out_kernel,
         [((T, WP), BF16), ((T, WP), F32), ((T, WP), BF16)],
-        o_recv, xp, spread, gain2, w2,
+        o_recv, xd, spread, gain2, w2,
         scratch=[pltpu.VMEM((T, WIDTH), BF16)],
     )
-    h2_near, h2_far = from_tensor(h2)
-    olp, h2_far = lax.optimization_barrier((olp, h2_far))
-    ol_near = from_pair(olp)
-
-    tiles = [((2, T, WP), BF16)] * 2 + [((4, T, FFS), BF16)] * 3
-    dh2, dh2_far, act, dgate, dup = call(
-        mlp_kernel, tiles, h2_near, h2_far, dy_near, dy_far, w2
-    )
-    part, part_far = call(mlp_part_kernel, [((2, T, WP), BF16)] * 2, act, w2)
-
-    def summed(own, far):
-        return (own.astype(F32) + swap(far, "tensor", 1).astype(F32)).astype(BF16)
-
-    dh2 = summed(dh2, dh2_far)
-    dh2, ol_near = lax.optimization_barrier((dh2, ol_near))
-    dh2_away = swap(dh2[1], "tensor", 2)
-    ol_far = swap(ol_near, "tensor", 1)
+    h2, xd_two = lax.optimization_barrier((h2, xd_two))
+    xd_three = swap(xd_two, "tensor", 1)
+    h2_one, h2_two, h2_three = (swap(h2, "tensor", k) for k in (1, 2, 3))
+    tiles = [((T, WP), BF16)] * 2 + [((2, T, FFS), BF16)] * 3
+    back0, back1, act_n, gate_n, up_n = call(
+        mlp_kernel, tiles, h2, h2_one, xd, xd_one, w2
+    )
+    h2_two, h2_three, back1 = lax.optimization_barrier((h2_two, h2_three, back1))
+    back2, back3, act_f, gate_f, up_f = call(
+        mlp_kernel, tiles, h2_two, h2_three, xd_two, xd_three, w2
+    )
+    back1, back2, back3 = (swap(b, "tensor", k + 1) for k, b in enumerate((back1, back2, back3)))
+    (mlp_grad,) = call(
+        mlp_grad_kernel, [((NB, 96, FFS), BF16)],
+        h2, h2_one, h2_two, h2_three, xd, xd_one, xd_two, xd_three,
+        act_n, act_f, gate_n, gate_f, up_n, up_f,
+    )
+    part, part_far = call(mlp_part_kernel, [((2, T, WP), BF16)] * 2, act_n, act_f, w2)
+    back1, back2, back3, mlp_grad, part, part_far = lax.optimization_barrier(
+        (back1, back2, back3, mlp_grad, part, part_far)
+    )
+    mlp_part = scattered(mlp_grad)
 
     dx1, da, d_send, gain2_part = call(
         mid_back_kernel,
         [((T, WP), F32), ((T, WIDTH), BF16), ((64, 16, 128), BF16), ((1, WP), F32)],
-        dh2, dh2_away, x1, gain2, dyp, w2, spread,
+        back0, back1, back2, back3, x1, gain2, xd, w2, spread,
         scratch=[pltpu.VMEM((T, WIDTH), BF16)],
     )
-    act, dgate, dup, d_send = lax.optimization_barrier((act, dgate, dup, d_send))
     d_recv = exchange(d_send, CT)
-    (mlp_grad,) = call(
-        mlp_grad_kernel, [((NB, 96, FFS), BF16)],
-        h2_near, h2_far, dy_near, dy_far, act, dgate, dup,
-    )
-    mlp_sum = scattered(mlp_grad)
-    part = summed(part, part_far)
-    part, d_recv = lax.optimization_barrier((part, d_recv))
+    part_far, olp, d_send = lax.optimization_barrier((part_far, olp, d_send))
+    part = part.astype(F32) + swap(part_far, "tensor", 1).astype(F32)
+    part = part.astype(BF16)
+    d_recv, part = lax.optimization_barrier((d_recv, part))
     part_away = swap(part[1], "tensor", 2)
+    ol_near = from_pair(olp)
     (back_send,) = call(
         attend_back_kernel,
         [((64, 80, 128), BF16)],
         recv, peer, kpos, qpos, core, d_recv, o_cols, lse,
         scratch=[pltpu.VMEM((QB, D, KB), BF16), pltpu.VMEM((QB, KB, 128), F32)],
     )
-    back_send, part_away = lax.optimization_barrier((back_send, part_away))
+    back_send, part_away, ol_near = lax.optimization_barrier((back_send, part_away, ol_near))
+    ol_far = swap(ol_near, "tensor", 1)
     back_recv = exchange(back_send, CT)
     (mixed,) = call(mixed_kernel, [((T, WIDTH), BF16)], part, part_away, x1, spread)
-    back_recv, mixed = lax.optimization_barrier((back_recv, mixed))
-
-    full, dq_send = call(
+    (h1_all,) = call(
+        hidden_kernel, [((4 * T, WP), BF16)], xd, xd_one, xd_two, xd_three, gain1
+    )
+    back_recv, mixed, h1_all = lax.optimization_barrier((back_recv, mixed, h1_all))
+
+    slot = jnp.bitwise_xor(tensor, jnp.arange(4, dtype=jnp.int32))
+    full, *dq_send = call(
         unpack_back_kernel,
-        [((T, QKV), BF16), ((4, T, QUART), BF16)],
-        back_recv, cos, sin, da,
-        scratch=[pltpu.VMEM((T, 1280), F32)],
-    )
-    dq_recv = exchange(dq_send, "tensor")
+        [((T, QKV), BF16)] + [((T, QUART), BF16)] * 4,
+        back_recv, cos, sin, da, slot,
+        specs={4: pl.BlockSpec(memory_space=pltpu.SMEM)},
+        scratch=[pltpu.VMEM((T, 1280), F32), pltpu.VMEM((4, T, QUART), BF16)],
+    )
+    dq_recv = from_each(dq_send)
     tokens_grad, gain1_part = call(
         tokens_back_kernel,
         [((T, WIDTH), F32), ((1, WP), F32)],
-        full, w1a, w1b, core, xp, gain1, dx1, spread,
+        full, w1a, w1b, core, xd, gain1, dx1, spread,
     )
     gains = jnp.concatenate(
         [gain1_part.reshape(NB, PADB), gain2_part.reshape(NB, PADB)], axis=1
     ).astype(BF16)
     gains = jnp.pad(gains, ((0, 0), (0, QUART - 2 * PADB))).reshape(NB, 1, QUART)
-    order = jnp.bitwise_xor(tensor, jnp.array([0, 2, 1, 3], jnp.int32))
     edge = (tensor * QUART + jnp.arange(QUART, dtype=jnp.int32)).reshape(1, QUART)
     (proj_grad,) = call(
         proj_grad_kernel, [((NB, 32, QUART), BF16)],
-        h1_near, h1_far, ol_near, ol_far, dq_recv, order, edge, gains,
-        specs={5: pl.BlockSpec(memory_space=pltpu.SMEM)},
-    )
-    proj_sum = jnp.sum(exchange(proj_grad, CS).astype(F32), axis=0)
-
-    near, far = from_tensor(proj_sum.astype(BF16))
-    quads = jnp.concatenate([near, far], axis=0)
-    gain_sums = jnp.sum(quads[:, 30, : 2 * PADB].astype(F32), axis=0)
-    quarters = []
-    for q in range(4):
-        apart = jnp.bitwise_xor(tensor, q)
-        at = (apart % 2) * 2 + apart // 2
-        quarters.append(lax.dynamic_index_in_dim(quads, at, 0, keepdims=False)[:BLK])
-    proj_full = jnp.concatenate(quarters, axis=1).astype(F32)
-    wout_grad = proj_full[:, QKV:]
+        h1_all, ol_near, ol_far, *dq_recv, edge, gains,
+    )
+    proj_recv = exchange(proj_grad, CS)
+    mlp_part, proj_grad = lax.optimization_barrier((mlp_part, proj_grad))
+    mlp_sum = over_shard(mlp_part)
+    (proj_sum,) = call(total_kernel, [((32, QUART), BF16)], proj_recv)
+    wq_grad, wk_grad, wv_grad, wo_grad, gain_sums = call(
+        last_kernel,
+        [((BLK, 960), F32), ((BLK, 320), F32), ((BLK, 320), F32), ((BLK, 960), F32), ((1, QUART), F32)],
+        *from_each([proj_sum] * 4), slot,
+        specs={4: pl.BlockSpec(memory_space=pltpu.SMEM)},
+        scratch=[pltpu.VMEM((4, 32, QUART), F32)],
+    )
+    gain_sums = gain_sums[0]
     return (
         mixed.reshape(tokens.shape),
         tokens_grad.reshape(tokens.shape),
         gain_sums[:BLK],
-        proj_full[:, :960],
-        proj_full[:, 960:1280],
-        proj_full[:, 1280:1600],
-        wout_grad,
+        wq_grad,
+        wk_grad,
+        wv_grad,
+        wo_grad,
         gain_sums[PADB : PADB + BLK],
         mlp_sum[:BLK],
         mlp_sum[32 : 32 + BLK],

time: 344 us -> 327 us (0.951)
  waiting for transfers between devices: 100 us -> 73.6 us
  Pallas kernels: 93.3 us -> 103 us
  other arithmetic: 17.9 us -> 9.35 us
    ppermute x18 -> x23, waiting for transfers between devices: 38.8 us -> 15.3 us  [swap(): return lax.ppermute(v, axis, pairs)]
    pallas_call x15 -> x18, Pallas kernels: 93.3 us -> 103 us  [call(): pl.pallas_call(fn, in_specs=[(specs or {}).get(k, whole) for k in range(l...]
    all_to_all x5 -> x4, waiting for transfers between devices: 51.2 us -> 45.5 us  [exchange(): return lax.all_to_all(v, axes, 0, 0, tiled=True)]
    convert_element_type x4 -> x1, other arithmetic: 5.92 us -> 0.19 us  [shards(): part = part.astype(BF16)]
    unnamed x48 -> x62, local copies, waits for them, and re-layouts: 5.31 us -> 8.31 us
    ppermute x18 -> x23, starting transfers between devices: 21.8 us -> 24.8 us  [swap(): return lax.ppermute(v, axis, pairs)]
    all_to_all x5 -> x4, starting transfers between devices: 33.3 us -> 32.1 us  [exchange(): return lax.all_to_all(v, axes, 0, 0, tiled=True)]
  transfers between devices with their start and end apart: 25 -> 29, of which waited for: 17 -> 11; matrix products, arithmetic and copies ran while one was open for 5% -> 3% of each run, Pallas kernels for 18% -> 31%
where the time goes in v4:
time: 327 us; the launch traced here: 321 us
  Pallas kernels  103 us (31%)
  waiting for transfers between devices  73.6 us (23%)
  starting transfers between devices  57 us (17%)
  blocking collectives  50.7 us (16%)
  between operations  14.8 us (5%)
  local copies, waits for them, and re-layouts  12.7 us (4%)
  other arithmetic  9.35 us (3%)
    pallas_call x18, Pallas kernels, call(): pl.pallas_call(fn, in_specs=[(specs or {}).get(k, whole) for k in range(l...  103 us
    all_to_all x2, blocking collectives, exchange(): return lax.all_to_all(v, axes, 0, 0, tiled=True)  50.7 us
    all_to_all x4, waiting for transfers between devices, exchange(): return lax.all_to_all(v, axes, 0, 0, tiled=True)  45.5 us
    all_to_all x4, starting transfers between devices, exchange(): return lax.all_to_all(v, axes, 0, 0, tiled=True)  32.1 us
    ppermute x23, starting transfers between devices, swap(): return lax.ppermute(v, axis, pairs)  24.8 us
    ppermute x23, waiting for transfers between devices, swap(): return lax.ppermute(v, axis, pairs)  15.3 us
    all_gather x1, waiting for transfers between devices, shards(): lax.all_gather(paired(own), 'context', axis=0, tiled=True)  12.8 us
    unnamed x62, local copies, waits for them, and re-layouts  8.31 us
  transfers between devices with their start and end apart: 29, of which 11 were waited for; matrix products, arithmetic and copies ran while one was open for 3% of the time, Pallas kernels for 31%

profile of v4, /device:TPU:1, one launch (start us, length us, event | category | flops | bytes accessed | tf_op | source)
XLA Modules:
  0.0 321.1 jit_solution(3478908750571241519)
XLA Ops:
  9.5 9.4 %all-to-all-start = ((bf16[32,32,832]{2,1,0:T(8,128)(2,1)}), bf16[32,32,832]{2,1,0:T(8,128)(2,1)S(1)}, u32[]{:S(2)}, u32[]{:S(2)}) async-start(bf16[32,32,832]{2,1,0:T(8,128)(2,1)} %shard_map.212), calls=%async_computation | async-start | bytes 3670016 | tf_op jit(solution)/shard_map/all_to_all | solution.py:69
  19.0 3.9 %shard_map.213 = (bf16[32,2944]{1,0:T(8,128)(2,1)}, bf16[2,128,1024]{2,1,0:T(8,128)(2,1)}) custom-call(bf16[30,640]{1,0:T(8,128)(2,1)} %wg, bf16[30,640]{1,0:T(8,128)(2,1)} %wu, bf16[30,640]{1,0:T(8,128)(2,1)} %bitcast.34, bf16[30,960]{1,0:T(8,128)(2,1)} %wo, bf16[1,30]{1,0:T(2,128)(2,1)} %bitcast.36, bf16[128,960]{1,0:T(8,128)(2,1)} %bitcast.29, ...), custom_call_target="tpu_custom_call" | custom-call | tf_op jit(solution)/shard_map/pallas_call | solution.py:58
  24.1 19.6 %all-to-all-done.wa = bf16[32,32,832]{2,1,0:T(8,128)(2,1)S(1)} async-done(((bf16[32,32,832]{2,1,0:T(8,128)(2,1)}), bf16[32,32,832]{2,1,0:T(8,128)(2,1)S(1)}, u32[]{:S(2)}, u32[]{:S(2)}) %all-to-all-start) | async-done | bytes 1703968 | tf_op jit(solution)/shard_map/all_to_all | solution.py:69
  44.0 4.3 %collective-permute-done.2 = bf16[32,2944]{1,0:T(8,128)(2,1)S(1)} collective-permute-done((bf16[32,2944]{1,0:T(8,128)(2,1)}, bf16[32,2944]{1,0:T(8,128)(2,1)S(1)}, u32[]{:S(2)}, u32[]{:S(2)}) %collective-permute-start.2) | collective-permute-done | bytes 188448 | tf_op jit(solution)/shard_map/ppermute | solution.py:79
  50.1 3.0 collective-permute-start
  56.7 4.4 %shard_map.214 = bf16[64,48,128]{2,1,0:T(8,128)(2,1)} custom-call(bf16[2,128,1024]{2,1,0:T(8,128)(2,1)} %get-tuple-element.92.xd.dy_a.d0.x0, f32[1,1024]{1,0:T(1,128)} %reshape.384.gain, bf16[32,32,832]{2,1,0:T(8,128)(2,1)} %copy-done.1, bf16[32,32,832]{2,1,0:T(8,128)(2,1)} %collective-permute-done.wb, s32[1,1]{1,0:T(1,128)} %bitcast.1.core, ...), custom_call_target="tpu_custom_call" | custom-call | tf_op jit(solution)/shard_map/pallas_call | solution.py:58
  61.1 25.7 %all_to_all.30.recv = bf16[64,48,128]{2,1,0:T(8,128)(2,1)S(1)} all-to-all(bf16[64,48,128]{2,1,0:T(8,128)(2,1)} %shard_map.214), channel_id=1, replica_groups=mesh['shard'=2,'context'=16,'tensor'=4] {'context','tensor'}, dimensions={0} | all-to-all | bytes 1572864 | tf_op jit(solution)/shard_map/all_to_all | solution.py:69
  90.1 10.9 %shard_map.215 = (bf16[64,16,128]{2,1,0:T(8,128)(2,1)}, f32[8,64,256]{2,1,0:T(8,128)}, f32[8,8,256]{2,1,0:T(8,128)}) custom-call(bf16[64,48,128]{2,1,0:T(8,128)(2,1)} %copy-done.2, bf16[64,32,128]{2,1,0:T(8,128)(2,1)} %copy-done.8, s32[512,1]{1,0:T(8,128)} %fusion.3.kpos, s32[1,256]{1,0:T(1,128)} %fusion.22.qpos), custom_call_target="tpu_custom_call" | custom-call | tf_op jit(solution)/shard_map/pallas_call | solution.py:58
  100.9 6.7 %all-to-all-start.2 = ((bf16[64,16,128]{2,1,0:T(8,128)(2,1)}), bf16[64,16,128]{2,1,0:T(8,128)(2,1)S(1)}, u32[]{:S(2)}, u32[]{:S(2)}) async-start(bf16[64,16,128]{2,1,0:T(8,128)(2,1)} %get-tuple-element.91), calls=%async_computation.2 | async-start | bytes 524288 | tf_op jit(solution)/shard_map/all_to_all | solution.py:69
  108.2 12.8 %all-gather.2.cloned.1.call-done = bf16[1024,2944]{1,0:T(8,128)(2,1)} async-done(((bf16[64,2944]{1,0:T(8,128)(2,1)}), bf16[1024,2944]{1,0:T(8,128)(2,1)}) %all-gather.2.cloned.1.call-update) | async-done | bytes 6029328 | tf_op jit(solution)/shard_map/all_gather | solution.py:510
  123.4 5.3 %shard_map.216 = (bf16[128,1024]{1,0:T(8,128)(2,1)}, f32[128,1024]{1,0:T(8,128)}, bf16[128,1024]{1,0:T(8,128)(2,1)}) custom-call(bf16[64,16,128]{2,1,0:T(8,128)(2,1)} %copy-done.11, bf16[2,128,1024]{2,1,0:T(8,128)(2,1)} %get-tuple-element.92.xd.dy_a.d0.x0, bf16[960,1024]{1,0:T(8,128)(2,1)} %constant.145.clone.e, f32[1,1024]{1,0:T(1,128)} %reshape.385.gain, ...), custom_call_target="tpu_custom_call" | custom-call | tf_op jit(solution)/shard_map/pallas_call | solution.py:58
  129.5 2.9 collective-permute-start.6
  134.7 7.2 %shard_map.217 = (bf16[128,1024]{1,0:T(8,128)(2,1)}, bf16[128,1024]{1,0:T(8,128)(2,1)}, bf16[2,128,640]{2,1,0:T(8,128)(2,1)}, bf16[2,128,640]{2,1,0:T(8,128)(2,1)}, bf16[2,128,640]{2,1,0:T(8,128)(2,1)}) custom-call(bf16[128,1024]{1,0:T(8,128)(2,1)} %get-tuple-element.95.h_a.h0, bf16[128,1024]{1,0:T(8,128)(2,1)} %copy-done.12, ...), custom_call_target="tpu_custom_call" | custom-call | tf_op jit(solution)/shard_map/pallas_call | solution.py:58
  141.9 3.0 collective-permute-done.7.h_b.h3
  146.4 7.2 %shard_map.218 = (bf16[128,1024]{1,0:T(8,128)(2,1)}, bf16[128,1024]{1,0:T(8,128)(2,1)}, bf16[2,128,640]{2,1,0:T(8,128)(2,1)}, bf16[2,128,640]{2,1,0:T(8,128)(2,1)}, bf16[2,128,640]{2,1,0:T(8,128)(2,1)}) custom-call(bf16[128,1024]{1,0:T(8,128)(2,1)} %copy-done.13, bf16[128,1024]{1,0:T(8,128)(2,1)} %copy-done.14, bf16[2,128,1024]{2,1,0:T(8,128)(2,1)} %copy-done.4, ...), custom_call_target="tpu_custom_call" | custom-call | tf_op jit(solution)/shard_map/pallas_call | solution.py:58
  156.7 5.5 %shard_map.220 = (bf16[2,128,1024]{2,1,0:T(8,128)(2,1)}, bf16[2,128,1024]{2,1,0:T(8,128)(2,1)}) custom-call(bf16[2,128,640]{2,1,0:T(8,128)(2,1)} %get-tuple-element.104.act_n.near, bf16[2,128,640]{2,1,0:T(8,128)(2,1)} %get-tuple-element.105.act_f.far, bf16[32,32,2944]{2,1,0:T(8,128)(2,1)} %bitcast.26), custom_call_target="tpu_custom_call" | custom-call | tf_op jit(solution)/shard_map/pallas_call | solution.py:58
  162.2 7.1 %shard_map.219 = bf16[32,96,640]{2,1,0:T(8,128)(2,1)} custom-call(bf16[128,1024]{1,0:T(8,128)(2,1)} %get-tuple-element.95.h_a.h0, bf16[128,1024]{1,0:T(8,128)(2,1)} %copy-done.12, bf16[128,1024]{1,0:T(8,128)(2,1)} %copy-done.13, bf16[128,1024]{1,0:T(8,128)(2,1)} %copy-done.14, bf16[2,128,1024]{2,1,0:T(8,128)(2,1)} %get-tuple-element.92.xd.dy_a.d0.x0, ...), custom_call_target="tpu_custom_call" | custom-call | tf_op jit(solution)/shard_map/pallas_call | solution.py:58
  170.1 7.1 %shard_map.221 = (f32[128,1024]{1,0:T(8,128)}, bf16[128,960]{1,0:T(8,128)(2,1)}, bf16[64,16,128]{2,1,0:T(8,128)(2,1)}, f32[1,1024]{1,0:T(1,128)}) custom-call(bf16[128,1024]{1,0:T(8,128)(2,1)} %get-tuple-element.96.b0, bf16[128,1024]{1,0:T(8,128)(2,1)} %copy-done.17, bf16[128,1024]{1,0:T(8,128)(2,1)} %copy-done.18, bf16[128,1024]{1,0:T(8,128)(2,1)} %copy-done.19, ...), custom_call_target="tpu_custom_call" | custom-call | tf_op jit(solution)/shard_map/pallas_call | solution.py:58
  177.6 8.4 %all-to-all-start.3 = ((bf16[64,16,128]{2,1,0:T(8,128)(2,1)}), bf16[64,16,128]{2,1,0:T(8,128)(2,1)S(1)}, u32[]{:S(2)}, u32[]{:S(2)}) async-start(bf16[64,16,128]{2,1,0:T(8,128)(2,1)} %get-tuple-element.116), calls=%async_computation.3 | async-start | bytes 524288 | tf_op jit(solution)/shard_map/all_to_all | solution.py:69
  186.0 3.0 collective-permute-start.14
  189.2 9.6 %all-to-all-done.3.drecv = bf16[64,16,128]{2,1,0:T(8,128)(2,1)S(1)} async-done(((bf16[64,16,128]{2,1,0:T(8,128)(2,1)}), bf16[64,16,128]{2,1,0:T(8,128)(2,1)S(1)}, u32[]{:S(2)}, u32[]{:S(2)}) %all-to-all-start.3) | async-done | bytes 262176 | tf_op jit(solution)/shard_map/all_to_all | solution.py:69
  199.4 16.8 %shard_map.222 = bf16[64,80,128]{2,1,0:T(8,128)(2,1)} custom-call(bf16[64,48,128]{2,1,0:T(8,128)(2,1)} %copy-done.2, bf16[64,32,128]{2,1,0:T(8,128)(2,1)} %copy-done.8, s32[512,1]{1,0:T(8,128)} %fusion.3.kpos, s32[1,256]{1,0:T(1,128)} %fusion.22.qpos, s32[1,1]{1,0:T(1,128)} %bitcast.1.core, bf16[64,16,128]{2,1,0:T(8,128)(2,1)} %copy-done.10, ...), custom_call_target="tpu_custom_call" | custom-call | tf_op jit(solution)/shard_map/pallas_call | solution.py:58
  216.2 7.7 %all-to-all-start.4 = ((bf16[64,80,128]{2,1,0:T(8,128)(2,1)}), bf16[64,80,128]{2,1,0:T(8,128)(2,1)S(1)}, u32[]{:S(2)}, u32[]{:S(2)}) async-start(bf16[64,80,128]{2,1,0:T(8,128)(2,1)} %shard_map.222), calls=%async_computation.4 | async-start | bytes 2621440 | tf_op jit(solution)/shard_map/all_to_all | solution.py:69
  225.6 2.9 shard_map.224.h1_all
  228.6 3.4 %shard_map.223 = bf16[128,960]{1,0:T(8,128)(2,1)} custom-call(bf16[2,128,1024]{2,1,0:T(8,128)(2,1)} %copy-done.7, bf16[128,1024]{1,0:T(8,128)(2,1)} %copy-done.20, f32[128,1024]{1,0:T(8,128)} %get-tuple-element.115.x1, bf16[960,1024]{1,0:T(8,128)(2,1)} %constant.145.clone.e), custom_call_target="tpu_custom_call" | custom-call | tf_op jit(solution)/shard_map/pallas_call | solution.py:58
  232.0 16.3 %all-to-all-done.4.recv = bf16[64,80,128]{2,1,0:T(8,128)(2,1)S(1)} async-done(((bf16[64,80,128]{2,1,0:T(8,128)(2,1)}), bf16[64,80,128]{2,1,0:T(8,128)(2,1)S(1)}, u32[]{:S(2)}, u32[]{:S(2)}) %all-to-all-start.4) | async-done | bytes 1310752 | tf_op jit(solution)/shard_map/all_to_all | solution.py:69
  249.4 3.1 shard_map.225
  253.2 2.9 collective-permute-start.18
  256.1 7.3 %shard_map.226 = (f32[128,960]{1,0:T(8,128)}, f32[1,1024]{1,0:T(1,128)}) custom-call(bf16[128,1600]{1,0:T(8,128)(2,1)} %get-tuple-element.131.full, bf16[32,32,832]{2,1,0:T(8,128)(2,1)} %copy-done.1, bf16[32,32,832]{2,1,0:T(8,128)(2,1)} %collective-permute-done.wb, s32[1,1]{1,0:T(1,128)} %bitcast.1.core, ...), custom_call_target="tpu_custom_call" | custom-call | tf_op jit(solution)/shard_map/pallas_call | solution.py:58
  266.0 4.7 %shard_map.227 = bf16[32,32,640]{2,1,0:T(8,128)(2,1)} custom-call(bf16[512,1024]{1,0:T(8,128)(2,1)} %shard_map.224.h1_all, bf16[2,128,1024]{2,1,0:T(8,128)(2,1)} %copy-done.9, bf16[2,128,1024]{2,1,0:T(8,128)(2,1)} %copy-done.16, bf16[128,640]{1,0:T(8,128)(2,1)} %get-tuple-element.136.g0, bf16[128,640]{1,0:T(8,128)(2,1)} %copy-done.22, ...), custom_call_target="tpu_custom_call" | custom-call | tf_op jit(solution)/shard_map/pallas_call | solution.py:58
  270.7 25.0 %all_to_all.31.pieces = bf16[32,32,640]{2,1,0:T(8,128)(2,1)} all-to-all(bf16[32,32,640]{2,1,0:T(8,128)(2,1)} %shard_map.227), channel_id=1, replica_groups=mesh['shard'=2,'context'=16,'tensor'=4] {'context','shard'}, dimensions={0} | all-to-all | bytes 2621440 | tf_op jit(solution)/shard_map/all_to_all | solution.py:69
  299.1 2.9 collective-permute-start.21
  (139 shorter events, 46.4 us)
Async XLA Ops:
  9.5 34.2 %all-to-all-start = ((bf16[32,32,832]{2,1,0:T(8,128)(2,1)}), bf16[32,32,832]{2,1,0:T(8,128)(2,1)S(1)}, u32[]{:S(2)}, u32[]{:S(2)}) async-start(bf16[32,32,832]{2,1,0:T(8,128)(2,1)} %shard_map.212), calls=%async_computation | async-start | bytes 3670016 | tf_op jit(solution)/shard_map/all_to_all | solution.py:69
  18.9 102.2 %all-gather.2.cloned.1.call-start = ((), (), s32[]{:S(2)}) async-start(), calls=%async_computation.7 | async-start | bytes 6406144 | tf_op jit(solution)/shard_map/all_gather | solution.py:510
  43.7 4.6 %collective-permute-start.2 = (bf16[32,2944]{1,0:T(8,128)(2,1)}, bf16[32,2944]{1,0:T(8,128)(2,1)S(1)}, u32[]{:S(2)}, u32[]{:S(2)}) collective-permute-start(bf16[32,2944]{1,0:T(8,128)(2,1)} %get-tuple-element.93), channel_id=1, source_target_pairs={{0,64},{64,0},{1,65},{65,1},{2,66},{66,2},{3,67},{67,3},{4,68},{68... | collective-permute-start | bytes 565256 | tf_op jit(solution)/shard_map/ppermute | solution.py:79
  50.1 6.6 %collective-permute-start = (bf16[32,32,832]{2,1,0:T(8,128)(2,1)S(1)}, bf16[32,32,832]{2,1,0:T(8,128)(2,1)}, u32[]{:S(2)}, u32[]{:S(2)}) collective-permute-start(bf16[32,32,832]{2,1,0:T(8,128)(2,1)S(1)} %all-to-all-done.wa), channel_id=1, source_target_pairs={{0,1},{1,0},{2,3},{3,2},{4,5},{5,4},{6,7},{7,6},{8,9},{9,8},{10,11... | collective-permute-start | bytes 5111816 | tf_op jit(solution)/shard_map/ppermute | solution.py:79
  86.8 2.5 collective-permute-start.1
  100.9 27.8 %collective-permute-start.3 = (bf16[2,128,1024]{2,1,0:T(8,128)(2,1)S(1)}, bf16[2,128,1024]{2,1,0:T(8,128)(2,1)S(1)}, u32[]{:S(2)}, u32[]{:S(2)}) collective-permute-start(bf16[2,128,1024]{2,1,0:T(8,128)(2,1)S(1)} %copy-done), channel_id=1, source_target_pairs={{0,2},{1,3},{2,0},{3,1},{4,6},{5,7},{6,4},{7,5},{8,10},{9,11},{10,... | collective-permute-start | bytes 1572872 | tf_op jit(solution)/shard_map/ppermute | solution.py:79
  100.9 21.7 %all-to-all-start.2 = ((bf16[64,16,128]{2,1,0:T(8,128)(2,1)}), bf16[64,16,128]{2,1,0:T(8,128)(2,1)S(1)}, u32[]{:S(2)}, u32[]{:S(2)}) async-start(bf16[64,16,128]{2,1,0:T(8,128)(2,1)} %get-tuple-element.91), calls=%async_computation.2 | async-start | bytes 524288 | tf_op jit(solution)/shard_map/all_to_all | solution.py:69
  107.7 199.3 %reduce-scatter.2.cloned.1.call-start = ((), (), s32[]{:S(2)}) async-start(), calls=%async_computation.8 | async-start | bytes 4177920 | tf_op jit(solution)/shard_map/reduce_scatter | solution.py:104
  107.7 25.5 %collective-permute-start.5 = (bf16[2,128,1024]{2,1,0:T(8,128)(2,1)S(1)}, bf16[2,128,1024]{2,1,0:T(8,128)(2,1)S(1)}, u32[]{:S(2)}, u32[]{:S(2)}) collective-permute-start(bf16[2,128,1024]{2,1,0:T(8,128)(2,1)S(1)} %copy-done), channel_id=1, source_target_pairs={{0,1},{1,0},{2,3},{3,2},{4,5},{5,4},{6,7},{7,6},{8,9},{9,8},{10,11... | collective-permute-start | bytes 1572872 | tf_op jit(solution)/shard_map/ppermute | solution.py:79
  128.7 16.1 %collective-permute-start.9 = (bf16[2,128,1024]{2,1,0:T(8,128)(2,1)S(1)}, bf16[2,128,1024]{2,1,0:T(8,128)(2,1)S(1)}, u32[]{:S(2)}, u32[]{:S(2)}) collective-permute-start(bf16[2,128,1024]{2,1,0:T(8,128)(2,1)S(1)} %collective-permute-done.3.dy_a.d2.x2), channel_id=1, source_target_pairs={{0,1},{1,0},{2,3},{3,2},{4,5},{5,4},{6,7},{7,6},{8,9},{9,8},{10,11... | collective-permute-start | bytes 1572872 | tf_op jit(solution)/shard_map/ppermute | solution.py:79
  129.4 3.8 %collective-permute-start.4 = (bf16[128,1024]{1,0:T(8,128)(2,1)}, bf16[128,1024]{1,0:T(8,128)(2,1)S(1)}, u32[]{:S(2)}, u32[]{:S(2)}) collective-permute-start(bf16[128,1024]{1,0:T(8,128)(2,1)} %get-tuple-element.95.h_a.h0), channel_id=1, source_target_pairs={{0,1},{1,0},{2,3},{3,2},{4,5},{5,4},{6,7},{7,6},{8,9},{9,8},{10,11... | collective-permute-start | bytes 786440 | tf_op jit(solution)/shard_map/ppermute | solution.py:79
  129.5 12.4 %collective-permute-start.6 = (bf16[128,1024]{1,0:T(8,128)(2,1)}, bf16[128,1024]{1,0:T(8,128)(2,1)S(1)}, u32[]{:S(2)}, u32[]{:S(2)}) collective-permute-start(bf16[128,1024]{1,0:T(8,128)(2,1)} %get-tuple-element.95.h_a.h0), channel_id=1, source_target_pairs={{0,2},{1,3},{2,0},{3,1},{4,6},{5,7},{6,4},{7,5},{8,10},{9,11},{10,... | collective-permute-start | bytes 786440 | tf_op jit(solution)/shard_map/ppermute | solution.py:79
  132.3 12.5 %collective-permute-start.7 = (bf16[128,1024]{1,0:T(8,128)(2,1)}, bf16[128,1024]{1,0:T(8,128)(2,1)S(1)}, u32[]{:S(2)}, u32[]{:S(2)}) collective-permute-start(bf16[128,1024]{1,0:T(8,128)(2,1)} %get-tuple-element.95.h_a.h0), channel_id=1, source_target_pairs={{0,3},{1,2},{2,1},{3,0},{4,7},{5,6},{6,5},{7,4},{8,11},{9,10},{10,... | collective-permute-start | bytes 786440 | tf_op jit(solution)/shard_map/ppermute | solution.py:79
  144.8 24.4 %collective-permute-start.8 = (bf16[128,1024]{1,0:T(8,128)(2,1)}, bf16[128,1024]{1,0:T(8,128)(2,1)S(1)}, u32[]{:S(2)}, u32[]{:S(2)}) collective-permute-start(bf16[128,1024]{1,0:T(8,128)(2,1)} %get-tuple-element.98), channel_id=1, source_target_pairs={{0,1},{1,0},{2,3},{3,2},{4,5},{5,4},{6,7},{7,6},{8,9},{9,8},{10,11... | collective-permute-start | bytes 786440 | tf_op jit(solution)/shard_map/ppermute | solution.py:79
  153.6 15.7 %collective-permute-start.10 = (bf16[128,1024]{1,0:T(8,128)(2,1)}, bf16[128,1024]{1,0:T(8,128)(2,1)S(1)}, u32[]{:S(2)}, u32[]{:S(2)}) collective-permute-start(bf16[128,1024]{1,0:T(8,128)(2,1)} %get-tuple-element.102), channel_id=1, source_target_pairs={{0,2},{1,3},{2,0},{3,1},{4,6},{5,7},{6,4},{7,5},{8,10},{9,11},{10,... | collective-permute-start | bytes 786440 | tf_op jit(solution)/shard_map/ppermute | solution.py:79
  156.4 12.9 %collective-permute-start.11 = (bf16[128,1024]{1,0:T(8,128)(2,1)}, bf16[128,1024]{1,0:T(8,128)(2,1)S(1)}, u32[]{:S(2)}, u32[]{:S(2)}) collective-permute-start(bf16[128,1024]{1,0:T(8,128)(2,1)} %get-tuple-element.103), channel_id=1, source_target_pairs={{0,3},{1,2},{2,1},{3,0},{4,7},{5,6},{6,5},{7,4},{8,11},{9,10},{10,... | collective-permute-start | bytes 786440 | tf_op jit(solution)/shard_map/ppermute | solution.py:79
  170.1 18.8 %copy-start.15 = (bf16[2,128,1024]{2,1,0:T(8,128)(2,1)S(1)}, bf16[2,128,1024]{2,1,0:T(8,128)(2,1)}, u32[]{:S(2)}) copy-start(bf16[2,128,1024]{2,1,0:T(8,128)(2,1)} %get-tuple-element.117) | copy-start | bytes 1572868
  177.3 11.7 %collective-permute-start.12 = (bf16[2,128,1024]{2,1,0:T(8,128)(2,1)S(1)}, bf16[2,128,1024]{2,1,0:T(8,128)(2,1)S(1)}, u32[]{:S(2)}, u32[]{:S(2)}) collective-permute-start(bf16[2,128,1024]{2,1,0:T(8,128)(2,1)S(1)} %copy-done.30), channel_id=1, source_target_pairs={{0,1},{1,0},{2,3},{3,2},{4,5},{5,4},{6,7},{7,6},{8,9},{9,8},{10,11... | collective-permute-start | bytes 1572872 | tf_op jit(solution)/shard_map/ppermute | solution.py:79
  177.6 21.2 %all-to-all-start.3 = ((bf16[64,16,128]{2,1,0:T(8,128)(2,1)}), bf16[64,16,128]{2,1,0:T(8,128)(2,1)S(1)}, u32[]{:S(2)}, u32[]{:S(2)}) async-start(bf16[64,16,128]{2,1,0:T(8,128)(2,1)} %get-tuple-element.116), calls=%async_computation.3 | async-start | bytes 524288 | tf_op jit(solution)/shard_map/all_to_all | solution.py:69
  186.0 13.1 %collective-permute-start.14 = (bf16[128,1024]{1,0:T(8,128)(2,1)S(1)}, bf16[128,1024]{1,0:T(8,128)(2,1)S(1)}, u32[]{:S(2)}, u32[]{:S(2)}) collective-permute-start(bf16[128,1024]{1,0:T(8,128)(2,1)S(1)} %copy-done.21), channel_id=1, source_target_pairs={{0,2},{1,3},{2,0},{3,1},{4,6},{5,7},{6,4},{7,5},{8,10},{9,11},{10,... | collective-permute-start | bytes 786440 | tf_op jit(solution)/shard_map/ppermute | solution.py:79
  189.1 27.1 %copy-start.7 = (bf16[2,128,1024]{2,1,0:T(8,128)(2,1)}, bf16[2,128,1024]{2,1,0:T(8,128)(2,1)S(1)}, u32[]{:S(2)}) copy-start(bf16[2,128,1024]{2,1,0:T(8,128)(2,1)S(1)} %add_convert_fusion.own) | copy-start | bytes 1572868
  198.7 17.5 %collective-permute-start.13 = (bf16[128,1024]{1,0:T(8,128)(2,1)S(1)}, bf16[128,1024]{1,0:T(8,128)(2,1)S(1)}, u32[]{:S(2)}, u32[]{:S(2)}) collective-permute-start(bf16[128,1024]{1,0:T(8,128)(2,1)S(1)} %slice_bitcast_fusion), channel_id=1, source_target_pairs={{0,2},{1,3},{2,0},{3,1},{4,6},{5,7},{6,4},{7,5},{8,10},{9,11},{10,... | collective-permute-start | bytes 786440 | tf_op jit(solution)/shard_map/ppermute | solution.py:79
  199.1 24.8 %copy-start.9 = (bf16[2,128,1024]{2,1,0:T(8,128)(2,1)}, bf16[2,128,1024]{2,1,0:T(8,128)(2,1)S(1)}, u32[]{:S(2)}) copy-start(bf16[2,128,1024]{2,1,0:T(8,128)(2,1)S(1)} %pad_maximum_fusion.o_near) | copy-start | bytes 1572868
  216.2 32.1 %all-to-all-start.4 = ((bf16[64,80,128]{2,1,0:T(8,128)(2,1)}), bf16[64,80,128]{2,1,0:T(8,128)(2,1)S(1)}, u32[]{:S(2)}, u32[]{:S(2)}) async-start(bf16[64,80,128]{2,1,0:T(8,128)(2,1)} %shard_map.222), calls=%async_computation.4 | async-start | bytes 2621440 | tf_op jit(solution)/shard_map/all_to_all | solution.py:69
  223.9 41.0 %collective-permute-start.15 = (bf16[2,128,1024]{2,1,0:T(8,128)(2,1)S(1)}, bf16[2,128,1024]{2,1,0:T(8,128)(2,1)S(1)}, u32[]{:S(2)}, u32[]{:S(2)}) collective-permute-start(bf16[2,128,1024]{2,1,0:T(8,128)(2,1)S(1)} %pad_maximum_fusion.o_near), channel_id=1, source_target_pairs={{0,1},{1,0},{2,3},{3,2},{4,5},{5,4},{6,7},{7,6},{8,9},{9,8},{10,11... | collective-permute-start | bytes 1572872 | tf_op jit(solution)/shard_map/ppermute | solution.py:79
  252.5 12.5 %collective-permute-start.16 = (bf16[128,640]{1,0:T(8,128)(2,1)}, bf16[128,640]{1,0:T(8,128)(2,1)S(1)}, u32[]{:S(2)}, u32[]{:S(2)}) collective-permute-start(bf16[128,640]{1,0:T(8,128)(2,1)} %get-tuple-element.137), channel_id=1, source_target_pairs={{0,1},{1,0},{2,3},{3,2},{4,5},{5,4},{6,7},{7,6},{8,9},{9,8},{10,11... | collective-permute-start | bytes 491528 | tf_op jit(solution)/shard_map/ppermute | solution.py:79
  252.5 12.6 %collective-permute-start.17 = (bf16[128,640]{1,0:T(8,128)(2,1)}, bf16[128,640]{1,0:T(8,128)(2,1)S(1)}, u32[]{:S(2)}, u32[]{:S(2)}) collective-permute-start(bf16[128,640]{1,0:T(8,128)(2,1)} %get-tuple-element.138), channel_id=1, source_target_pairs={{0,2},{1,3},{2,0},{3,1},{4,6},{5,7},{6,4},{7,5},{8,10},{9,11},{10,... | collective-permute-start | bytes 491528 | tf_op jit(solution)/shard_map/ppermute | solution.py:79
  253.2 11.8 %collective-permute-start.18 = (bf16[128,640]{1,0:T(8,128)(2,1)}, bf16[128,640]{1,0:T(8,128)(2,1)S(1)}, u32[]{:S(2)}, u32[]{:S(2)}) collective-permute-start(bf16[128,640]{1,0:T(8,128)(2,1)} %get-tuple-element.139), channel_id=1, source_target_pairs={{0,3},{1,2},{2,1},{3,0},{4,7},{5,6},{6,5},{7,4},{8,11},{9,10},{10,... | collective-permute-start | bytes 491528 | tf_op jit(solution)/shard_map/ppermute | solution.py:79
  297.8 4.2 %collective-permute-start.19 = (bf16[32,640]{1,0:T(8,128)(2,1)}, bf16[32,640]{1,0:T(8,128)(2,1)S(1)}, u32[]{:S(2)}, u32[]{:S(2)}) collective-permute-start(bf16[32,640]{1,0:T(8,128)(2,1)} %shard_map.228.p0), channel_id=1, source_target_pairs={{0,1},{1,0},{2,3},{3,2},{4,5},{5,4},{6,7},{7,6},{8,9},{9,8},{10,11... | collective-permute-start | bytes 122888 | tf_op jit(solution)/shard_map/ppermute | solution.py:79
  298.8 4.6 %collective-permute-start.20 = (bf16[32,640]{1,0:T(8,128)(2,1)}, bf16[32,640]{1,0:T(8,128)(2,1)S(1)}, u32[]{:S(2)}, u32[]{:S(2)}) collective-permute-start(bf16[32,640]{1,0:T(8,128)(2,1)} %shard_map.228.p0), channel_id=1, source_target_pairs={{0,2},{1,3},{2,0},{3,1},{4,6},{5,7},{6,4},{7,5},{8,10},{9,11},{10,... | collective-permute-start | bytes 122888 | tf_op jit(solution)/shard_map/ppermute | solution.py:79
  299.1 5.7 %collective-permute-start.21 = (bf16[32,640]{1,0:T(8,128)(2,1)}, bf16[32,640]{1,0:T(8,128)(2,1)S(1)}, u32[]{:S(2)}, u32[]{:S(2)}) collective-permute-start(bf16[32,640]{1,0:T(8,128)(2,1)} %shard_map.228.p0), channel_id=1, source_target_pairs={{0,3},{1,2},{2,1},{3,0},{4,7},{5,6},{6,5},{7,4},{8,11},{9,10},{10,... | collective-permute-start | bytes 122888 | tf_op jit(solution)/shard_map/ppermute | solution.py:79
  308.0 4.1 %collective-permute-start.22 = (bf16[96,640]{1,0:T(8,128)(2,1)S(1)}, bf16[96,640]{1,0:T(8,128)(2,1)S(1)}, u32[]{:S(2)}, u32[]{:S(2)}) collective-permute-start(bf16[96,640]{1,0:T(8,128)(2,1)S(1)} %broadcast_select_fusion.2), channel_id=1, source_target_pairs={{0,64},{64,0},{1,65},{65,1},{2,66},{66,2},{3,67},{67,3},{4,68},{68... | collective-permute-start | bytes 368648 | tf_op jit(solution)/shard_map/ppermute | solution.py:79
  (28 other events, 111.8 us)
Sparse Core Ops, SparseCore 0:
  50.2 70.7 all-gather.1
  169.4 80.8 reduce-scatter.1

commit v5 on v4

--- a/solution.py
+++ b/solution.py
@@ -88,12 +88,6 @@
     return near, swap(near, "tensor", 1)
 
 
-def paired(v):
-    mine = lax.axis_index("shard") == 0
-    other = swap(v, "shard", 1)
-    return jnp.concatenate([jnp.where(mine, v, other), jnp.where(mine, other, v)], axis=0)
-
-
 def from_each(pieces):
     return [pieces[0]] + [swap(pieces[k], "tensor", k) for k in range(1, 4)]
 
@@ -165,17 +159,27 @@
         out[b] = block
 
 
-def prep_kernel(wg, wu, wd, wo, gain, x, dy, e, out, xd):
+def prep_kernel(own, other, shard, x, dy, e, out, xd):
     i = lax.broadcasted_iota(jnp.int32, (PADB, BLK), 0)
     j = lax.broadcasted_iota(jnp.int32, (PADB, BLK), 1)
     eye = (i == j).astype(F32).astype(BF16)
-    out[:, 0:FFS] = dot(eye, wg[...]).astype(BF16)
-    out[:, FFS : 2 * FFS] = dot(eye, wu[...]).astype(BF16)
-    out[:, 2 * FFS : 3 * FFS] = dot(eye, wd[...]).astype(BF16)
     row = lax.broadcasted_iota(jnp.int32, (PADB, WP), 0)
-    tail = jnp.concatenate([gain[...].astype(F32), jnp.zeros((1, WP - BLK), F32)], axis=1)
-    own = dot(eye, dot(wo[...], e[...]).astype(BF16))
-    out[:, 3 * FFS :] = jnp.where(row == BLK, tail, own).astype(BF16)
+    mine = shard[...] == 0
+    rows = 3 * FFS
+
+    def block(v):
+        tail = jnp.concatenate(
+            [v[BLK : BLK + 1, :BLK].astype(F32), jnp.zeros((1, WP - BLK), F32)], axis=1
+        )
+        wide = dot(v[:BLK, rows:], e[...]).astype(BF16)
+        return dot(eye, v[:BLK, :rows]), jnp.where(row == BLK, tail, dot(eye, wide))
+
+    mlp_own, out_own = block(own)
+    mlp_other, out_other = block(other)
+    out[0:PADB, :rows] = jnp.where(mine, mlp_own, mlp_other).astype(BF16)
+    out[PADB:, :rows] = jnp.where(mine, mlp_other, mlp_own).astype(BF16)
+    out[0:PADB, rows:] = jnp.where(mine, out_own, out_other).astype(BF16)
+    out[PADB:, rows:] = jnp.where(mine, out_other, out_own).astype(BF16)
     xd[0] = dot(x[...], e[...]).astype(BF16)
     xd[1] = dot(dy[...], e[...]).astype(BF16)
 
@@ -488,16 +492,19 @@
         first_kernel, [((NB, PADB, HALF), BF16)],
         w_query, key_weight, value_weight, attn_gain.reshape(1, BLK), core,
     )
+    rows = jnp.concatenate([w_gate, w_up, w_down.T, w_out], axis=1)
+    gain_row = jnp.pad(mlp_gain[None, :], ((0, 0), (0, rows.shape[1] - BLK)))
+    rows = jnp.concatenate([rows, gain_row], axis=0)
+    other = swap(rows, "shard", 1)
+    rows, other, w1_send = lax.optimization_barrier((rows, other, w1_send))
     w1a = exchange(w1_send, CS)
-    w_gate, w_up, w_down, w_out, mlp_gain, w1_send = lax.optimization_barrier(
-        (w_gate, w_up, w_down, w_out, mlp_gain, w1_send)
-    )
-    own, xd = call(
+    shard = lax.axis_index("shard").reshape(1, 1).astype(jnp.int32)
+    pair, xd = call(
         prep_kernel,
-        [((PADB, 3 * FFS + WP), BF16), ((2, T, WP), BF16)],
-        w_gate, w_up, w_down.T, w_out, mlp_gain.reshape(1, BLK),
-        tokens.reshape(T, WIDTH), out_grad.reshape(T, WIDTH), spread,
-    )
+        [((2 * PADB, 3 * FFS + WP), BF16), ((2, T, WP), BF16)],
+        rows, other, shard, tokens.reshape(T, WIDTH), out_grad.reshape(T, WIDTH), spread,
+    )
+
     half = D // 2
     freq = ROPE_BASE ** (-2.0 * jnp.arange(half, dtype=F32) / D)
     theta = positions.reshape(T).astype(F32)[:, None] * freq
@@ -505,9 +512,9 @@
     cos = jnp.concatenate([c, c, c, c], axis=1)
     sin = jnp.concatenate([-s, s, -s, s], axis=1)
 
-    w1a, own, xd, cos, sin = lax.optimization_barrier((w1a, own, xd, cos, sin))
+    w1a, pair, xd, cos, sin = lax.optimization_barrier((w1a, pair, xd, cos, sin))
     w1b = swap(w1a, "tensor", 1)
-    w2 = lax.all_gather(paired(own), "context", axis=0, tiled=True).reshape(NB, *own.shape)
+    w2 = lax.all_gather(pair, "context", axis=0, tiled=True).reshape(NB, PADB, -1)
     gain2 = w2[:, 30, 3 * FFS : 3 * FFS + PADB].reshape(1, WP).astype(F32)
     gain1 = w1a[:, 30, :PADB].reshape(1, WP).astype(F32)
 
@@ -626,6 +633,7 @@
     proj_recv = exchange(proj_grad, CS)
     mlp_part, proj_grad = lax.optimization_barrier((mlp_part, proj_grad))
     mlp_sum = over_shard(mlp_part)
+    proj_recv, mlp_sum = lax.optimization_barrier((proj_recv, mlp_sum))
     (proj_sum,) = call(total_kernel, [((32, QUART), BF16)], proj_recv)
     wq_grad, wk_grad, wv_grad, wo_grad, gain_sums = call(
         last_kernel,

time: 327 us -> 318 us (0.972)
  blocking collectives: 50.7 us -> 25.4 us
  waiting for transfers between devices: 73.6 us -> 84.3 us
  starting transfers between devices: 57 us -> 61.5 us
    all_to_all x2 -> x1, blocking collectives: 50.7 us -> 25.4 us  [exchange(): return lax.all_to_all(v, axes, 0, 0, tiled=True)]
    ppermute x23, waiting for transfers between devices: 15.3 us -> 24.7 us  [swap(): return lax.ppermute(v, axis, pairs)]
    all_to_all x4 -> x5, starting transfers between devices: 32.1 us -> 34.5 us  [exchange(): return lax.all_to_all(v, axes, 0, 0, tiled=True)]
    unnamed x62 -> x68, local copies, waits for them, and re-layouts: 8.31 us -> 10.1 us
    all_to_all x4 -> x5, waiting for transfers between devices: 45.5 us -> 46.7 us  [exchange(): return lax.all_to_all(v, axes, 0, 0, tiled=True)]
  transfers between devices with their start and end apart: 29 -> 30, of which waited for: 11 -> 12; matrix products, arithmetic and copies ran while one was open for 3% -> 3% of each run, Pallas kernels for 31% -> 32%
where the time goes in v5:
time: 318 us; the launch traced here: 312 us
  Pallas kernels  104 us (33%)
  waiting for transfers between devices  84.3 us (27%)
  starting transfers between devices  61.5 us (19%)
  blocking collectives  25.4 us (8%)
  between operations  14.9 us (5%)
  local copies, waits for them, and re-layouts  14.5 us (5%)
  other arithmetic  8.51 us (3%)
    pallas_call x18, Pallas kernels, call(): pl.pallas_call(fn, in_specs=[(specs or {}).get(k, whole) for k in range(l...  104 us
    all_to_all x5, waiting for transfers between devices, exchange(): return lax.all_to_all(v, axes, 0, 0, tiled=True)  46.7 us
    all_to_all x5, starting transfers between devices, exchange(): return lax.all_to_all(v, axes, 0, 0, tiled=True)  34.5 us
    ppermute x23, starting transfers between devices, swap(): return lax.ppermute(v, axis, pairs)  26.9 us
    all_to_all x1, blocking collectives, exchange(): return lax.all_to_all(v, axes, 0, 0, tiled=True)  25.4 us
    ppermute x23, waiting for transfers between devices, swap(): return lax.ppermute(v, axis, pairs)  24.7 us
    all_gather x1, waiting for transfers between devices, shards(): lax.all_gather(pair, 'context', axis=0, tiled=True).reshape(NB, PADB, -1)  12.8 us
    unnamed x68, local copies, waits for them, and re-layouts  10.1 us
  transfers between devices with their start and end apart: 30, of which 12 were waited for; matrix products, arithmetic and copies ran while one was open for 3% of the time, Pallas kernels for 32%

profile of v5, /device:TPU:1, one launch (start us, length us, event | category | flops | bytes accessed | tf_op | source)
XLA Modules:
  0.0 312.5 jit_solution(15049820291279354224)
XLA Ops:
  15.7 7.9 %all-to-all-start = ((bf16[32,32,832]{2,1,0:T(8,128)(2,1)}), bf16[32,32,832]{2,1,0:T(8,128)(2,1)S(1)}, u32[]{:S(2)}, u32[]{:S(2)}) async-start(bf16[32,32,832]{2,1,0:T(8,128)(2,1)} %shard_map.212), calls=%async_computation | async-start | bytes 3670016 | tf_op jit(solution)/shard_map/all_to_all | solution.py:69
  25.0 4.4 %shard_map.213 = (bf16[64,2944]{1,0:T(8,128)(2,1)}, bf16[2,128,1024]{2,1,0:T(8,128)(2,1)}) custom-call(bf16[31,2880]{1,0:T(8,128)(2,1)} %copy-done.16, bf16[31,2880]{1,0:T(8,128)(2,1)} %copy-done.24, s32[1,1]{1,0:T(1,128)} %bitcast.4.shard, bf16[128,960]{1,0:T(8,128)(2,1)} %bitcast.30, bf16[128,960]{1,0:T(8,128)(2,1)} %bitcast.31, ...), custom_call_target="tpu_custom_call" | custom-call | tf_op jit(solution)/shard_map/pallas_call | solution.py:58
  29.4 18.1 %all-to-all-done.wa = bf16[32,32,832]{2,1,0:T(8,128)(2,1)S(1)} async-done(((bf16[32,32,832]{2,1,0:T(8,128)(2,1)}), bf16[32,32,832]{2,1,0:T(8,128)(2,1)S(1)}, u32[]{:S(2)}, u32[]{:S(2)}) %all-to-all-start) | async-done | bytes 1703968 | tf_op jit(solution)/shard_map/all_to_all | solution.py:69
  47.5 2.9 collective-permute-start.1
  53.9 4.4 %shard_map.214 = bf16[64,48,128]{2,1,0:T(8,128)(2,1)} custom-call(bf16[2,128,1024]{2,1,0:T(8,128)(2,1)} %get-tuple-element.90.xd.dy_a.d0.x0, f32[1,1024]{1,0:T(1,128)} %reshape.384.gain, bf16[32,32,832]{2,1,0:T(8,128)(2,1)} %copy-done.1, bf16[32,32,832]{2,1,0:T(8,128)(2,1)} %collective-permute-done.1.wb, s32[1,1]{1,0:T(1,128)} %bitcast.3.core, ...), custom_call_target="tpu_custom_call" | custom-call | tf_op jit(solution)/shard_map/pallas_call | solution.py:58
  58.3 25.4 %all_to_all.30.recv = bf16[64,48,128]{2,1,0:T(8,128)(2,1)S(1)} all-to-all(bf16[64,48,128]{2,1,0:T(8,128)(2,1)} %shard_map.214), channel_id=1, replica_groups=mesh['shard'=2,'context'=16,'tensor'=4] {'context','tensor'}, dimensions={0} | all-to-all | bytes 1572864 | tf_op jit(solution)/shard_map/all_to_all | solution.py:69
  87.0 10.9 %shard_map.215 = (bf16[64,16,128]{2,1,0:T(8,128)(2,1)}, f32[8,64,256]{2,1,0:T(8,128)}, f32[8,8,256]{2,1,0:T(8,128)}) custom-call(bf16[64,48,128]{2,1,0:T(8,128)(2,1)} %copy-done.2, bf16[64,32,128]{2,1,0:T(8,128)(2,1)} %copy-done.9, s32[512,1]{1,0:T(8,128)} %fusion.4.kpos, s32[1,256]{1,0:T(1,128)} %fusion.24.qpos), custom_call_target="tpu_custom_call" | custom-call | tf_op jit(solution)/shard_map/pallas_call | solution.py:58
  97.9 6.7 %all-to-all-start.2 = ((bf16[64,16,128]{2,1,0:T(8,128)(2,1)}), bf16[64,16,128]{2,1,0:T(8,128)(2,1)S(1)}, u32[]{:S(2)}, u32[]{:S(2)}) async-start(bf16[64,16,128]{2,1,0:T(8,128)(2,1)} %get-tuple-element.89), calls=%async_computation.2 | async-start | bytes 524288 | tf_op jit(solution)/shard_map/all_to_all | solution.py:69
  105.2 12.8 %all-gather.2.cloned.1.call-done = bf16[1024,2944]{1,0:T(8,128)(2,1)} async-done(((bf16[64,2944]{1,0:T(8,128)(2,1)}), bf16[1024,2944]{1,0:T(8,128)(2,1)}) %all-gather.2.cloned.1.call-update) | async-done | bytes 6029328 | tf_op jit(solution)/shard_map/all_gather | solution.py:517
  120.3 5.3 %shard_map.216 = (bf16[128,1024]{1,0:T(8,128)(2,1)}, f32[128,1024]{1,0:T(8,128)}, bf16[128,1024]{1,0:T(8,128)(2,1)}) custom-call(bf16[64,16,128]{2,1,0:T(8,128)(2,1)} %copy-done.12, bf16[2,128,1024]{2,1,0:T(8,128)(2,1)} %get-tuple-element.90.xd.dy_a.d0.x0, bf16[960,1024]{1,0:T(8,128)(2,1)} %constant.145.clone.e, f32[1,1024]{1,0:T(1,128)} %reshape.385.gain, ...), custom_call_target="tpu_custom_call" | custom-call | tf_op jit(solution)/shard_map/pallas_call | solution.py:58
  126.3 2.9 collective-permute-start.6
  131.6 7.2 %shard_map.217 = (bf16[128,1024]{1,0:T(8,128)(2,1)}, bf16[128,1024]{1,0:T(8,128)(2,1)}, bf16[2,128,640]{2,1,0:T(8,128)(2,1)}, bf16[2,128,640]{2,1,0:T(8,128)(2,1)}, bf16[2,128,640]{2,1,0:T(8,128)(2,1)}) custom-call(bf16[128,1024]{1,0:T(8,128)(2,1)} %get-tuple-element.93.h_a.h0, bf16[128,1024]{1,0:T(8,128)(2,1)} %copy-done.13, ...), custom_call_target="tpu_custom_call" | custom-call | tf_op jit(solution)/shard_map/pallas_call | solution.py:58
  138.8 2.9 collective-permute-done.7.h_b.h3
  143.2 7.2 %shard_map.218 = (bf16[128,1024]{1,0:T(8,128)(2,1)}, bf16[128,1024]{1,0:T(8,128)(2,1)}, bf16[2,128,640]{2,1,0:T(8,128)(2,1)}, bf16[2,128,640]{2,1,0:T(8,128)(2,1)}, bf16[2,128,640]{2,1,0:T(8,128)(2,1)}) custom-call(bf16[128,1024]{1,0:T(8,128)(2,1)} %copy-done.14, bf16[128,1024]{1,0:T(8,128)(2,1)} %copy-done.15, bf16[2,128,1024]{2,1,0:T(8,128)(2,1)} %copy-done.5, ...), custom_call_target="tpu_custom_call" | custom-call | tf_op jit(solution)/shard_map/pallas_call | solution.py:58
  150.4 2.9 collective-permute-start.10
  153.5 5.5 %shard_map.220 = (bf16[2,128,1024]{2,1,0:T(8,128)(2,1)}, bf16[2,128,1024]{2,1,0:T(8,128)(2,1)}) custom-call(bf16[2,128,640]{2,1,0:T(8,128)(2,1)} %get-tuple-element.102.act_n.near, bf16[2,128,640]{2,1,0:T(8,128)(2,1)} %get-tuple-element.103.act_f.far, bf16[32,32,2944]{2,1,0:T(8,128)(2,1)} %bitcast.27), custom_call_target="tpu_custom_call" | custom-call | tf_op jit(solution)/shard_map/pallas_call | solution.py:58
  159.0 7.1 %shard_map.219 = bf16[32,96,640]{2,1,0:T(8,128)(2,1)} custom-call(bf16[128,1024]{1,0:T(8,128)(2,1)} %get-tuple-element.93.h_a.h0, bf16[128,1024]{1,0:T(8,128)(2,1)} %copy-done.13, bf16[128,1024]{1,0:T(8,128)(2,1)} %copy-done.14, bf16[128,1024]{1,0:T(8,128)(2,1)} %copy-done.15, bf16[2,128,1024]{2,1,0:T(8,128)(2,1)} %get-tuple-element.90.xd.dy_a.d0.x0, ...), custom_call_target="tpu_custom_call" | custom-call | tf_op jit(solution)/shard_map/pallas_call | solution.py:58
  167.0 7.1 %shard_map.221 = (f32[128,1024]{1,0:T(8,128)}, bf16[128,960]{1,0:T(8,128)(2,1)}, bf16[64,16,128]{2,1,0:T(8,128)(2,1)}, f32[1,1024]{1,0:T(1,128)}) custom-call(bf16[128,1024]{1,0:T(8,128)(2,1)} %get-tuple-element.94.b0, bf16[128,1024]{1,0:T(8,128)(2,1)} %copy-done.19, bf16[128,1024]{1,0:T(8,128)(2,1)} %copy-done.20, bf16[128,1024]{1,0:T(8,128)(2,1)} %copy-done.21, ...), custom_call_target="tpu_custom_call" | custom-call | tf_op jit(solution)/shard_map/pallas_call | solution.py:58
  174.4 8.5 %all-to-all-start.3 = ((bf16[64,16,128]{2,1,0:T(8,128)(2,1)}), bf16[64,16,128]{2,1,0:T(8,128)(2,1)S(1)}, u32[]{:S(2)}, u32[]{:S(2)}) async-start(bf16[64,16,128]{2,1,0:T(8,128)(2,1)} %get-tuple-element.114), calls=%async_computation.3 | async-start | bytes 524288 | tf_op jit(solution)/shard_map/all_to_all | solution.py:69
  182.9 3.0 collective-permute-start.14
  186.1 9.8 %all-to-all-done.3.drecv = bf16[64,16,128]{2,1,0:T(8,128)(2,1)S(1)} async-done(((bf16[64,16,128]{2,1,0:T(8,128)(2,1)}), bf16[64,16,128]{2,1,0:T(8,128)(2,1)S(1)}, u32[]{:S(2)}, u32[]{:S(2)}) %all-to-all-start.3) | async-done | bytes 262176 | tf_op jit(solution)/shard_map/all_to_all | solution.py:69
  196.6 16.9 %shard_map.222 = bf16[64,80,128]{2,1,0:T(8,128)(2,1)} custom-call(bf16[64,48,128]{2,1,0:T(8,128)(2,1)} %copy-done.2, bf16[64,32,128]{2,1,0:T(8,128)(2,1)} %copy-done.9, s32[512,1]{1,0:T(8,128)} %fusion.4.kpos, s32[1,256]{1,0:T(1,128)} %fusion.24.qpos, s32[1,1]{1,0:T(1,128)} %bitcast.3.core, bf16[64,16,128]{2,1,0:T(8,128)(2,1)} %copy-done.11, ...), custom_call_target="tpu_custom_call" | custom-call | tf_op jit(solution)/shard_map/pallas_call | solution.py:58
  213.4 7.4 %all-to-all-start.4 = ((bf16[64,80,128]{2,1,0:T(8,128)(2,1)}), bf16[64,80,128]{2,1,0:T(8,128)(2,1)S(1)}, u32[]{:S(2)}, u32[]{:S(2)}) async-start(bf16[64,80,128]{2,1,0:T(8,128)(2,1)} %shard_map.222), calls=%async_computation.4 | async-start | bytes 2621440 | tf_op jit(solution)/shard_map/all_to_all | solution.py:69
  222.5 2.9 shard_map.224.h1_all
  225.5 3.4 %shard_map.223 = bf16[128,960]{1,0:T(8,128)(2,1)} custom-call(bf16[2,128,1024]{2,1,0:T(8,128)(2,1)} %copy-done.8, bf16[128,1024]{1,0:T(8,128)(2,1)} %copy-done.22, f32[128,1024]{1,0:T(8,128)} %get-tuple-element.113.x1, bf16[960,1024]{1,0:T(8,128)(2,1)} %constant.145.clone.e), custom_call_target="tpu_custom_call" | custom-call | tf_op jit(solution)/shard_map/pallas_call | solution.py:58
  229.0 16.3 %all-to-all-done.4.recv = bf16[64,80,128]{2,1,0:T(8,128)(2,1)S(1)} async-done(((bf16[64,80,128]{2,1,0:T(8,128)(2,1)}), bf16[64,80,128]{2,1,0:T(8,128)(2,1)S(1)}, u32[]{:S(2)}, u32[]{:S(2)}) %all-to-all-start.4) | async-done | bytes 1310752 | tf_op jit(solution)/shard_map/all_to_all | solution.py:69
  246.3 3.1 shard_map.225
  250.1 3.0 collective-permute-start.18
  253.1 7.3 %shard_map.226 = (f32[128,960]{1,0:T(8,128)}, f32[1,1024]{1,0:T(1,128)}) custom-call(bf16[128,1600]{1,0:T(8,128)(2,1)} %get-tuple-element.129.full, bf16[32,32,832]{2,1,0:T(8,128)(2,1)} %copy-done.1, bf16[32,32,832]{2,1,0:T(8,128)(2,1)} %collective-permute-done.1.wb, s32[1,1]{1,0:T(1,128)} %bitcast.3.core, ...), custom_call_target="tpu_custom_call" | custom-call | tf_op jit(solution)/shard_map/pallas_call | solution.py:58
  262.9 4.8 %shard_map.227 = bf16[32,32,640]{2,1,0:T(8,128)(2,1)} custom-call(bf16[512,1024]{1,0:T(8,128)(2,1)} %shard_map.224.h1_all, bf16[2,128,1024]{2,1,0:T(8,128)(2,1)} %copy-done.10, bf16[2,128,1024]{2,1,0:T(8,128)(2,1)} %copy-done.18, bf16[128,640]{1,0:T(8,128)(2,1)} %get-tuple-element.134.g0, bf16[128,640]{1,0:T(8,128)(2,1)} %copy-done.25, ...), custom_call_target="tpu_custom_call" | custom-call | tf_op jit(solution)/shard_map/pallas_call | solution.py:58
  267.7 3.9 %all-to-all-start.5 = ((bf16[32,32,640]{2,1,0:T(8,128)(2,1)}), bf16[32,32,640]{2,1,0:T(8,128)(2,1)S(1)}, u32[]{:S(2)}, u32[]{:S(2)}) async-start(bf16[32,32,640]{2,1,0:T(8,128)(2,1)} %shard_map.227), calls=%async_computation.5 | async-start | bytes 2621440 | tf_op jit(solution)/shard_map/all_to_all | solution.py:69
  273.9 14.3 %collective-permute-done.19 = bf16[96,640]{1,0:T(8,128)(2,1)S(1)} collective-permute-done((bf16[96,640]{1,0:T(8,128)(2,1)S(1)}, bf16[96,640]{1,0:T(8,128)(2,1)S(1)}, u32[]{:S(2)}, u32[]{:S(2)}) %collective-permute-start.19) | collective-permute-done | bytes 122912 | tf_op jit(solution)/shard_map/ppermute | solution.py:79
  (145 shorter events, 51.5 us)
Async XLA Ops:
  8.1 7.0 %collective-permute-start = (bf16[31,2880]{1,0:T(8,128)(2,1)S(1)}, bf16[31,2880]{1,0:T(8,128)(2,1)S(1)}, u32[]{:S(2)}, u32[]{:S(2)}) collective-permute-start(bf16[31,2880]{1,0:T(8,128)(2,1)S(1)} %fusion.17.own), channel_id=1, source_target_pairs={{0,64},{64,0},{1,65},{65,1},{2,66},{66,2},{3,67},{67,3},{4,68},{68... | collective-permute-start | bytes 535688 | tf_op jit(solution)/shard_map/ppermute | solution.py:79
  15.7 31.8 %all-to-all-start = ((bf16[32,32,832]{2,1,0:T(8,128)(2,1)}), bf16[32,32,832]{2,1,0:T(8,128)(2,1)S(1)}, u32[]{:S(2)}, u32[]{:S(2)}) async-start(bf16[32,32,832]{2,1,0:T(8,128)(2,1)} %shard_map.212), calls=%async_computation | async-start | bytes 3670016 | tf_op jit(solution)/shard_map/all_to_all | solution.py:69
  23.7 94.3 %all-gather.2.cloned.1.call-start = ((), (), s32[]{:S(2)}) async-start(), calls=%async_computation.7 | async-start | bytes 6406144 | tf_op jit(solution)/shard_map/all_gather | solution.py:517
  47.5 6.4 %collective-permute-start.1 = (bf16[32,32,832]{2,1,0:T(8,128)(2,1)S(1)}, bf16[32,32,832]{2,1,0:T(8,128)(2,1)}, u32[]{:S(2)}, u32[]{:S(2)}) collective-permute-start(bf16[32,32,832]{2,1,0:T(8,128)(2,1)S(1)} %all-to-all-done.wa), channel_id=1, source_target_pairs={{0,1},{1,0},{2,3},{3,2},{4,5},{5,4},{6,7},{7,6},{8,9},{9,8},{10,11... | collective-permute-start | bytes 5111816 | tf_op jit(solution)/shard_map/ppermute | solution.py:79
  83.7 2.5 collective-permute-start.2
  97.9 27.7 %collective-permute-start.3 = (bf16[2,128,1024]{2,1,0:T(8,128)(2,1)S(1)}, bf16[2,128,1024]{2,1,0:T(8,128)(2,1)S(1)}, u32[]{:S(2)}, u32[]{:S(2)}) collective-permute-start(bf16[2,128,1024]{2,1,0:T(8,128)(2,1)S(1)} %copy-done), channel_id=1, source_target_pairs={{0,2},{1,3},{2,0},{3,1},{4,6},{5,7},{6,4},{7,5},{8,10},{9,11},{10,... | collective-permute-start | bytes 1572872 | tf_op jit(solution)/shard_map/ppermute | solution.py:79
  97.9 21.7 %all-to-all-start.2 = ((bf16[64,16,128]{2,1,0:T(8,128)(2,1)}), bf16[64,16,128]{2,1,0:T(8,128)(2,1)S(1)}, u32[]{:S(2)}, u32[]{:S(2)}) async-start(bf16[64,16,128]{2,1,0:T(8,128)(2,1)} %get-tuple-element.89), calls=%async_computation.2 | async-start | bytes 524288 | tf_op jit(solution)/shard_map/all_to_all | solution.py:69
  104.6 167.1 %reduce-scatter.2.cloned.1.call-start = ((), (), s32[]{:S(2)}) async-start(), calls=%async_computation.8 | async-start | bytes 4177920 | tf_op jit(solution)/shard_map/reduce_scatter | solution.py:98
  104.6 25.4 %collective-permute-start.5 = (bf16[2,128,1024]{2,1,0:T(8,128)(2,1)S(1)}, bf16[2,128,1024]{2,1,0:T(8,128)(2,1)S(1)}, u32[]{:S(2)}, u32[]{:S(2)}) collective-permute-start(bf16[2,128,1024]{2,1,0:T(8,128)(2,1)S(1)} %copy-done), channel_id=1, source_target_pairs={{0,1},{1,0},{2,3},{3,2},{4,5},{5,4},{6,7},{7,6},{8,9},{9,8},{10,11... | collective-permute-start | bytes 1572872 | tf_op jit(solution)/shard_map/ppermute | solution.py:79
  125.6 16.1 %collective-permute-start.9 = (bf16[2,128,1024]{2,1,0:T(8,128)(2,1)S(1)}, bf16[2,128,1024]{2,1,0:T(8,128)(2,1)S(1)}, u32[]{:S(2)}, u32[]{:S(2)}) collective-permute-start(bf16[2,128,1024]{2,1,0:T(8,128)(2,1)S(1)} %collective-permute-done.3.dy_a.d2.x2), channel_id=1, source_target_pairs={{0,1},{1,0},{2,3},{3,2},{4,5},{5,4},{6,7},{7,6},{8,9},{9,8},{10,11... | collective-permute-start | bytes 1572872 | tf_op jit(solution)/shard_map/ppermute | solution.py:79
  126.3 3.8 %collective-permute-start.4 = (bf16[128,1024]{1,0:T(8,128)(2,1)}, bf16[128,1024]{1,0:T(8,128)(2,1)S(1)}, u32[]{:S(2)}, u32[]{:S(2)}) collective-permute-start(bf16[128,1024]{1,0:T(8,128)(2,1)} %get-tuple-element.93.h_a.h0), channel_id=1, source_target_pairs={{0,1},{1,0},{2,3},{3,2},{4,5},{5,4},{6,7},{7,6},{8,9},{9,8},{10,11... | collective-permute-start | bytes 786440 | tf_op jit(solution)/shard_map/ppermute | solution.py:79
  126.3 12.4 %collective-permute-start.6 = (bf16[128,1024]{1,0:T(8,128)(2,1)}, bf16[128,1024]{1,0:T(8,128)(2,1)S(1)}, u32[]{:S(2)}, u32[]{:S(2)}) collective-permute-start(bf16[128,1024]{1,0:T(8,128)(2,1)} %get-tuple-element.93.h_a.h0), channel_id=1, source_target_pairs={{0,2},{1,3},{2,0},{3,1},{4,6},{5,7},{6,4},{7,5},{8,10},{9,11},{10,... | collective-permute-start | bytes 786440 | tf_op jit(solution)/shard_map/ppermute | solution.py:79
  129.2 12.5 %collective-permute-start.7 = (bf16[128,1024]{1,0:T(8,128)(2,1)}, bf16[128,1024]{1,0:T(8,128)(2,1)S(1)}, u32[]{:S(2)}, u32[]{:S(2)}) collective-permute-start(bf16[128,1024]{1,0:T(8,128)(2,1)} %get-tuple-element.93.h_a.h0), channel_id=1, source_target_pairs={{0,3},{1,2},{2,1},{3,0},{4,7},{5,6},{6,5},{7,4},{8,11},{9,10},{10,... | collective-permute-start | bytes 786440 | tf_op jit(solution)/shard_map/ppermute | solution.py:79
  141.7 24.4 %collective-permute-start.8 = (bf16[128,1024]{1,0:T(8,128)(2,1)}, bf16[128,1024]{1,0:T(8,128)(2,1)S(1)}, u32[]{:S(2)}, u32[]{:S(2)}) collective-permute-start(bf16[128,1024]{1,0:T(8,128)(2,1)} %get-tuple-element.96), channel_id=1, source_target_pairs={{0,1},{1,0},{2,3},{3,2},{4,5},{5,4},{6,7},{7,6},{8,9},{9,8},{10,11... | collective-permute-start | bytes 786440 | tf_op jit(solution)/shard_map/ppermute | solution.py:79
  150.4 15.7 %collective-permute-start.10 = (bf16[128,1024]{1,0:T(8,128)(2,1)}, bf16[128,1024]{1,0:T(8,128)(2,1)S(1)}, u32[]{:S(2)}, u32[]{:S(2)}) collective-permute-start(bf16[128,1024]{1,0:T(8,128)(2,1)} %get-tuple-element.100), channel_id=1, source_target_pairs={{0,2},{1,3},{2,0},{3,1},{4,6},{5,7},{6,4},{7,5},{8,10},{9,11},{10,... | collective-permute-start | bytes 786440 | tf_op jit(solution)/shard_map/ppermute | solution.py:79
  153.3 12.8 %collective-permute-start.11 = (bf16[128,1024]{1,0:T(8,128)(2,1)}, bf16[128,1024]{1,0:T(8,128)(2,1)S(1)}, u32[]{:S(2)}, u32[]{:S(2)}) collective-permute-start(bf16[128,1024]{1,0:T(8,128)(2,1)} %get-tuple-element.101), channel_id=1, source_target_pairs={{0,3},{1,2},{2,1},{3,0},{4,7},{5,6},{6,5},{7,4},{8,11},{9,10},{10,... | collective-permute-start | bytes 786440 | tf_op jit(solution)/shard_map/ppermute | solution.py:79
  174.1 11.7 %collective-permute-start.12 = (bf16[2,128,1024]{2,1,0:T(8,128)(2,1)S(1)}, bf16[2,128,1024]{2,1,0:T(8,128)(2,1)S(1)}, u32[]{:S(2)}, u32[]{:S(2)}) collective-permute-start(bf16[2,128,1024]{2,1,0:T(8,128)(2,1)S(1)} %copy-done.33), channel_id=1, source_target_pairs={{0,1},{1,0},{2,3},{3,2},{4,5},{5,4},{6,7},{7,6},{8,9},{9,8},{10,11... | collective-permute-start | bytes 1572872 | tf_op jit(solution)/shard_map/ppermute | solution.py:79
  174.4 21.4 %all-to-all-start.3 = ((bf16[64,16,128]{2,1,0:T(8,128)(2,1)}), bf16[64,16,128]{2,1,0:T(8,128)(2,1)S(1)}, u32[]{:S(2)}, u32[]{:S(2)}) async-start(bf16[64,16,128]{2,1,0:T(8,128)(2,1)} %get-tuple-element.114), calls=%async_computation.3 | async-start | bytes 524288 | tf_op jit(solution)/shard_map/all_to_all | solution.py:69
  182.9 13.3 %collective-permute-start.14 = (bf16[128,1024]{1,0:T(8,128)(2,1)S(1)}, bf16[128,1024]{1,0:T(8,128)(2,1)S(1)}, u32[]{:S(2)}, u32[]{:S(2)}) collective-permute-start(bf16[128,1024]{1,0:T(8,128)(2,1)S(1)} %copy-done.23), channel_id=1, source_target_pairs={{0,2},{1,3},{2,0},{3,1},{4,6},{5,7},{6,4},{7,5},{8,10},{9,11},{10,... | collective-permute-start | bytes 786440 | tf_op jit(solution)/shard_map/ppermute | solution.py:79
  186.1 27.3 %copy-start.8 = (bf16[2,128,1024]{2,1,0:T(8,128)(2,1)}, bf16[2,128,1024]{2,1,0:T(8,128)(2,1)S(1)}, u32[]{:S(2)}) copy-start(bf16[2,128,1024]{2,1,0:T(8,128)(2,1)S(1)} %add_convert_fusion.own) | copy-start | bytes 1572868
  195.9 17.5 %collective-permute-start.13 = (bf16[128,1024]{1,0:T(8,128)(2,1)S(1)}, bf16[128,1024]{1,0:T(8,128)(2,1)S(1)}, u32[]{:S(2)}, u32[]{:S(2)}) collective-permute-start(bf16[128,1024]{1,0:T(8,128)(2,1)S(1)} %slice_bitcast_fusion), channel_id=1, source_target_pairs={{0,2},{1,3},{2,0},{3,1},{4,6},{5,7},{6,4},{7,5},{8,10},{9,11},{10,... | collective-permute-start | bytes 786440 | tf_op jit(solution)/shard_map/ppermute | solution.py:79
  196.3 24.6 %copy-start.10 = (bf16[2,128,1024]{2,1,0:T(8,128)(2,1)}, bf16[2,128,1024]{2,1,0:T(8,128)(2,1)S(1)}, u32[]{:S(2)}) copy-start(bf16[2,128,1024]{2,1,0:T(8,128)(2,1)S(1)} %pad_maximum_fusion.o_near) | copy-start | bytes 1572868
  213.4 31.8 %all-to-all-start.4 = ((bf16[64,80,128]{2,1,0:T(8,128)(2,1)}), bf16[64,80,128]{2,1,0:T(8,128)(2,1)S(1)}, u32[]{:S(2)}, u32[]{:S(2)}) async-start(bf16[64,80,128]{2,1,0:T(8,128)(2,1)} %shard_map.222), calls=%async_computation.4 | async-start | bytes 2621440 | tf_op jit(solution)/shard_map/all_to_all | solution.py:69
  220.9 41.1 %collective-permute-start.15 = (bf16[2,128,1024]{2,1,0:T(8,128)(2,1)S(1)}, bf16[2,128,1024]{2,1,0:T(8,128)(2,1)S(1)}, u32[]{:S(2)}, u32[]{:S(2)}) collective-permute-start(bf16[2,128,1024]{2,1,0:T(8,128)(2,1)S(1)} %pad_maximum_fusion.o_near), channel_id=1, source_target_pairs={{0,1},{1,0},{2,3},{3,2},{4,5},{5,4},{6,7},{7,6},{8,9},{9,8},{10,11... | collective-permute-start | bytes 1572872 | tf_op jit(solution)/shard_map/ppermute | solution.py:79
  249.4 12.5 %collective-permute-start.16 = (bf16[128,640]{1,0:T(8,128)(2,1)}, bf16[128,640]{1,0:T(8,128)(2,1)S(1)}, u32[]{:S(2)}, u32[]{:S(2)}) collective-permute-start(bf16[128,640]{1,0:T(8,128)(2,1)} %get-tuple-element.135), channel_id=1, source_target_pairs={{0,1},{1,0},{2,3},{3,2},{4,5},{5,4},{6,7},{7,6},{8,9},{9,8},{10,11... | collective-permute-start | bytes 491528 | tf_op jit(solution)/shard_map/ppermute | solution.py:79
  249.4 12.5 %collective-permute-start.17 = (bf16[128,640]{1,0:T(8,128)(2,1)}, bf16[128,640]{1,0:T(8,128)(2,1)S(1)}, u32[]{:S(2)}, u32[]{:S(2)}) collective-permute-start(bf16[128,640]{1,0:T(8,128)(2,1)} %get-tuple-element.136), channel_id=1, source_target_pairs={{0,2},{1,3},{2,0},{3,1},{4,6},{5,7},{6,4},{7,5},{8,10},{9,11},{10,... | collective-permute-start | bytes 491528 | tf_op jit(solution)/shard_map/ppermute | solution.py:79
  250.1 11.9 %collective-permute-start.18 = (bf16[128,640]{1,0:T(8,128)(2,1)}, bf16[128,640]{1,0:T(8,128)(2,1)S(1)}, u32[]{:S(2)}, u32[]{:S(2)}) collective-permute-start(bf16[128,640]{1,0:T(8,128)(2,1)} %get-tuple-element.137), channel_id=1, source_target_pairs={{0,3},{1,2},{2,1},{3,0},{4,7},{5,6},{6,5},{7,4},{8,11},{9,10},{10,... | collective-permute-start | bytes 491528 | tf_op jit(solution)/shard_map/ppermute | solution.py:79
  267.7 24.1 %all-to-all-start.5 = ((bf16[32,32,640]{2,1,0:T(8,128)(2,1)}), bf16[32,32,640]{2,1,0:T(8,128)(2,1)S(1)}, u32[]{:S(2)}, u32[]{:S(2)}) async-start(bf16[32,32,640]{2,1,0:T(8,128)(2,1)} %shard_map.227), calls=%async_computation.5 | async-start | bytes 2621440 | tf_op jit(solution)/shard_map/all_to_all | solution.py:69
  272.7 15.5 %collective-permute-start.19 = (bf16[96,640]{1,0:T(8,128)(2,1)S(1)}, bf16[96,640]{1,0:T(8,128)(2,1)S(1)}, u32[]{:S(2)}, u32[]{:S(2)}) collective-permute-start(bf16[96,640]{1,0:T(8,128)(2,1)S(1)} %broadcast_select_fusion), channel_id=1, source_target_pairs={{0,64},{64,0},{1,65},{65,1},{2,66},{66,2},{3,67},{67,3},{4,68},{68... | collective-permute-start | bytes 368648 | tf_op jit(solution)/shard_map/ppermute | solution.py:79
  295.0 4.4 %collective-permute-start.20 = (bf16[32,640]{1,0:T(8,128)(2,1)}, bf16[32,640]{1,0:T(8,128)(2,1)S(1)}, u32[]{:S(2)}, u32[]{:S(2)}) collective-permute-start(bf16[32,640]{1,0:T(8,128)(2,1)} %shard_map.228.p0), channel_id=1, source_target_pairs={{0,1},{1,0},{2,3},{3,2},{4,5},{5,4},{6,7},{7,6},{8,9},{9,8},{10,11... | collective-permute-start | bytes 122888 | tf_op jit(solution)/shard_map/ppermute | solution.py:79
  295.6 4.6 %collective-permute-start.21 = (bf16[32,640]{1,0:T(8,128)(2,1)}, bf16[32,640]{1,0:T(8,128)(2,1)S(1)}, u32[]{:S(2)}, u32[]{:S(2)}) collective-permute-start(bf16[32,640]{1,0:T(8,128)(2,1)} %shard_map.228.p0), channel_id=1, source_target_pairs={{0,2},{1,3},{2,0},{3,1},{4,6},{5,7},{6,4},{7,5},{8,10},{9,11},{10,... | collective-permute-start | bytes 122888 | tf_op jit(solution)/shard_map/ppermute | solution.py:79
  296.4 5.2 %collective-permute-start.22 = (bf16[32,640]{1,0:T(8,128)(2,1)}, bf16[32,640]{1,0:T(8,128)(2,1)S(1)}, u32[]{:S(2)}, u32[]{:S(2)}) collective-permute-start(bf16[32,640]{1,0:T(8,128)(2,1)} %shard_map.228.p0), channel_id=1, source_target_pairs={{0,3},{1,2},{2,1},{3,0},{4,7},{5,6},{6,5},{7,4},{8,11},{9,10},{10,... | collective-permute-start | bytes 122888 | tf_op jit(solution)/shard_map/ppermute | solution.py:79
  (32 other events, 133.7 us)
Sparse Core Ops, SparseCore 0:
  47.6 70.2 all-gather.1
  166.3 80.9 reduce-scatter.1

commit v6 on v5

--- a/solution.py
+++ b/solution.py
@@ -512,9 +512,10 @@
     cos = jnp.concatenate([c, c, c, c], axis=1)
     sin = jnp.concatenate([-s, s, -s, s], axis=1)
 
+    early = pair
     w1a, pair, xd, cos, sin = lax.optimization_barrier((w1a, pair, xd, cos, sin))
     w1b = swap(w1a, "tensor", 1)
-    w2 = lax.all_gather(pair, "context", axis=0, tiled=True).reshape(NB, PADB, -1)
+    w2 = lax.all_gather(early, "context", axis=0, tiled=True).reshape(NB, PADB, -1)
     gain2 = w2[:, 30, 3 * FFS : 3 * FFS + PADB].reshape(1, WP).astype(F32)
     gain1 = w1a[:, 30, :PADB].reshape(1, WP).astype(F32)
 

time: 318 us -> 327 us (1.028)
  blocking collectives: 25.4 us -> 33.6 us
  waiting for transfers between devices: 84.3 us -> 89.2 us
  starting transfers between devices: 61.5 us -> 57.9 us
    all_to_all x5, waiting for transfers between devices: 46.7 us -> 64.3 us  [exchange(): return lax.all_to_all(v, axes, 0, 0, tiled=True)]
    all_gather x1, waiting for transfers between devices: 12.8 us -> 0.01 us  [shards(): lax.all_gather(early, 'context', axis=0, tiled=True).reshape(NB, PADB, -1)]
    all_to_all x1, blocking collectives: 25.4 us -> 33.6 us  [exchange(): return lax.all_to_all(v, axes, 0, 0, tiled=True)]
    all_to_all x5, starting transfers between devices: 34.5 us -> 29.6 us  [exchange(): return lax.all_to_all(v, axes, 0, 0, tiled=True)]
  transfers between devices with their start and end apart: 30 -> 30, of which waited for: 12 -> 12; matrix products, arithmetic and copies ran while one was open for 3% -> 3% of each run, Pallas kernels for 32% -> 30%
where the time goes in v6:
time: 327 us; the launch traced here: 322 us
  Pallas kernels  103 us (31%)
  waiting for transfers between devices  89.2 us (27%)
  starting transfers between devices  57.9 us (18%)
  blocking collectives  33.6 us (10%)
  between operations  14.9 us (5%)
  local copies, waits for them, and re-layouts  14.5 us (4%)
  other arithmetic  8.52 us (3%)
    pallas_call x18, Pallas kernels, call(): pl.pallas_call(fn, in_specs=[(specs or {}).get(k, whole) for k in range(l...  103 us
    all_to_all x5, waiting for transfers between devices, exchange(): return lax.all_to_all(v, axes, 0, 0, tiled=True)  64.3 us
    all_to_all x1, blocking collectives, exchange(): return lax.all_to_all(v, axes, 0, 0, tiled=True)  33.6 us
    all_to_all x5, starting transfers between devices, exchange(): return lax.all_to_all(v, axes, 0, 0, tiled=True)  29.6 us
    ppermute x23, starting transfers between devices, swap(): return lax.ppermute(v, axis, pairs)  28.2 us
    ppermute x23, waiting for transfers between devices, swap(): return lax.ppermute(v, axis, pairs)  24.8 us
    unnamed x68, local copies, waits for them, and re-layouts  10.1 us
  transfers between devices with their start and end apart: 30, of which 12 were waited for; matrix products, arithmetic and copies ran while one was open for 3% of the time, Pallas kernels for 30%

profile of v6, /device:TPU:1, one launch (start us, length us, event | category | flops | bytes accessed | tf_op | source)
XLA Modules:
  0.0 321.7 jit_solution(5609547537673465823)
XLA Ops:
  15.8 4.4 %shard_map.213 = (bf16[64,2944]{1,0:T(8,128)(2,1)}, bf16[2,128,1024]{2,1,0:T(8,128)(2,1)}) custom-call(bf16[31,2880]{1,0:T(8,128)(2,1)} %copy-done.16, bf16[31,2880]{1,0:T(8,128)(2,1)} %copy-done.24, s32[1,1]{1,0:T(1,128)} %bitcast.4.shard, bf16[128,960]{1,0:T(8,128)(2,1)} %bitcast.30, bf16[128,960]{1,0:T(8,128)(2,1)} %bitcast.31, ...), custom_call_target="tpu_custom_call" | custom-call | tf_op jit(solution)/shard_map/pallas_call | solution.py:58
  20.2 7.9 %all-to-all-start = ((bf16[32,32,832]{2,1,0:T(8,128)(2,1)}), bf16[32,32,832]{2,1,0:T(8,128)(2,1)S(1)}, u32[]{:S(2)}, u32[]{:S(2)}) async-start(bf16[32,32,832]{2,1,0:T(8,128)(2,1)} %shard_map.212), calls=%async_computation | async-start | bytes 3670016 | tf_op jit(solution)/shard_map/all_to_all | solution.py:69
  29.4 25.6 %all-to-all-done.wa = bf16[32,32,832]{2,1,0:T(8,128)(2,1)S(1)} async-done(((bf16[32,32,832]{2,1,0:T(8,128)(2,1)}), bf16[32,32,832]{2,1,0:T(8,128)(2,1)S(1)}, u32[]{:S(2)}, u32[]{:S(2)}) %all-to-all-start) | async-done | bytes 1703968 | tf_op jit(solution)/shard_map/all_to_all | solution.py:69
  55.1 4.6 %collective-permute-start.1 = (bf16[32,32,832]{2,1,0:T(8,128)(2,1)S(1)}, bf16[32,32,832]{2,1,0:T(8,128)(2,1)}, u32[]{:S(2)}, u32[]{:S(2)}) collective-permute-start(bf16[32,32,832]{2,1,0:T(8,128)(2,1)S(1)} %all-to-all-done.wa), channel_id=1, source_target_pairs={{0,1},{1,0},{2,3},{3,2},{4,5},{5,4},{6,7},{7,6},{8,9},{9,8},{10,11... | collective-permute-start | bytes 5111816 | tf_op jit(solution)/shard_map/ppermute | solution.py:79
  63.3 4.4 %shard_map.214 = bf16[64,48,128]{2,1,0:T(8,128)(2,1)} custom-call(bf16[2,128,1024]{2,1,0:T(8,128)(2,1)} %get-tuple-element.89.xd.dy_a.d0.x0, f32[1,1024]{1,0:T(1,128)} %reshape.384.gain, bf16[32,32,832]{2,1,0:T(8,128)(2,1)} %copy-done.1, bf16[32,32,832]{2,1,0:T(8,128)(2,1)} %collective-permute-done.1.wb, s32[1,1]{1,0:T(1,128)} %bitcast.3.core, ...), custom_call_target="tpu_custom_call" | custom-call | tf_op jit(solution)/shard_map/pallas_call | solution.py:58
  67.6 33.6 %all_to_all.30.recv = bf16[64,48,128]{2,1,0:T(8,128)(2,1)S(1)} all-to-all(bf16[64,48,128]{2,1,0:T(8,128)(2,1)} %shard_map.214), channel_id=1, replica_groups=mesh['shard'=2,'context'=16,'tensor'=4] {'context','tensor'}, dimensions={0} | all-to-all | bytes 1572864 | tf_op jit(solution)/shard_map/all_to_all | solution.py:69
  104.6 10.5 %shard_map.215 = (bf16[64,16,128]{2,1,0:T(8,128)(2,1)}, f32[8,64,256]{2,1,0:T(8,128)}, f32[8,8,256]{2,1,0:T(8,128)}) custom-call(bf16[64,48,128]{2,1,0:T(8,128)(2,1)} %copy-done.2, bf16[64,32,128]{2,1,0:T(8,128)(2,1)} %copy-done.9, s32[512,1]{1,0:T(8,128)} %fusion.4.kpos, s32[1,256]{1,0:T(1,128)} %fusion.24.qpos), custom_call_target="tpu_custom_call" | custom-call | tf_op jit(solution)/shard_map/pallas_call | solution.py:58
  115.0 6.0 %all-to-all-start.2 = ((bf16[64,16,128]{2,1,0:T(8,128)(2,1)}), bf16[64,16,128]{2,1,0:T(8,128)(2,1)S(1)}, u32[]{:S(2)}, u32[]{:S(2)}) async-start(bf16[64,16,128]{2,1,0:T(8,128)(2,1)} %get-tuple-element.88), calls=%async_computation.2 | async-start | bytes 524288 | tf_op jit(solution)/shard_map/all_to_all | solution.py:69
  123.2 10.0 %all-to-all-done.2.recv = bf16[64,16,128]{2,1,0:T(8,128)(2,1)S(1)} async-done(((bf16[64,16,128]{2,1,0:T(8,128)(2,1)}), bf16[64,16,128]{2,1,0:T(8,128)(2,1)S(1)}, u32[]{:S(2)}, u32[]{:S(2)}) %all-to-all-start.2) | async-done | bytes 262176 | tf_op jit(solution)/shard_map/all_to_all | solution.py:69
  134.0 5.3 %shard_map.216 = (bf16[128,1024]{1,0:T(8,128)(2,1)}, f32[128,1024]{1,0:T(8,128)}, bf16[128,1024]{1,0:T(8,128)(2,1)}) custom-call(bf16[64,16,128]{2,1,0:T(8,128)(2,1)} %copy-done.12, bf16[2,128,1024]{2,1,0:T(8,128)(2,1)} %get-tuple-element.89.xd.dy_a.d0.x0, bf16[960,1024]{1,0:T(8,128)(2,1)} %constant.145.clone.e, f32[1,1024]{1,0:T(1,128)} %reshape.385.gain, ...), custom_call_target="tpu_custom_call" | custom-call | tf_op jit(solution)/shard_map/pallas_call | solution.py:58
  139.8 3.7 %collective-permute-start.7 = (bf16[128,1024]{1,0:T(8,128)(2,1)}, bf16[128,1024]{1,0:T(8,128)(2,1)S(1)}, u32[]{:S(2)}, u32[]{:S(2)}) collective-permute-start(bf16[128,1024]{1,0:T(8,128)(2,1)} %get-tuple-element.91.h_a.h0), channel_id=1, source_target_pairs={{0,3},{1,2},{2,1},{3,0},{4,7},{5,6},{6,5},{7,4},{8,11},{9,10},{10,... | collective-permute-start | bytes 786440 | tf_op jit(solution)/shard_map/ppermute | solution.py:79
  145.0 7.2 %shard_map.217 = (bf16[128,1024]{1,0:T(8,128)(2,1)}, bf16[128,1024]{1,0:T(8,128)(2,1)}, bf16[2,128,640]{2,1,0:T(8,128)(2,1)}, bf16[2,128,640]{2,1,0:T(8,128)(2,1)}, bf16[2,128,640]{2,1,0:T(8,128)(2,1)}) custom-call(bf16[128,1024]{1,0:T(8,128)(2,1)} %get-tuple-element.91.h_a.h0, bf16[128,1024]{1,0:T(8,128)(2,1)} %copy-done.13, ...), custom_call_target="tpu_custom_call" | custom-call | tf_op jit(solution)/shard_map/pallas_call | solution.py:58
  152.2 3.0 collective-permute-done.7.h_b.h3
  156.7 7.2 %shard_map.218 = (bf16[128,1024]{1,0:T(8,128)(2,1)}, bf16[128,1024]{1,0:T(8,128)(2,1)}, bf16[2,128,640]{2,1,0:T(8,128)(2,1)}, bf16[2,128,640]{2,1,0:T(8,128)(2,1)}, bf16[2,128,640]{2,1,0:T(8,128)(2,1)}) custom-call(bf16[128,1024]{1,0:T(8,128)(2,1)} %copy-done.14, bf16[128,1024]{1,0:T(8,128)(2,1)} %copy-done.15, bf16[2,128,1024]{2,1,0:T(8,128)(2,1)} %copy-done.5, ...), custom_call_target="tpu_custom_call" | custom-call | tf_op jit(solution)/shard_map/pallas_call | solution.py:58
  163.9 3.0 collective-permute-start.11
  166.9 5.5 %shard_map.220 = (bf16[2,128,1024]{2,1,0:T(8,128)(2,1)}, bf16[2,128,1024]{2,1,0:T(8,128)(2,1)}) custom-call(bf16[2,128,640]{2,1,0:T(8,128)(2,1)} %get-tuple-element.100.act_n.near, bf16[2,128,640]{2,1,0:T(8,128)(2,1)} %get-tuple-element.101.act_f.far, bf16[32,32,2944]{2,1,0:T(8,128)(2,1)} %bitcast.27), custom_call_target="tpu_custom_call" | custom-call | tf_op jit(solution)/shard_map/pallas_call | solution.py:58
  172.4 7.1 %shard_map.219 = bf16[32,96,640]{2,1,0:T(8,128)(2,1)} custom-call(bf16[128,1024]{1,0:T(8,128)(2,1)} %get-tuple-element.91.h_a.h0, bf16[128,1024]{1,0:T(8,128)(2,1)} %copy-done.13, bf16[128,1024]{1,0:T(8,128)(2,1)} %copy-done.14, bf16[128,1024]{1,0:T(8,128)(2,1)} %copy-done.15, bf16[2,128,1024]{2,1,0:T(8,128)(2,1)} %get-tuple-element.89.xd.dy_a.d0.x0, ...), custom_call_target="tpu_custom_call" | custom-call | tf_op jit(solution)/shard_map/pallas_call | solution.py:58
  180.4 7.1 %shard_map.221 = (f32[128,1024]{1,0:T(8,128)}, bf16[128,960]{1,0:T(8,128)(2,1)}, bf16[64,16,128]{2,1,0:T(8,128)(2,1)}, f32[1,1024]{1,0:T(1,128)}) custom-call(bf16[128,1024]{1,0:T(8,128)(2,1)} %get-tuple-element.92.b0, bf16[128,1024]{1,0:T(8,128)(2,1)} %copy-done.19, bf16[128,1024]{1,0:T(8,128)(2,1)} %copy-done.20, bf16[128,1024]{1,0:T(8,128)(2,1)} %copy-done.21, ...), custom_call_target="tpu_custom_call" | custom-call | tf_op jit(solution)/shard_map/pallas_call | solution.py:58
  187.9 4.2 %all-to-all-start.3 = ((bf16[64,16,128]{2,1,0:T(8,128)(2,1)}), bf16[64,16,128]{2,1,0:T(8,128)(2,1)S(1)}, u32[]{:S(2)}, u32[]{:S(2)}) async-start(bf16[64,16,128]{2,1,0:T(8,128)(2,1)} %get-tuple-element.112), calls=%async_computation.3 | async-start | bytes 524288 | tf_op jit(solution)/shard_map/all_to_all | solution.py:69
  192.1 3.0 collective-permute-start.14
  195.3 9.8 %all-to-all-done.3.drecv = bf16[64,16,128]{2,1,0:T(8,128)(2,1)S(1)} async-done(((bf16[64,16,128]{2,1,0:T(8,128)(2,1)}), bf16[64,16,128]{2,1,0:T(8,128)(2,1)S(1)}, u32[]{:S(2)}, u32[]{:S(2)}) %all-to-all-start.3) | async-done | bytes 262176 | tf_op jit(solution)/shard_map/all_to_all | solution.py:69
  205.8 16.9 %shard_map.222 = bf16[64,80,128]{2,1,0:T(8,128)(2,1)} custom-call(bf16[64,48,128]{2,1,0:T(8,128)(2,1)} %copy-done.2, bf16[64,32,128]{2,1,0:T(8,128)(2,1)} %copy-done.9, s32[512,1]{1,0:T(8,128)} %fusion.4.kpos, s32[1,256]{1,0:T(1,128)} %fusion.24.qpos, s32[1,1]{1,0:T(1,128)} %bitcast.3.core, bf16[64,16,128]{2,1,0:T(8,128)(2,1)} %copy-done.11, ...), custom_call_target="tpu_custom_call" | custom-call | tf_op jit(solution)/shard_map/pallas_call | solution.py:58
  222.7 7.5 %all-to-all-start.4 = ((bf16[64,80,128]{2,1,0:T(8,128)(2,1)}), bf16[64,80,128]{2,1,0:T(8,128)(2,1)S(1)}, u32[]{:S(2)}, u32[]{:S(2)}) async-start(bf16[64,80,128]{2,1,0:T(8,128)(2,1)} %shard_map.222), calls=%async_computation.4 | async-start | bytes 2621440 | tf_op jit(solution)/shard_map/all_to_all | solution.py:69
  231.8 2.9 shard_map.224.h1_all
  234.8 3.4 %shard_map.223 = bf16[128,960]{1,0:T(8,128)(2,1)} custom-call(bf16[2,128,1024]{2,1,0:T(8,128)(2,1)} %copy-done.8, bf16[128,1024]{1,0:T(8,128)(2,1)} %copy-done.22, f32[128,1024]{1,0:T(8,128)} %get-tuple-element.111.x1, bf16[960,1024]{1,0:T(8,128)(2,1)} %constant.145.clone.e), custom_call_target="tpu_custom_call" | custom-call | tf_op jit(solution)/shard_map/pallas_call | solution.py:58
  238.3 16.3 %all-to-all-done.4.recv = bf16[64,80,128]{2,1,0:T(8,128)(2,1)S(1)} async-done(((bf16[64,80,128]{2,1,0:T(8,128)(2,1)}), bf16[64,80,128]{2,1,0:T(8,128)(2,1)S(1)}, u32[]{:S(2)}, u32[]{:S(2)}) %all-to-all-start.4) | async-done | bytes 1310752 | tf_op jit(solution)/shard_map/all_to_all | solution.py:69
  255.7 3.1 shard_map.225
  259.4 2.9 collective-permute-start.18
  262.4 7.3 %shard_map.226 = (f32[128,960]{1,0:T(8,128)}, f32[1,1024]{1,0:T(1,128)}) custom-call(bf16[128,1600]{1,0:T(8,128)(2,1)} %get-tuple-element.127.full, bf16[32,32,832]{2,1,0:T(8,128)(2,1)} %copy-done.1, bf16[32,32,832]{2,1,0:T(8,128)(2,1)} %collective-permute-done.1.wb, s32[1,1]{1,0:T(1,128)} %bitcast.3.core, ...), custom_call_target="tpu_custom_call" | custom-call | tf_op jit(solution)/shard_map/pallas_call | solution.py:58
  272.2 4.8 %shard_map.227 = bf16[32,32,640]{2,1,0:T(8,128)(2,1)} custom-call(bf16[512,1024]{1,0:T(8,128)(2,1)} %shard_map.224.h1_all, bf16[2,128,1024]{2,1,0:T(8,128)(2,1)} %copy-done.10, bf16[2,128,1024]{2,1,0:T(8,128)(2,1)} %copy-done.18, bf16[128,640]{1,0:T(8,128)(2,1)} %get-tuple-element.132.g0, bf16[128,640]{1,0:T(8,128)(2,1)} %copy-done.25, ...), custom_call_target="tpu_custom_call" | custom-call | tf_op jit(solution)/shard_map/pallas_call | solution.py:58
  277.0 3.9 %all-to-all-start.5 = ((bf16[32,32,640]{2,1,0:T(8,128)(2,1)}), bf16[32,32,640]{2,1,0:T(8,128)(2,1)S(1)}, u32[]{:S(2)}, u32[]{:S(2)}) async-start(bf16[32,32,640]{2,1,0:T(8,128)(2,1)} %shard_map.227), calls=%async_computation.5 | async-start | bytes 2621440 | tf_op jit(solution)/shard_map/all_to_all | solution.py:69
  283.2 14.3 %collective-permute-done.19 = bf16[96,640]{1,0:T(8,128)(2,1)S(1)} collective-permute-done((bf16[96,640]{1,0:T(8,128)(2,1)S(1)}, bf16[96,640]{1,0:T(8,128)(2,1)S(1)}, u32[]{:S(2)}, u32[]{:S(2)}) %collective-permute-start.19) | collective-permute-done | bytes 122912 | tf_op jit(solution)/shard_map/ppermute | solution.py:79
  (145 shorter events, 50.3 us)
Async XLA Ops:
  7.2 114.5 %all-gather.2.cloned.1.call-start = ((), (), s32[]{:S(2)}) async-start(), calls=%async_computation.7 | async-start | bytes 6406144 | tf_op jit(solution)/shard_map/all_gather | solution.py:518
  8.1 7.0 %collective-permute-start = (bf16[31,2880]{1,0:T(8,128)(2,1)S(1)}, bf16[31,2880]{1,0:T(8,128)(2,1)S(1)}, u32[]{:S(2)}, u32[]{:S(2)}) collective-permute-start(bf16[31,2880]{1,0:T(8,128)(2,1)S(1)} %fusion.17.own), channel_id=1, source_target_pairs={{0,64},{64,0},{1,65},{65,1},{2,66},{66,2},{3,67},{67,3},{4,68},{68... | collective-permute-start | bytes 535688 | tf_op jit(solution)/shard_map/ppermute | solution.py:79
  20.2 34.8 %all-to-all-start = ((bf16[32,32,832]{2,1,0:T(8,128)(2,1)}), bf16[32,32,832]{2,1,0:T(8,128)(2,1)S(1)}, u32[]{:S(2)}, u32[]{:S(2)}) async-start(bf16[32,32,832]{2,1,0:T(8,128)(2,1)} %shard_map.212), calls=%async_computation | async-start | bytes 3670016 | tf_op jit(solution)/shard_map/all_to_all | solution.py:69
  55.1 8.2 %collective-permute-start.1 = (bf16[32,32,832]{2,1,0:T(8,128)(2,1)S(1)}, bf16[32,32,832]{2,1,0:T(8,128)(2,1)}, u32[]{:S(2)}, u32[]{:S(2)}) collective-permute-start(bf16[32,32,832]{2,1,0:T(8,128)(2,1)S(1)} %all-to-all-done.wa), channel_id=1, source_target_pairs={{0,1},{1,0},{2,3},{3,2},{4,5},{5,4},{6,7},{7,6},{8,9},{9,8},{10,11... | collective-permute-start | bytes 5111816 | tf_op jit(solution)/shard_map/ppermute | solution.py:79
  101.3 2.5 collective-permute-start.2
  115.0 24.2 %collective-permute-start.3 = (bf16[2,128,1024]{2,1,0:T(8,128)(2,1)S(1)}, bf16[2,128,1024]{2,1,0:T(8,128)(2,1)S(1)}, u32[]{:S(2)}, u32[]{:S(2)}) collective-permute-start(bf16[2,128,1024]{2,1,0:T(8,128)(2,1)S(1)} %copy-done), channel_id=1, source_target_pairs={{0,2},{1,3},{2,0},{3,1},{4,6},{5,7},{6,4},{7,5},{8,10},{9,11},{10,... | collective-permute-start | bytes 1572872 | tf_op jit(solution)/shard_map/ppermute | solution.py:79
  115.0 18.2 %all-to-all-start.2 = ((bf16[64,16,128]{2,1,0:T(8,128)(2,1)}), bf16[64,16,128]{2,1,0:T(8,128)(2,1)S(1)}, u32[]{:S(2)}, u32[]{:S(2)}) async-start(bf16[64,16,128]{2,1,0:T(8,128)(2,1)} %get-tuple-element.88), calls=%async_computation.2 | async-start | bytes 524288 | tf_op jit(solution)/shard_map/all_to_all | solution.py:69
  121.1 159.9 %reduce-scatter.2.cloned.1.call-start = ((), (), s32[]{:S(2)}) async-start(), calls=%async_computation.8 | async-start | bytes 4177920 | tf_op jit(solution)/shard_map/reduce_scatter | solution.py:98
  121.1 22.4 %collective-permute-start.5 = (bf16[2,128,1024]{2,1,0:T(8,128)(2,1)S(1)}, bf16[2,128,1024]{2,1,0:T(8,128)(2,1)S(1)}, u32[]{:S(2)}, u32[]{:S(2)}) collective-permute-start(bf16[2,128,1024]{2,1,0:T(8,128)(2,1)S(1)} %copy-done), channel_id=1, source_target_pairs={{0,1},{1,0},{2,3},{3,2},{4,5},{5,4},{6,7},{7,6},{8,9},{9,8},{10,11... | collective-permute-start | bytes 1572872 | tf_op jit(solution)/shard_map/ppermute | solution.py:79
  139.3 15.9 %collective-permute-start.9 = (bf16[2,128,1024]{2,1,0:T(8,128)(2,1)S(1)}, bf16[2,128,1024]{2,1,0:T(8,128)(2,1)S(1)}, u32[]{:S(2)}, u32[]{:S(2)}) collective-permute-start(bf16[2,128,1024]{2,1,0:T(8,128)(2,1)S(1)} %collective-permute-done.3.dy_a.d2.x2), channel_id=1, source_target_pairs={{0,1},{1,0},{2,3},{3,2},{4,5},{5,4},{6,7},{7,6},{8,9},{9,8},{10,11... | collective-permute-start | bytes 1572872 | tf_op jit(solution)/shard_map/ppermute | solution.py:79
  139.7 3.8 %collective-permute-start.4 = (bf16[128,1024]{1,0:T(8,128)(2,1)}, bf16[128,1024]{1,0:T(8,128)(2,1)S(1)}, u32[]{:S(2)}, u32[]{:S(2)}) collective-permute-start(bf16[128,1024]{1,0:T(8,128)(2,1)} %get-tuple-element.91.h_a.h0), channel_id=1, source_target_pairs={{0,1},{1,0},{2,3},{3,2},{4,5},{5,4},{6,7},{7,6},{8,9},{9,8},{10,11... | collective-permute-start | bytes 786440 | tf_op jit(solution)/shard_map/ppermute | solution.py:79
  139.8 12.4 %collective-permute-start.6 = (bf16[128,1024]{1,0:T(8,128)(2,1)}, bf16[128,1024]{1,0:T(8,128)(2,1)S(1)}, u32[]{:S(2)}, u32[]{:S(2)}) collective-permute-start(bf16[128,1024]{1,0:T(8,128)(2,1)} %get-tuple-element.91.h_a.h0), channel_id=1, source_target_pairs={{0,2},{1,3},{2,0},{3,1},{4,6},{5,7},{6,4},{7,5},{8,10},{9,11},{10,... | collective-permute-start | bytes 786440 | tf_op jit(solution)/shard_map/ppermute | solution.py:79
  139.8 15.4 %collective-permute-start.7 = (bf16[128,1024]{1,0:T(8,128)(2,1)}, bf16[128,1024]{1,0:T(8,128)(2,1)S(1)}, u32[]{:S(2)}, u32[]{:S(2)}) collective-permute-start(bf16[128,1024]{1,0:T(8,128)(2,1)} %get-tuple-element.91.h_a.h0), channel_id=1, source_target_pairs={{0,3},{1,2},{2,1},{3,0},{4,7},{5,6},{6,5},{7,4},{8,11},{9,10},{10,... | collective-permute-start | bytes 786440 | tf_op jit(solution)/shard_map/ppermute | solution.py:79
  155.2 24.3 %collective-permute-start.8 = (bf16[128,1024]{1,0:T(8,128)(2,1)}, bf16[128,1024]{1,0:T(8,128)(2,1)S(1)}, u32[]{:S(2)}, u32[]{:S(2)}) collective-permute-start(bf16[128,1024]{1,0:T(8,128)(2,1)} %get-tuple-element.94), channel_id=1, source_target_pairs={{0,1},{1,0},{2,3},{3,2},{4,5},{5,4},{6,7},{7,6},{8,9},{9,8},{10,11... | collective-permute-start | bytes 786440 | tf_op jit(solution)/shard_map/ppermute | solution.py:79
  163.9 15.6 %collective-permute-start.10 = (bf16[128,1024]{1,0:T(8,128)(2,1)}, bf16[128,1024]{1,0:T(8,128)(2,1)S(1)}, u32[]{:S(2)}, u32[]{:S(2)}) collective-permute-start(bf16[128,1024]{1,0:T(8,128)(2,1)} %get-tuple-element.98), channel_id=1, source_target_pairs={{0,2},{1,3},{2,0},{3,1},{4,6},{5,7},{6,4},{7,5},{8,10},{9,11},{10,... | collective-permute-start | bytes 786440 | tf_op jit(solution)/shard_map/ppermute | solution.py:79
  163.9 15.6 %collective-permute-start.11 = (bf16[128,1024]{1,0:T(8,128)(2,1)}, bf16[128,1024]{1,0:T(8,128)(2,1)S(1)}, u32[]{:S(2)}, u32[]{:S(2)}) collective-permute-start(bf16[128,1024]{1,0:T(8,128)(2,1)} %get-tuple-element.99), channel_id=1, source_target_pairs={{0,3},{1,2},{2,1},{3,0},{4,7},{5,6},{6,5},{7,4},{8,11},{9,10},{10,... | collective-permute-start | bytes 786440 | tf_op jit(solution)/shard_map/ppermute | solution.py:79
  187.5 7.6 %collective-permute-start.12 = (bf16[2,128,1024]{2,1,0:T(8,128)(2,1)S(1)}, bf16[2,128,1024]{2,1,0:T(8,128)(2,1)S(1)}, u32[]{:S(2)}, u32[]{:S(2)}) collective-permute-start(bf16[2,128,1024]{2,1,0:T(8,128)(2,1)S(1)} %copy-done.33), channel_id=1, source_target_pairs={{0,1},{1,0},{2,3},{3,2},{4,5},{5,4},{6,7},{7,6},{8,9},{9,8},{10,11... | collective-permute-start | bytes 1572872 | tf_op jit(solution)/shard_map/ppermute | solution.py:79
  187.9 17.2 %all-to-all-start.3 = ((bf16[64,16,128]{2,1,0:T(8,128)(2,1)}), bf16[64,16,128]{2,1,0:T(8,128)(2,1)S(1)}, u32[]{:S(2)}, u32[]{:S(2)}) async-start(bf16[64,16,128]{2,1,0:T(8,128)(2,1)} %get-tuple-element.112), calls=%async_computation.3 | async-start | bytes 524288 | tf_op jit(solution)/shard_map/all_to_all | solution.py:69
  192.1 13.3 %collective-permute-start.14 = (bf16[128,1024]{1,0:T(8,128)(2,1)S(1)}, bf16[128,1024]{1,0:T(8,128)(2,1)S(1)}, u32[]{:S(2)}, u32[]{:S(2)}) collective-permute-start(bf16[128,1024]{1,0:T(8,128)(2,1)S(1)} %copy-done.23), channel_id=1, source_target_pairs={{0,2},{1,3},{2,0},{3,1},{4,6},{5,7},{6,4},{7,5},{8,10},{9,11},{10,... | collective-permute-start | bytes 786440 | tf_op jit(solution)/shard_map/ppermute | solution.py:79
  195.3 27.4 %copy-start.8 = (bf16[2,128,1024]{2,1,0:T(8,128)(2,1)}, bf16[2,128,1024]{2,1,0:T(8,128)(2,1)S(1)}, u32[]{:S(2)}) copy-start(bf16[2,128,1024]{2,1,0:T(8,128)(2,1)S(1)} %add_convert_fusion.own) | copy-start | bytes 1572868
  205.1 17.5 %collective-permute-start.13 = (bf16[128,1024]{1,0:T(8,128)(2,1)S(1)}, bf16[128,1024]{1,0:T(8,128)(2,1)S(1)}, u32[]{:S(2)}, u32[]{:S(2)}) collective-permute-start(bf16[128,1024]{1,0:T(8,128)(2,1)S(1)} %slice_bitcast_fusion), channel_id=1, source_target_pairs={{0,2},{1,3},{2,0},{3,1},{4,6},{5,7},{6,4},{7,5},{8,10},{9,11},{10,... | collective-permute-start | bytes 786440 | tf_op jit(solution)/shard_map/ppermute | solution.py:79
  205.5 24.7 %copy-start.10 = (bf16[2,128,1024]{2,1,0:T(8,128)(2,1)}, bf16[2,128,1024]{2,1,0:T(8,128)(2,1)S(1)}, u32[]{:S(2)}) copy-start(bf16[2,128,1024]{2,1,0:T(8,128)(2,1)S(1)} %pad_maximum_fusion.o_near) | copy-start | bytes 1572868
  222.7 31.9 %all-to-all-start.4 = ((bf16[64,80,128]{2,1,0:T(8,128)(2,1)}), bf16[64,80,128]{2,1,0:T(8,128)(2,1)S(1)}, u32[]{:S(2)}, u32[]{:S(2)}) async-start(bf16[64,80,128]{2,1,0:T(8,128)(2,1)} %shard_map.222), calls=%async_computation.4 | async-start | bytes 2621440 | tf_op jit(solution)/shard_map/all_to_all | solution.py:69
  230.2 41.1 %collective-permute-start.15 = (bf16[2,128,1024]{2,1,0:T(8,128)(2,1)S(1)}, bf16[2,128,1024]{2,1,0:T(8,128)(2,1)S(1)}, u32[]{:S(2)}, u32[]{:S(2)}) collective-permute-start(bf16[2,128,1024]{2,1,0:T(8,128)(2,1)S(1)} %pad_maximum_fusion.o_near), channel_id=1, source_target_pairs={{0,1},{1,0},{2,3},{3,2},{4,5},{5,4},{6,7},{7,6},{8,9},{9,8},{10,11... | collective-permute-start | bytes 1572872 | tf_op jit(solution)/shard_map/ppermute | solution.py:79
  258.7 12.5 %collective-permute-start.16 = (bf16[128,640]{1,0:T(8,128)(2,1)}, bf16[128,640]{1,0:T(8,128)(2,1)S(1)}, u32[]{:S(2)}, u32[]{:S(2)}) collective-permute-start(bf16[128,640]{1,0:T(8,128)(2,1)} %get-tuple-element.133), channel_id=1, source_target_pairs={{0,1},{1,0},{2,3},{3,2},{4,5},{5,4},{6,7},{7,6},{8,9},{9,8},{10,11... | collective-permute-start | bytes 491528 | tf_op jit(solution)/shard_map/ppermute | solution.py:79
  258.7 12.5 %collective-permute-start.17 = (bf16[128,640]{1,0:T(8,128)(2,1)}, bf16[128,640]{1,0:T(8,128)(2,1)S(1)}, u32[]{:S(2)}, u32[]{:S(2)}) collective-permute-start(bf16[128,640]{1,0:T(8,128)(2,1)} %get-tuple-element.134), channel_id=1, source_target_pairs={{0,2},{1,3},{2,0},{3,1},{4,6},{5,7},{6,4},{7,5},{8,10},{9,11},{10,... | collective-permute-start | bytes 491528 | tf_op jit(solution)/shard_map/ppermute | solution.py:79
  259.4 11.9 %collective-permute-start.18 = (bf16[128,640]{1,0:T(8,128)(2,1)}, bf16[128,640]{1,0:T(8,128)(2,1)S(1)}, u32[]{:S(2)}, u32[]{:S(2)}) collective-permute-start(bf16[128,640]{1,0:T(8,128)(2,1)} %get-tuple-element.135), channel_id=1, source_target_pairs={{0,3},{1,2},{2,1},{3,0},{4,7},{5,6},{6,5},{7,4},{8,11},{9,10},{10,... | collective-permute-start | bytes 491528 | tf_op jit(solution)/shard_map/ppermute | solution.py:79
  277.0 24.1 %all-to-all-start.5 = ((bf16[32,32,640]{2,1,0:T(8,128)(2,1)}), bf16[32,32,640]{2,1,0:T(8,128)(2,1)S(1)}, u32[]{:S(2)}, u32[]{:S(2)}) async-start(bf16[32,32,640]{2,1,0:T(8,128)(2,1)} %shard_map.227), calls=%async_computation.5 | async-start | bytes 2621440 | tf_op jit(solution)/shard_map/all_to_all | solution.py:69
  282.0 15.5 %collective-permute-start.19 = (bf16[96,640]{1,0:T(8,128)(2,1)S(1)}, bf16[96,640]{1,0:T(8,128)(2,1)S(1)}, u32[]{:S(2)}, u32[]{:S(2)}) collective-permute-start(bf16[96,640]{1,0:T(8,128)(2,1)S(1)} %broadcast_select_fusion), channel_id=1, source_target_pairs={{0,64},{64,0},{1,65},{65,1},{2,66},{66,2},{3,67},{67,3},{4,68},{68... | collective-permute-start | bytes 368648 | tf_op jit(solution)/shard_map/ppermute | solution.py:79
  304.3 4.4 %collective-permute-start.20 = (bf16[32,640]{1,0:T(8,128)(2,1)}, bf16[32,640]{1,0:T(8,128)(2,1)S(1)}, u32[]{:S(2)}, u32[]{:S(2)}) collective-permute-start(bf16[32,640]{1,0:T(8,128)(2,1)} %shard_map.228.p0), channel_id=1, source_target_pairs={{0,1},{1,0},{2,3},{3,2},{4,5},{5,4},{6,7},{7,6},{8,9},{9,8},{10,11... | collective-permute-start | bytes 122888 | tf_op jit(solution)/shard_map/ppermute | solution.py:79
  304.9 4.6 %collective-permute-start.21 = (bf16[32,640]{1,0:T(8,128)(2,1)}, bf16[32,640]{1,0:T(8,128)(2,1)S(1)}, u32[]{:S(2)}, u32[]{:S(2)}) collective-permute-start(bf16[32,640]{1,0:T(8,128)(2,1)} %shard_map.228.p0), channel_id=1, source_target_pairs={{0,2},{1,3},{2,0},{3,1},{4,6},{5,7},{6,4},{7,5},{8,10},{9,11},{10,... | collective-permute-start | bytes 122888 | tf_op jit(solution)/shard_map/ppermute | solution.py:79
  305.5 5.3 %collective-permute-start.22 = (bf16[32,640]{1,0:T(8,128)(2,1)}, bf16[32,640]{1,0:T(8,128)(2,1)S(1)}, u32[]{:S(2)}, u32[]{:S(2)}) collective-permute-start(bf16[32,640]{1,0:T(8,128)(2,1)} %shard_map.228.p0), channel_id=1, source_target_pairs={{0,3},{1,2},{2,1},{3,0},{4,7},{5,6},{6,5},{7,4},{8,11},{9,10},{10,... | collective-permute-start | bytes 122888 | tf_op jit(solution)/shard_map/ppermute | solution.py:79
  (32 other events, 123.5 us)
Sparse Core Ops, SparseCore 0:
  20.3 83.2 all-gather.1
  179.7 76.8 reduce-scatter.1
